TPU v7x, 32 devices: a whole 2x2x4 slice. The times are simulated.
32 devices in a mesh: slab: 8 (over z, x), tile: 4 (over y, core).
Axes of the slice: x: 2, y: 2, z: 4, core: 2. Of those that a mesh axis runs over, the one named last changes fastest.
Arguments:
- particles: float32 [1024, 16, 128], P(('slab', 'tile')), may hold values from -6 to 6, as said below
- dest_slot: int32 [1024], P(('slab', 'tile')), may hold values from 0 to 31, as said below
- neighbours: int32 [1024, 4], P(('slab', 'tile')), may hold values from 0 to 95, as said below
- counts: int32 [1024], P(('slab', 'tile')), may hold values from 1 to 4, as said below
Outputs:
- updated: float32 [1024, 16, 128], P(('slab', 'tile'))
- derived: float32 [1024, 5, 128], P(('slab', 'tile'))
Inputs may be any that keep to these rules, and one draw needn't show every extreme that they name: `dest_slot`: A bin on device (s, t) with value d goes to tile d // 8 of slab s. The values of one device are distinct, so at most 8 of its bins go to one owner; in every slab some owner receives 8 bins from every device of the slab. `neighbours`: entries index the 96 candidates of the slot's device: first the slab on the lower side (periodic), then the device's own slots, then the higher side. Entry 0 is the slot itself; the entries of a row are distinct. `counts`: every device has a slot that uses all 4 entries. `particles`: positions lie in 0 to 2, masses in 0.5 / 512 to 2 / 512, energies in 0.5 to 4, smoothing lengths in 0.6 to 1; velocities and carried quantities lie within -6 to 6.
All inputs are finite; a program needn't handle non-finite values.
Results may differ from a plain program's by a relative error of at most 0.0003.
Values sent between devices are 32-bit elements; how exact they have to be, the bound alone decides.
No kernel may reach another device: no remote copies, remote signals or barrier semaphores. Data moves between devices by JAX's collectives and lax.ppermute only.
A program may use at most 64 MiB of HBM per device.

v0:
```python
import math

import jax
import jax.numpy as jnp
from jax import lax
from jax.sharding import PartitionSpec as P

ADIABATIC = 5.0 / 3.0
TIMESTEP = 0.5
KERNEL_NORM = 21.0 / (16.0 * math.pi)


def extended(cells, sides, width):
    for axis, dim in sides:
        count = lax.axis_size(axis)
        head = lax.slice_in_dim(cells, 0, width, axis=dim)
        tail = lax.slice_in_dim(cells, cells.shape[dim] - width, cells.shape[dim], axis=dim)
        cells = jnp.concatenate(
            [
                lax.ppermute(tail, axis, [(i, (i + 1) % count) for i in range(count)]),
                cells,
                lax.ppermute(head, axis, [((i + 1) % count, i) for i in range(count)]),
            ],
            axis=dim,
        )
    return cells


def pair_terms(near_place, near_width, far_place, far_width):
    offset = near_place[:, :, None] - far_place[:, None, :]
    spacing = jnp.sqrt(jnp.sum(offset * offset, axis=0))
    blended = 0.5 * (near_width[:, None] + far_width[None, :])
    ratio = spacing / blended
    remain = jnp.maximum(1.0 - 0.5 * ratio, 0.0)
    scaled = KERNEL_NORM / (blended * blended * blended)
    cubed = remain * remain * remain
    weight = scaled * cubed * remain * (1.0 + 2.0 * ratio)
    slope = -5.0 * scaled / (blended * blended) * cubed
    return (weight, slope, offset)


def slot_density(self_place, self_width, picked, entries):
    active = (jnp.arange(picked.shape[0]) < entries).astype(jnp.float32)
    weight, slope, offset = jax.vmap(pair_terms, in_axes=(None, None, 0, 0))(
        self_place, self_width, picked[:, 0:3], picked[:, 4]
    )
    return jnp.sum(weight * (picked[:, 3] * active[:, None])[:, None, :], axis=(0, 2))


def slot_force(self_place, self_width, self_speed, self_ratio, picked, entries):
    active = (jnp.arange(picked.shape[0]) < entries).astype(jnp.float32)
    weight, slope, offset = jax.vmap(pair_terms, in_axes=(None, None, 0, 0))(
        self_place, self_width, picked[:, 0:3], picked[:, 4]
    )
    factor = (picked[:, 3] * active[:, None])[:, None, :] * slope
    pairing = factor * (self_ratio[None, :, None] + picked[:, 8][:, None, :])
    accel = -jnp.sum(pairing[:, None] * offset, axis=(0, 3))
    relative = self_speed[None, :, :, None] - picked[:, 5:8][:, :, None, :]
    closing = jnp.sum(relative * offset, axis=1)
    heating = self_ratio * jnp.sum(factor * closing, axis=(0, 2))
    return jnp.concatenate([accel, heating[None]], axis=0)


def over_blocks(worker, members):
    overall_number = members[0].shape[0]
    blocks = tuple(
        (member.reshape((overall_number // 8, 8) + member.shape[1:]) for member in members)
    )

    def run(block):
        return jax.vmap(worker)(*block)

    result = lax.map(run, blocks)
    return result.reshape((overall_number,) + result.shape[2:])


def pressure_of(local_density, energy):
    return (ADIABATIC - 1.0) * local_density * energy


def final_state(particle_states, local_density, change_rates):
    present = (particle_states[:, 6] > 0).astype(jnp.float32)
    speed = particle_states[:, 3:6] + TIMESTEP * change_rates[:, 0:3]
    place = particle_states[:, 0:3] + TIMESTEP * speed
    heat = particle_states[:, 7:8] + TIMESTEP * change_rates[:, 3:4]
    updated = (
        jnp.concatenate(
            [place, speed, particle_states[:, 6:7], heat, particle_states[:, 8:]], axis=1
        )
        * present[:, None, :]
    )
    derived = jnp.concatenate([local_density[:, None], change_rates], axis=1) * present[:, None, :]
    return (updated, derived)


def body(particles, dest_slot, neighbours, counts):
    slot_total = neighbours.shape[0]
    place_position = jnp.arange(slot_total, dtype=jnp.int32)
    routing = (dest_slot[:, None] == place_position[None, :]).astype(jnp.float32)
    packed = jnp.einsum("bs,bfp->sfp", routing, particles, precision=lax.Precision.HIGHEST)
    particle_states = lax.all_to_all(packed, "tile", split_axis=0, concat_axis=0, tiled=True)
    masses = particle_states[:, 6]
    present = masses > 0
    smooth = jnp.where(present, particle_states[:, 8], 1.0)
    energy = particle_states[:, 7]
    self_place = particle_states[:, 0:3]
    self_speed = particle_states[:, 3:6]
    moving = jnp.concatenate([self_place, masses[:, None], smooth[:, None]], axis=1)
    gathered = extended(moving, (("slab", 0),), slot_total)
    dense_pick = jnp.take(gathered, neighbours, axis=0)
    local_density = over_blocks(slot_density, (self_place, smooth, dense_pick, counts))
    pressure = pressure_of(local_density, energy)
    thermal = jnp.concatenate([local_density[:, None], pressure[:, None], self_speed], axis=1)
    remote = extended(thermal, (("slab", 0),), slot_total)
    pool_present = gathered[:, 3] > 0
    pool_ratio = remote[:, 1] / jnp.square(jnp.where(pool_present, remote[:, 0], 1.0))
    force_pool = jnp.concatenate([gathered, remote[:, 2:5], pool_ratio[:, None]], axis=1)
    self_ratio = pressure / jnp.square(jnp.where(present, local_density, 1.0))
    force_pick = jnp.take(force_pool, neighbours, axis=0)
    change_rates = over_blocks(
        slot_force, (self_place, smooth, self_speed, self_ratio, force_pick, counts)
    )
    return final_state(particle_states, local_density, change_rates)


def solution(mesh):
    in_specs = (
        P(("slab", "tile"), None, None),
        P(("slab", "tile")),
        P(("slab", "tile"), None),
        P(("slab", "tile")),
    )
    out_specs = (P(("slab", "tile"), None, None), P(("slab", "tile"), None, None))
    return jax.shard_map(body, mesh=mesh, in_specs=in_specs, out_specs=out_specs, check_vma=False)
```

profile of v0, /device:TPU:0, one launch (start us, length us, event | category | flops | bytes accessed | tf_op | source)
XLA Modules:
  0.0 75.5 jit_solution(3242729344215393662)
XLA Ops:
  0.6 0.9 %copy-done = f32[32,16,128]{2,1,0:T(8,128)S(1)} copy-done((f32[32,16,128]{2,1,0:T(8,128)S(1)}, f32[32,16,128]{2,1,0:T(8,128)}, u32[]{:S(2)}) %copy-start) | copy-done | bytes 262168
  1.6 1.0 %fusion.20 = f32[32,16,128]{2,0,1:T(8,128)S(1)} fusion(f32[32,16,128]{2,1,0:T(8,128)S(1)} %copy-done, s32[32]{0:T(128)} %param.9), kind=kOutput, calls=%fused_computation.57 | convolution fusion | flops 25166848 | bytes 524416 | tf_op jit(solution)/shard_map/bs,bfp->sfp/dot_general | solution.py:100
  2.6 0.9 %copy.44 = f32[32,16,128]{2,1,0:T(8,128)} copy(f32[32,16,128]{2,0,1:T(8,128)S(1)} %fusion.20) | data formatting | bytes 524288 | tf_op jit(solution)/shard_map/bs,bfp->sfp/dot_general | solution.py:100
  3.5 4.2 %all-to-all-start = ((f32[32,16,128]{2,1,0:T(8,128)}), f32[32,16,128]{2,1,0:T(8,128)S(1)}, u32[]{:S(2)}, u32[]{:S(2)}) async-start(f32[32,16,128]{2,1,0:T(8,128)} %copy.44), calls=%async_computation | async-start | bytes 524288 | tf_op jit(solution)/shard_map/all_to_all | solution.py:101
  7.7 0.7 compare_select_fusion.1
  8.4 0.7 compare_and_fusion
  9.1 0.1 copy.47
  9.2 0.1 reshape.159
  9.3 0.1 copy.51
  9.4 0.7 reshape.153
  10.1 3.6 %all-to-all-done = f32[32,16,128]{2,1,0:T(8,128)S(1)} async-done(((f32[32,16,128]{2,1,0:T(8,128)}), f32[32,16,128]{2,1,0:T(8,128)S(1)}, u32[]{:S(2)}, u32[]{:S(2)}) %all-to-all-start) | async-done | bytes 262176 | tf_op jit(solution)/shard_map/all_to_all | solution.py:101
  13.9 2.1 %collective-permute-start = (f32[32,5,128]{2,1,0:T(8,128)S(1)}, f32[32,5,128]{2,1,0:T(8,128)S(1)}, u32[]{:S(2)}, u32[]{:S(2)}) collective-permute-start(f32[32,5,128]{2,1,0:T(8,128)S(1)} %pad_maximum_fusion.5), channel_id=1, source_target_pairs={{0,4},{4,8},{8,12},{12,16},{16,20},{20,24},{24,28},{28,0},{1,5},{5... | collective-permute-start | bytes 245768 | tf_op jit(solution)/shard_map/ppermute | solution.py:20
  16.0 3.1 %collective-permute-start.1 = (f32[32,5,128]{2,1,0:T(8,128)S(1)}, f32[32,5,128]{2,1,0:T(8,128)S(1)}, u32[]{:S(2)}, u32[]{:S(2)}) collective-permute-start(f32[32,5,128]{2,1,0:T(8,128)S(1)} %pad_maximum_fusion.5), channel_id=1, source_target_pairs={{4,0},{8,4},{12,8},{16,12},{20,16},{24,20},{28,24},{0,28},{5,1},{9... | collective-permute-start | bytes 245768 | tf_op jit(solution)/shard_map/ppermute | solution.py:22
  19.2 3.3 %collective-permute-done = f32[32,5,128]{2,1,0:T(8,128)S(1)} collective-permute-done((f32[32,5,128]{2,1,0:T(8,128)S(1)}, f32[32,5,128]{2,1,0:T(8,128)S(1)}, u32[]{:S(2)}, u32[]{:S(2)}) %collective-permute-start) | collective-permute-done | bytes 81952 | tf_op jit(solution)/shard_map/ppermute | solution.py:20
  22.4 1.3 %collective-permute-done.1 = f32[32,5,128]{2,1,0:T(8,128)S(1)} collective-permute-done((f32[32,5,128]{2,1,0:T(8,128)S(1)}, f32[32,5,128]{2,1,0:T(8,128)S(1)}, u32[]{:S(2)}, u32[]{:S(2)}) %collective-permute-start.1) | collective-permute-done | bytes 81952 | tf_op jit(solution)/shard_map/ppermute | solution.py:22
  23.8 0.8 %gather_fusion = f32[128,5,128]{2,1,0:T(8,128)S(1)} fusion(f32[96,5,128]{2,1,0:T(8,128)S(1)} %pad_maximum_fusion.1, s32[1024]{0:T(1024)S(1)} %pad_clamp_fusion), kind=kCustom, calls=%fused_computation | custom fusion | bytes 655872 | tf_op jit(solution)/shard_map/jit(_take)/gather | solution.py:110
  24.6 0.2 copy_select_fusion.1
  24.7 13.9 %while.20 = (s32[]{:T(128)}, f32[4,8,128]{2,1,0:T(8,128)S(1)}, f32[4,8,128]{2,1,0:T(8,128)S(1)}, f32[4,8,4,5,128]{4,2,1,3,0:T(4,128)S(1)}, f32[4,8,3,128]{3,2,1,0:T(4,128)S(1)}, /*index=5*/s32[4,8]{1,0:T(4,128)S(1)}, s32[]{:T(128)}) while((s32[]{:T(128)}, f32[4,8,128]{2,1,0:T(8,128)S(1)}, f32[4,8,128]{2,1,0:T(8,128)S(1)}, ...), condition=%wide.region_3.4_spmd, body=%wide.region_0.0_spmd.sunk | while | flops 13634626 | bytes 4764097 | solution.py:73
  24.8 0.1 fusion.52
  24.9 0.1 slice_bitcast_fusion.4
  25.0 1.1 %multiply_reduce_fusion.4 = f32[8,4,128,128]{3,2,1,0:T(8,128)S(1)} fusion(f32[8,4,3,128]{3,2,1,0:T(4,128)S(1)} %copy.61, f32[8,3,128]{2,1,0:T(4,128)S(1)} %dynamic-slice_bitcast_fusion.14), kind=kLoop, calls=%fused_computation.2.clone.1 | loop fusion | flops 4194304 | bytes 2158592 | tf_op jit(solution)/shard_map/while/body/eval_jaxpr/vmap(vmap())/reduce_sum | solution.py:31
  26.1 2.1 %fusion.53 = f32[8,128]{1,0:T(8,128)S(1)} fusion(f32[8,4,128,128]{3,2,1,0:T(8,128)S(1)} %multiply_reduce_fusion.4, f32[8,4,128]{2,1,0:T(4,128)S(1)} %get-tuple-element.261, f32[8,4,128]{2,1,0:T(4,128)S(1)} %get-tuple-element.262, f32[8,128]{1,0:T(8,128)S(1)} %dynamic-slice_bitcast_fusion.15), kind=kLoop, calls=%fused_computation.10.clone.1 | loop fusion | flops 9436160 | bytes 2138112 | tf_op jit(solution)/shard_map/while/body/eval_jaxpr/vmap()/reduce_sum | solution.py:47
  28.3 0.1 slice_bitcast_fusion.4
  28.5 1.1 %multiply_reduce_fusion.4 = f32[8,4,128,128]{3,2,1,0:T(8,128)S(1)} fusion(f32[8,4,3,128]{3,2,1,0:T(4,128)S(1)} %copy.61, f32[8,3,128]{2,1,0:T(4,128)S(1)} %dynamic-slice_bitcast_fusion.14), kind=kLoop, calls=%fused_computation.2.clone.1 | loop fusion | flops 4194304 | bytes 2158592 | tf_op jit(solution)/shard_map/while/body/eval_jaxpr/vmap(vmap())/reduce_sum | solution.py:31
  29.6 2.1 %fusion.53 = f32[8,128]{1,0:T(8,128)S(1)} fusion(f32[8,4,128,128]{3,2,1,0:T(8,128)S(1)} %multiply_reduce_fusion.4, f32[8,4,128]{2,1,0:T(4,128)S(1)} %get-tuple-element.261, f32[8,4,128]{2,1,0:T(4,128)S(1)} %get-tuple-element.262, f32[8,128]{1,0:T(8,128)S(1)} %dynamic-slice_bitcast_fusion.15), kind=kLoop, calls=%fused_computation.10.clone.1 | loop fusion | flops 9436160 | bytes 2138112 | tf_op jit(solution)/shard_map/while/body/eval_jaxpr/vmap()/reduce_sum | solution.py:47
  31.8 0.1 slice_bitcast_fusion.4
  31.9 1.1 %multiply_reduce_fusion.4 = f32[8,4,128,128]{3,2,1,0:T(8,128)S(1)} fusion(f32[8,4,3,128]{3,2,1,0:T(4,128)S(1)} %copy.61, f32[8,3,128]{2,1,0:T(4,128)S(1)} %dynamic-slice_bitcast_fusion.14), kind=kLoop, calls=%fused_computation.2.clone.1 | loop fusion | flops 4194304 | bytes 2158592 | tf_op jit(solution)/shard_map/while/body/eval_jaxpr/vmap(vmap())/reduce_sum | solution.py:31
  33.0 2.1 %fusion.53 = f32[8,128]{1,0:T(8,128)S(1)} fusion(f32[8,4,128,128]{3,2,1,0:T(8,128)S(1)} %multiply_reduce_fusion.4, f32[8,4,128]{2,1,0:T(4,128)S(1)} %get-tuple-element.261, f32[8,4,128]{2,1,0:T(4,128)S(1)} %get-tuple-element.262, f32[8,128]{1,0:T(8,128)S(1)} %dynamic-slice_bitcast_fusion.15), kind=kLoop, calls=%fused_computation.10.clone.1 | loop fusion | flops 9436160 | bytes 2138112 | tf_op jit(solution)/shard_map/while/body/eval_jaxpr/vmap()/reduce_sum | solution.py:47
  35.3 0.1 slice_bitcast_fusion.4
  35.4 1.1 %multiply_reduce_fusion.4 = f32[8,4,128,128]{3,2,1,0:T(8,128)S(1)} fusion(f32[8,4,3,128]{3,2,1,0:T(4,128)S(1)} %copy.61, f32[8,3,128]{2,1,0:T(4,128)S(1)} %dynamic-slice_bitcast_fusion.14), kind=kLoop, calls=%fused_computation.2.clone.1 | loop fusion | flops 4194304 | bytes 2158592 | tf_op jit(solution)/shard_map/while/body/eval_jaxpr/vmap(vmap())/reduce_sum | solution.py:31
  36.5 2.1 %fusion.53 = f32[8,128]{1,0:T(8,128)S(1)} fusion(f32[8,4,128,128]{3,2,1,0:T(8,128)S(1)} %multiply_reduce_fusion.4, f32[8,4,128]{2,1,0:T(4,128)S(1)} %get-tuple-element.261, f32[8,4,128]{2,1,0:T(4,128)S(1)} %get-tuple-element.262, f32[8,128]{1,0:T(8,128)S(1)} %dynamic-slice_bitcast_fusion.15), kind=kLoop, calls=%fused_computation.10.clone.1 | loop fusion | flops 9436160 | bytes 2138112 | tf_op jit(solution)/shard_map/while/body/eval_jaxpr/vmap()/reduce_sum | solution.py:47
  38.7 0.2 collective-permute-start.2
  38.9 4.6 %collective-permute-start.3 = (f32[32,5,128]{2,1,0:T(8,128)S(1)}, f32[32,5,128]{2,1,0:T(8,128)S(1)}, u32[]{:S(2)}, u32[]{:S(2)}) collective-permute-start(f32[32,5,128]{2,1,0:T(8,128)S(1)} %fusion.22), channel_id=1, source_target_pairs={{4,0},{8,4},{12,8},{16,12},{20,16},{24,20},{28,24},{0,28},{5,1},{9... | collective-permute-start | bytes 245768 | tf_op jit(solution)/shard_map/ppermute | solution.py:22
  43.5 3.0 %collective-permute-done.2 = f32[32,5,128]{2,1,0:T(8,128)S(1)} collective-permute-done((f32[32,5,128]{2,1,0:T(8,128)S(1)}, f32[32,5,128]{2,1,0:T(8,128)S(1)}, u32[]{:S(2)}, u32[]{:S(2)}) %collective-permute-start.2) | collective-permute-done | bytes 81952 | tf_op jit(solution)/shard_map/ppermute | solution.py:20
  46.5 0.8 %collective-permute-done.3 = f32[32,5,128]{2,1,0:T(8,128)S(1)} collective-permute-done((f32[32,5,128]{2,1,0:T(8,128)S(1)}, f32[32,5,128]{2,1,0:T(8,128)S(1)}, u32[]{:S(2)}, u32[]{:S(2)}) %collective-permute-start.3) | collective-permute-done | bytes 81952 | tf_op jit(solution)/shard_map/ppermute | solution.py:22
  47.5 0.2 fusion.26
  47.7 0.2 pad_maximum_fusion
  47.9 0.8 %gather_fusion.1 = f32[128,9,128]{2,1,0:T(8,128)S(1)} fusion(f32[96,9,128]{2,1,0:T(8,128)S(1)} %pad_maximum_fusion, s32[1024]{0:T(1024)S(1)} %pad_clamp_fusion), kind=kCustom, calls=%fused_computation.1 | custom fusion | bytes 1180160 | tf_op jit(solution)/shard_map/jit(_take)/gather | solution.py:119
  48.7 0.3 copy_select_fusion
  49.0 24.9 %while.21 = (s32[]{:T(128)}, f32[4,8,4,128]{3,2,1,0:T(4,128)S(1)}, f32[4,8,4,9,128]{4,2,1,3,0:T(4,128)S(1)}, s32[4,8]{1,0:T(4,128)S(1)}, f32[4,8,128]{2,1,0:T(8,...) while((s32[]{:T(128)}, f32[4,8,4,128]{3,2,1,0:T(4,128)S(1)}, ...), condition=%wide.region_9.10_spmd, body=%wide.region_4.9_spmd.sunk | while | flops 23076928 | bytes 17969624 | solution.py:73
  49.1 1.1 %fusion.59 = f32[8,4,128,128]{3,2,1,0:T(8,128)S(1)} fusion(f32[8,4,3,128]{3,2,1,0:T(4,128)S(1)} %copy.62, f32[8,3,128]{2,1,0:T(4,128)S(1)} %get-tuple-element.273), kind=kLoop, calls=%fused_computation.25.clone.1 | loop fusion | flops 4194304 | bytes 2158592 | tf_op jit(solution)/shard_map/while/body/eval_jaxpr/vmap(vmap())/reduce_sum | solution.py:31
  50.2 0.1 fusion.55
  50.3 0.1 fusion.56
  50.4 2.1 %add_multiply_fusion.2 = (f32[8,4,128,128]{3,2,1,0:T(8,128)S(1)}, f32[8,4,128,128]{3,2,1,0:T(8,128)S(1)}) fusion(f32[8,4,128]{2,1,0:T(4,128)S(1)} %get-tuple-element.271, f32[8,128]{1,0:T(8,128)S(1)} %fusion.57, f32[8,4,128,128]{3,2,1,0:T(8,128)S(1)} %fusion.59, f32[8,4,128]{2,1,0:T(4,128)S(1)} %get-tuple-element.274, ...), kind=kLoop, calls=%fused_computation.35.clone.1 | loop fusion | flops 8912896 | bytes 6348800 | tf_op jit(solution)/shard_map/while/body/eval_jaxpr/vmap()/mul | solution.py:56
  52.6 2.3 %fusion.60 = (f32[8,3,128]{2,1,0:T(4,128)S(1)}, f32[8,4,128,128]{3,2,1,0:T(8,128)S(1)}) fusion(f32[8,4,128,128]{3,2,1,0:T(8,128)S(1)} %get-tuple-element.277, f32[8,4,3,128]{3,2,1,0:T(4,128)S(1)} %copy.62, f32[8,3,128]{2,1,0:T(4,128)S(1)} %get-tuple-element.273, f32[8,4,3,128]{3,2,1,0:T(4,128)S(1)} %copy.63, f32[8,3,128]{2,1,0:T(4,128)S(1)} %get-tuple-element.279), kind=kLoop, calls=%fused_computation.26.clone.1 | loop fusion | flops 8909824 | bytes 4329472 | tf_op jit(solution)/shard_map/while/body/eval_jaxpr/vmap()/reduce_sum | solution.py:57
  54.9 0.3 multiply_reduce_fusion.5
  55.3 1.1 %fusion.59 = f32[8,4,128,128]{3,2,1,0:T(8,128)S(1)} fusion(f32[8,4,3,128]{3,2,1,0:T(4,128)S(1)} %copy.62, f32[8,3,128]{2,1,0:T(4,128)S(1)} %get-tuple-element.273), kind=kLoop, calls=%fused_computation.25.clone.1 | loop fusion | flops 4194304 | bytes 2158592 | tf_op jit(solution)/shard_map/while/body/eval_jaxpr/vmap(vmap())/reduce_sum | solution.py:31
  56.5 0.1 fusion.56
  56.6 2.1 %add_multiply_fusion.2 = (f32[8,4,128,128]{3,2,1,0:T(8,128)S(1)}, f32[8,4,128,128]{3,2,1,0:T(8,128)S(1)}) fusion(f32[8,4,128]{2,1,0:T(4,128)S(1)} %get-tuple-element.271, f32[8,128]{1,0:T(8,128)S(1)} %fusion.57, f32[8,4,128,128]{3,2,1,0:T(8,128)S(1)} %fusion.59, f32[8,4,128]{2,1,0:T(4,128)S(1)} %get-tuple-element.274, ...), kind=kLoop, calls=%fused_computation.35.clone.1 | loop fusion | flops 8912896 | bytes 6348800 | tf_op jit(solution)/shard_map/while/body/eval_jaxpr/vmap()/mul | solution.py:56
  58.8 2.3 %fusion.60 = (f32[8,3,128]{2,1,0:T(4,128)S(1)}, f32[8,4,128,128]{3,2,1,0:T(8,128)S(1)}) fusion(f32[8,4,128,128]{3,2,1,0:T(8,128)S(1)} %get-tuple-element.277, f32[8,4,3,128]{3,2,1,0:T(4,128)S(1)} %copy.62, f32[8,3,128]{2,1,0:T(4,128)S(1)} %get-tuple-element.273, f32[8,4,3,128]{3,2,1,0:T(4,128)S(1)} %copy.63, f32[8,3,128]{2,1,0:T(4,128)S(1)} %get-tuple-element.279), kind=kLoop, calls=%fused_computation.26.clone.1 | loop fusion | flops 8909824 | bytes 4329472 | tf_op jit(solution)/shard_map/while/body/eval_jaxpr/vmap()/reduce_sum | solution.py:57
  61.1 0.3 multiply_reduce_fusion.5
  61.6 1.1 %fusion.59 = f32[8,4,128,128]{3,2,1,0:T(8,128)S(1)} fusion(f32[8,4,3,128]{3,2,1,0:T(4,128)S(1)} %copy.62, f32[8,3,128]{2,1,0:T(4,128)S(1)} %get-tuple-element.273), kind=kLoop, calls=%fused_computation.25.clone.1 | loop fusion | flops 4194304 | bytes 2158592 | tf_op jit(solution)/shard_map/while/body/eval_jaxpr/vmap(vmap())/reduce_sum | solution.py:31
  62.7 0.1 fusion.56
  62.8 2.1 %add_multiply_fusion.2 = (f32[8,4,128,128]{3,2,1,0:T(8,128)S(1)}, f32[8,4,128,128]{3,2,1,0:T(8,128)S(1)}) fusion(f32[8,4,128]{2,1,0:T(4,128)S(1)} %get-tuple-element.271, f32[8,128]{1,0:T(8,128)S(1)} %fusion.57, f32[8,4,128,128]{3,2,1,0:T(8,128)S(1)} %fusion.59, f32[8,4,128]{2,1,0:T(4,128)S(1)} %get-tuple-element.274, ...), kind=kLoop, calls=%fused_computation.35.clone.1 | loop fusion | flops 8912896 | bytes 6348800 | tf_op jit(solution)/shard_map/while/body/eval_jaxpr/vmap()/mul | solution.py:56
  65.0 2.3 %fusion.60 = (f32[8,3,128]{2,1,0:T(4,128)S(1)}, f32[8,4,128,128]{3,2,1,0:T(8,128)S(1)}) fusion(f32[8,4,128,128]{3,2,1,0:T(8,128)S(1)} %get-tuple-element.277, f32[8,4,3,128]{3,2,1,0:T(4,128)S(1)} %copy.62, f32[8,3,128]{2,1,0:T(4,128)S(1)} %get-tuple-element.273, f32[8,4,3,128]{3,2,1,0:T(4,128)S(1)} %copy.63, f32[8,3,128]{2,1,0:T(4,128)S(1)} %get-tuple-element.279), kind=kLoop, calls=%fused_computation.26.clone.1 | loop fusion | flops 8909824 | bytes 4329472 | tf_op jit(solution)/shard_map/while/body/eval_jaxpr/vmap()/reduce_sum | solution.py:57
  67.4 0.3 multiply_reduce_fusion.5
  67.8 1.1 %fusion.59 = f32[8,4,128,128]{3,2,1,0:T(8,128)S(1)} fusion(f32[8,4,3,128]{3,2,1,0:T(4,128)S(1)} %copy.62, f32[8,3,128]{2,1,0:T(4,128)S(1)} %get-tuple-element.273), kind=kLoop, calls=%fused_computation.25.clone.1 | loop fusion | flops 4194304 | bytes 2158592 | tf_op jit(solution)/shard_map/while/body/eval_jaxpr/vmap(vmap())/reduce_sum | solution.py:31
  69.0 0.1 fusion.56
  69.1 2.1 %add_multiply_fusion.2 = (f32[8,4,128,128]{3,2,1,0:T(8,128)S(1)}, f32[8,4,128,128]{3,2,1,0:T(8,128)S(1)}) fusion(f32[8,4,128]{2,1,0:T(4,128)S(1)} %get-tuple-element.271, f32[8,128]{1,0:T(8,128)S(1)} %fusion.57, f32[8,4,128,128]{3,2,1,0:T(8,128)S(1)} %fusion.59, f32[8,4,128]{2,1,0:T(4,128)S(1)} %get-tuple-element.274, ...), kind=kLoop, calls=%fused_computation.35.clone.1 | loop fusion | flops 8912896 | bytes 6348800 | tf_op jit(solution)/shard_map/while/body/eval_jaxpr/vmap()/mul | solution.py:56
  71.2 2.3 %fusion.60 = (f32[8,3,128]{2,1,0:T(4,128)S(1)}, f32[8,4,128,128]{3,2,1,0:T(8,128)S(1)}) fusion(f32[8,4,128,128]{3,2,1,0:T(8,128)S(1)} %get-tuple-element.277, f32[8,4,3,128]{3,2,1,0:T(4,128)S(1)} %copy.62, f32[8,3,128]{2,1,0:T(4,128)S(1)} %get-tuple-element.273, f32[8,4,3,128]{3,2,1,0:T(4,128)S(1)} %copy.63, f32[8,3,128]{2,1,0:T(4,128)S(1)} %get-tuple-element.279), kind=kLoop, calls=%fused_computation.26.clone.1 | loop fusion | flops 8909824 | bytes 4329472 | tf_op jit(solution)/shard_map/while/body/eval_jaxpr/vmap()/reduce_sum | solution.py:57
  73.6 0.3 multiply_reduce_fusion.5
  74.0 0.7 copy.50
  74.7 0.1 concatenate.29
  74.8 0.7 broadcast_multiply_fusion
  (101 shorter events, 2.1 us)
Async XLA Ops:
  0.6 1.0 %copy-start = (f32[32,16,128]{2,1,0:T(8,128)S(1)}, f32[32,16,128]{2,1,0:T(8,128)}, u32[]{:S(2)}) copy-start(f32[32,16,128]{2,1,0:T(8,128)} %param.8) | copy-start | bytes 786436
  3.5 10.3 %all-to-all-start = ((f32[32,16,128]{2,1,0:T(8,128)}), f32[32,16,128]{2,1,0:T(8,128)S(1)}, u32[]{:S(2)}, u32[]{:S(2)}) async-start(f32[32,16,128]{2,1,0:T(8,128)} %copy.44), calls=%async_computation | async-start | bytes 524288 | tf_op jit(solution)/shard_map/all_to_all | solution.py:101
  13.9 8.6 %collective-permute-start = (f32[32,5,128]{2,1,0:T(8,128)S(1)}, f32[32,5,128]{2,1,0:T(8,128)S(1)}, u32[]{:S(2)}, u32[]{:S(2)}) collective-permute-start(f32[32,5,128]{2,1,0:T(8,128)S(1)} %pad_maximum_fusion.5), channel_id=1, source_target_pairs={{0,4},{4,8},{8,12},{12,16},{16,20},{20,24},{24,28},{28,0},{1,5},{5... | collective-permute-start | bytes 245768 | tf_op jit(solution)/shard_map/ppermute | solution.py:20
  16.0 7.7 %collective-permute-start.1 = (f32[32,5,128]{2,1,0:T(8,128)S(1)}, f32[32,5,128]{2,1,0:T(8,128)S(1)}, u32[]{:S(2)}, u32[]{:S(2)}) collective-permute-start(f32[32,5,128]{2,1,0:T(8,128)S(1)} %pad_maximum_fusion.5), channel_id=1, source_target_pairs={{4,0},{8,4},{12,8},{16,12},{20,16},{24,20},{28,24},{0,28},{5,1},{9... | collective-permute-start | bytes 245768 | tf_op jit(solution)/shard_map/ppermute | solution.py:22
  38.7 7.8 %collective-permute-start.2 = (f32[32,5,128]{2,1,0:T(8,128)S(1)}, f32[32,5,128]{2,1,0:T(8,128)S(1)}, u32[]{:S(2)}, u32[]{:S(2)}) collective-permute-start(f32[32,5,128]{2,1,0:T(8,128)S(1)} %fusion.22), channel_id=1, source_target_pairs={{0,4},{4,8},{8,12},{12,16},{16,20},{20,24},{24,28},{28,0},{1,5},{5... | collective-permute-start | bytes 245768 | tf_op jit(solution)/shard_map/ppermute | solution.py:20
  38.9 8.5 %collective-permute-start.3 = (f32[32,5,128]{2,1,0:T(8,128)S(1)}, f32[32,5,128]{2,1,0:T(8,128)S(1)}, u32[]{:S(2)}, u32[]{:S(2)}) collective-permute-start(f32[32,5,128]{2,1,0:T(8,128)S(1)} %fusion.22), channel_id=1, source_target_pairs={{4,0},{8,4},{12,8},{16,12},{20,16},{24,20},{28,24},{0,28},{5,1},{9... | collective-permute-start | bytes 245768 | tf_op jit(solution)/shard_map/ppermute | solution.py:22
where the time goes:
time: 75.8 us; the launch traced here: 75.5 us
  other arithmetic  40.6 us (54%)
  starting transfers between devices  14.2 us (19%)
  waiting for transfers between devices  12 us (16%)
  local copies, waits for them, and re-layouts  6.13 us (8%)
  matrix products  1.01 us (1%)
  between operations  0.81 us (1%)
  loops' own time  0.76 us (1%)
    reduce_sum x4, other arithmetic, slot_force(): accel = -jnp.sum(pairing[:, None] * offset, axis=(0, 3))  9.27 us
    reduce_sum x8, other arithmetic, pair_terms(): spacing = jnp.sqrt(jnp.sum(offset * offset, axis=0))  8.58 us
    mul x4, other arithmetic, slot_force(): pairing = factor * (self_ratio[None, :, None] + picked[:, 8][:, None, :])  8.53 us
    reduce_sum x4, other arithmetic, slot_density(): jnp.sum(weight * (picked[:, 3] * active[:, None])[:, None, :], axis=(0, 2))  8.32 us
    ppermute x2, starting transfers between devices, extended(): lax.ppermute(head, axis, [((i + 1) % count, i) for i in range(count)])  7.7 us
    ppermute x2, waiting for transfers between devices, extended(): lax.ppermute(tail, axis, [(i, (i + 1) % count) for i in range(count)])  6.3 us
    all_to_all x1, starting transfers between devices, body(): lax.all_to_all(packed, 'tile', split_axis=0, concat_axis=0, tiled=True)  4.24 us
    all_to_all x1, waiting for transfers between devices, body(): lax.all_to_all(packed, 'tile', split_axis=0, concat_axis=0, tiled=True)  3.62 us
  transfers between devices with their start and end apart: 5, of which 5 were waited for; matrix products, arithmetic and copies ran while one was open for 3% of the time, Pallas kernels for 0%

commit v1 on v0

v1 whole, which is shorter than its diff:
```python
import math

import jax
import jax.numpy as jnp
from jax import lax
from jax.experimental import pallas as pl
from jax.experimental.pallas import tpu as pltpu
from jax.sharding import PartitionSpec as P

ADIABATIC = 5.0 / 3.0
TIMESTEP = 0.5
KERNEL_NORM = 21.0 / (16.0 * math.pi)
WEIGHT_FACTOR = 8.0 * KERNEL_NORM
SLOPE_FACTOR = -5.0 * 32.0 * KERNEL_NORM
CENTRE = 1.0
LANES = 128
UNROLL = 4

F32 = jnp.float32
BF16 = jnp.bfloat16


def vmem_spec():
    return pl.BlockSpec(memory_space=pltpu.VMEM)


def smem_spec():
    return pl.BlockSpec(memory_space=pltpu.SMEM)


def kernel_call(kernel, ins, outs, scratch, flops, name):
    specs = [smem_spec() if kind == "s" else vmem_spec() for kind, _ in ins]
    arrays = [array for _, array in ins]
    moved = sum(a.size * 4 for a in arrays) + sum(math.prod(o) * 4 for o in outs)
    return pl.pallas_call(
        kernel,
        out_shape=[jax.ShapeDtypeStruct(o, F32) for o in outs],
        in_specs=specs,
        out_specs=[vmem_spec() for _ in outs],
        scratch_shapes=scratch,
        compiler_params=pltpu.CompilerParams(vmem_limit_bytes=48 * 1024 * 1024),
        cost_estimate=pl.CostEstimate(flops=flops, bytes_accessed=moved, transcendentals=0),
        name=name,
    )(*arrays)


def partner_tile(index, step, count):
    if count & (count - 1) == 0:
        return index ^ step
    return (index + step) % count


def source_tile(index, step, count):
    if count & (count - 1) == 0:
        return index ^ step
    return (index + count - step) % count


def rounded(value):
    return value.astype(BF16).astype(F32)


def row_index():
    return lax.broadcasted_iota(jnp.int32, (8, LANES), 0)


def sum_rows(tile):
    tile = tile + pltpu.roll(tile, 4, 0)
    tile = tile + pltpu.roll(tile, 2, 0)
    return tile + pltpu.roll(tile, 1, 0)


def geometry_parts(tile, row):
    hi = rounded(tile)
    lo = rounded(tile - hi)
    point = jnp.where(row < 3, hi + lo, 0.0)
    norm = sum_rows(point * point)
    n1 = rounded(norm)
    n2 = rounded(norm - n1)
    n3 = rounded(norm - n1 - n2)
    return hi, lo, n1, n2, n3


def far_features(tile, row):
    hi, lo, n1, n2, n3 = geometry_parts(tile, row)
    ones = jnp.ones_like(tile)

    def block(part):
        return jnp.where(row < 3, part, jnp.where(row < 6, pltpu.roll(part, 3, 0), jnp.where(row == 6, ones, part)))

    b0, b1 = block(hi), block(lo)
    b2 = jnp.where(row == 0, n1, jnp.where(row == 1, n2, jnp.where(row == 2, n3, jnp.where(row < 6, ones, 0.0))))
    zero = jnp.zeros_like(tile)
    low = row < 6
    left = jnp.concatenate([jnp.where(low, -2.0 * b0, 0.0), jnp.where(low, -2.0 * b1, 0.0), b2, zero], axis=0)
    right = jnp.concatenate([jnp.where(low, 0.0, b0), jnp.where(low, 0.0, b1), zero, zero], axis=0)
    return left.astype(BF16), right.astype(BF16)


def near_features(tile, row):
    hi, lo, n1, n2, n3 = geometry_parts(tile, row)
    ones = jnp.ones_like(tile)
    shifted = pltpu.roll(lo, 3, 0)

    def block(part):
        return jnp.where(row < 3, hi, jnp.where(row < 6, shifted, jnp.where(row == 6, pltpu.roll(part, 7, 0), ones)))

    b2 = jnp.where(row < 3, ones, jnp.where(row == 3, n1, jnp.where(row == 4, n2, jnp.where(row == 5, n3, 0.0))))
    stacked = jnp.concatenate([block(hi), block(lo), b2, jnp.zeros_like(tile)], axis=0)
    return jnp.transpose(stacked).astype(BF16)


def store_far(far_ref, index, tile, row):
    left, right = far_features(tile, row)
    far_ref[index, :, 0:LANES] = left
    far_ref[index, :, LANES : 2 * LANES] = right


def dummy_tile(row):
    return jnp.where(row == 7, 1.0, jnp.zeros((8, LANES), F32))


def split3(value):
    hi = rounded(value)
    mid = rounded(value - hi)
    return hi, mid, rounded(value - hi - mid)


def closeness(near, far):
    both = jnp.dot(near, far, preferred_element_type=F32)
    squared = jnp.maximum(both[:, 0:LANES], 1e-24)
    inverse = pl.reciprocal(both[:, LANES : 2 * LANES], approx=True)
    remain = jnp.maximum(1.0 - squared * lax.rsqrt(squared) * inverse, 0.0)
    scaled = inverse * remain
    return inverse, remain, scaled * scaled * scaled


def build_list(neighbours_ref, counts_ref, near_list, far_list, slots, width):
    def fill(i, total):
        used = counts_ref[i]
        for k in range(width):
            near_list[total] = i
            far_list[total] = neighbours_ref[i, k]
            total = total + (k < used).astype(jnp.int32)
        return total

    total = lax.fori_loop(0, slots, fill, jnp.int32(0))
    for k in range(UNROLL):
        near_list[total + k] = slots
        far_list[total + k] = 3 * slots
    return total


def pack_kernel(tiles, cap, dest_ref, particles_ref, *refs):
    outs, packed = refs[:-1], refs[-1]
    packed[...] = jnp.zeros_like(packed)
    me = lax.axis_index("tile")

    def place(b, carry):
        dest = dest_ref[b]
        owner = lax.div(dest, cap)
        if tiles & (tiles - 1) == 0:
            step = owner ^ me
        else:
            step = lax.rem(owner + tiles - me, tiles)
        packed[step * cap + lax.rem(dest, cap)] = particles_ref[b]
        return carry

    lax.fori_loop(0, particles_ref.shape[0], place, 0, unroll=4)
    for k in range(tiles):
        outs[k][...] = packed[k * cap : (k + 1) * cap]


def state_kernel(tiles, cap, *refs):
    parts, (states_ref, halo_ref) = refs[:tiles], refs[tiles:]
    me = lax.axis_index("tile")
    row = row_index()
    for k in range(tiles):
        base = source_tile(me, k, tiles) * cap
        for j in range(cap):
            top = parts[k][j, 0:8, :]
            low = parts[k][j, 8:16, :]
            states_ref[base + j, 0:8, :] = top
            states_ref[base + j, 8:16, :] = low
            smooth = jnp.where(pltpu.roll(top, 1, 0) > 0, pltpu.roll(low, 7, 0), 1.0)
            halo_ref[base + j] = jnp.where(row < 3, top - CENTRE, jnp.where(row == 7, smooth, top))


def region_base(region, slots):
    upper = lax.rem(lax.axis_index("slab"), 2) == 0
    first = jnp.where(upper, 2 * slots, 0)
    return first if region == 0 else 2 * slots - first


def fill_far(far_ref, own_ref, side_refs, bases, slots):
    row = row_index()
    far_ref[3 * slots, :, :] = jnp.zeros_like(far_ref[3 * slots, :, :])
    store_far(far_ref, 3 * slots, dummy_tile(row), row)

    def fill(i, carry):
        store_far(far_ref, slots + i, own_ref[i], row)
        for side_ref, base in zip(side_refs, bases):
            store_far(far_ref, base + i, side_ref[i], row)
        return carry

    lax.fori_loop(0, slots, fill, 0, unroll=2)


def fill_near(near_ref, own_ref, slots):
    row = row_index()
    near_ref[slots] = near_features(dummy_tile(row), row)

    def fill(i, carry):
        near_ref[i] = near_features(own_ref[i], row)
        return carry

    lax.fori_loop(0, slots, fill, 0, unroll=2)


def density_kernel(slots, width, neighbours_ref, counts_ref, own_ref, first_ref, second_ref, states_ref,
                   density_ref, ratio_ref, near_ref, far_ref, sum_ref, mass_ref, near_list, far_list):
    total = build_list(neighbours_ref, counts_ref, near_list, far_list, slots, width)
    bases = [region_base(r, slots) for r in range(2)]
    fill_far(far_ref, own_ref, (first_ref, second_ref), bases, slots)
    fill_near(near_ref, own_ref, slots)
    mass_ref[3 * slots] = jnp.zeros((8, LANES), F32)

    def masses(i, carry):
        for ref, base in ((own_ref, slots), (first_ref, bases[0]), (second_ref, bases[1])):
            mass_ref[base + i] = jnp.broadcast_to(ref[i, 6:7, :], (8, LANES))
        return carry

    lax.fori_loop(0, slots, masses, 0, unroll=4)
    sum_ref[...] = jnp.zeros_like(sum_ref)

    def pairs(g, carry):
        for u in range(UNROLL):
            i = near_list[g * UNROLL + u]
            c = far_list[g * UNROLL + u]
            inverse, remain, cubed = closeness(near_ref[i], far_ref[c])
            weight = cubed * (remain * (5.0 - 4.0 * remain))
            mass = mass_ref[c]
            sum_ref[i] += (weight.reshape(LANES // 8, 8, LANES) * mass[None]).reshape(LANES, LANES)
        return carry

    lax.fori_loop(0, lax.div(total + UNROLL - 1, UNROLL), pairs, 0)
    ones = jnp.ones((8, LANES), BF16)

    def reduce(i, carry):
        part = sum_ref[i]
        hi = part.astype(BF16)
        lo = (part - hi.astype(F32)).astype(BF16)
        dims = (((1,), (1,)), ((), ()))
        summed = lax.dot_general(ones, hi, dims, preferred_element_type=F32) + lax.dot_general(
            ones, lo, dims, preferred_element_type=F32
        )
        density = WEIGHT_FACTOR * summed[0:1, :]
        density_ref[pl.ds(i, 1), :] = density
        energy = states_ref[i, 7:8, :]
        mass = states_ref[i, 6:7, :]
        safe = jnp.where(mass > 0, density, 1.0)
        ratio_ref[pl.ds(i, 1), :] = (ADIABATIC - 1.0) * density * energy / (safe * safe)
        return carry

    lax.fori_loop(0, slots, reduce, 0, unroll=4)


def force_features(tile, ratio, row):
    mass = jnp.broadcast_to(tile[6:7, :], (8, LANES))
    dotted = sum_rows(jnp.where(row < 3, tile * pltpu.roll(tile, 5, 0), 0.0))
    plain = jnp.where(row < 6, tile, jnp.where(row == 6, 1.0, dotted)) * mass
    heavy = jnp.where((row < 3) | (row == 6), plain * ratio, 0.0)
    p, h = split3(plain), split3(heavy)
    return jnp.concatenate([p[0], h[0], p[1], h[1], p[2], h[2]], axis=0).astype(BF16)


def force_kernel(slots, width, neighbours_ref, counts_ref, own_ref, first_ref, second_ref, states_ref,
                 density_ref, ratio_ref, first_ratio_ref, second_ratio_ref,
                 updated_ref, derived_ref, near_ref, far_ref, field_ref, sum_ref, near_list, far_list):
    total = build_list(neighbours_ref, counts_ref, near_list, far_list, slots, width)
    bases = [region_base(r, slots) for r in range(2)]
    row = row_index()
    fill_far(far_ref, own_ref, (first_ref, second_ref), bases, slots)
    fill_near(near_ref, own_ref, slots)
    field_ref[3 * slots] = jnp.zeros((48, LANES), BF16)

    def fields(i, carry):
        for ref, ratios, base in (
            (own_ref, ratio_ref, slots),
            (first_ref, first_ratio_ref, bases[0]),
            (second_ref, second_ratio_ref, bases[1]),
        ):
            field_ref[base + i] = force_features(ref[i], ratios[pl.ds(i, 1), :], row)
        return carry

    lax.fori_loop(0, slots, fields, 0, unroll=2)
    sum_ref[...] = jnp.zeros_like(sum_ref)

    def pairs(g, carry):
        for u in range(UNROLL):
            i = near_list[g * UNROLL + u]
            c = far_list[g * UNROLL + u]
            inverse, remain, cubed = closeness(near_ref[i], far_ref[c])
            slope = cubed * (inverse * inverse)
            hi = slope.astype(BF16)
            lo = (slope - hi.astype(F32)).astype(BF16)
            dims = (((1,), (1,)), ((), ()))
            field = field_ref[c]
            both = lax.dot_general(field, hi, dims, preferred_element_type=F32) + lax.dot_general(
                field, lo, dims, preferred_element_type=F32
            )
            sum_ref[i] += both[0:16] + (both[16:32] + both[32:48])
        return carry

    lax.fori_loop(0, lax.div(total + UNROLL - 1, UNROLL), pairs, 0)

    def finish(i, carry):
        tile = own_ref[i]
        ratio = ratio_ref[pl.ds(i, 1), :]
        density = density_ref[pl.ds(i, 1), :]
        plain = SLOPE_FACTOR * sum_ref[i, 0:8, :]
        heavy = SLOPE_FACTOR * sum_ref[i, 8:16, :]
        spread = tile * plain[6:7, :] - plain
        change = -(ratio * spread + (tile * heavy[6:7, :] - heavy))
        crossed = tile * pltpu.roll(spread, 5, 0) - pltpu.roll(tile, 5, 0) * plain
        heating = ratio * (sum_rows(jnp.where(row < 3, crossed, 0.0)) + plain[7:8, :])
        top = states_ref[i, 0:8, :]
        low = states_ref[i, 8:16, :]
        present = (top[6:7, :] > 0).astype(F32)
        moved = top + TIMESTEP * pltpu.roll(change, 3, 0)
        heated = top + TIMESTEP * heating
        placed = top + TIMESTEP * pltpu.roll(moved, 5, 0)
        fresh = jnp.where(row < 3, placed, jnp.where(row < 6, moved, jnp.where(row == 6, top, heated)))
        updated_ref[i, 0:8, :] = fresh * present
        updated_ref[i, 8:16, :] = low * present
        shown = jnp.where(row == 0, density, jnp.where(row < 4, pltpu.roll(change, 1, 0), heating)) * present
        derived_ref[i] = shown[0:5, :]
        return carry

    lax.fori_loop(0, slots, finish, 0, unroll=2)


def body(tiles, slabs, particles, dest_slot, neighbours, counts):
    bins, floats, lanes = particles.shape
    slots, width = neighbours.shape
    cap = slots // tiles
    chunk = (cap, floats, lanes)
    packed = kernel_call(
        lambda *refs: pack_kernel(tiles, cap, *refs),
        [("s", dest_slot), ("v", particles)],
        [chunk] * tiles,
        [pltpu.VMEM((slots, floats, lanes), F32)],
        0,
        "pack",
    )
    parts = [packed[0]] + [
        lax.ppermute(packed[k], "tile", [(t, partner_tile(t, k, tiles)) for t in range(tiles)])
        for k in range(1, tiles)
    ]
    states, halo = kernel_call(
        lambda *refs: state_kernel(tiles, cap, *refs),
        [("v", part) for part in parts],
        [(slots, floats, lanes), (slots, 8, lanes)],
        [],
        0,
        "states",
    )
    first_pairs = [(s, s ^ 1) for s in range(slabs)]
    second_pairs = [(s, (((s + 1) ^ 1) - 1) % slabs) for s in range(slabs)]

    def both_sides(array):
        second = lax.ppermute(array, "slab", second_pairs)
        first = lax.ppermute(array, "slab", first_pairs)
        return first, second

    first, second = both_sides(halo)
    pair_terms = slots * width * lanes * lanes
    tables = [
        pltpu.VMEM((slots + 1, lanes, 32), BF16),
        pltpu.VMEM((3 * slots + 1, 32, 2 * lanes), BF16),
    ]
    lists = [pltpu.SMEM((slots * width + UNROLL,), jnp.int32)] * 2
    density, ratio = kernel_call(
        lambda *refs: density_kernel(slots, width, *refs),
        [("s", neighbours), ("s", counts), ("v", halo), ("v", first), ("v", second), ("v", states)],
        [(slots, lanes)] * 2,
        tables
        + [pltpu.VMEM((slots + 1, lanes, lanes), F32), pltpu.VMEM((3 * slots + 1, 8, lanes), F32)]
        + lists,
        30 * pair_terms,
        "density",
    )
    first_ratio, second_ratio = both_sides(ratio)
    updated, derived = kernel_call(
        lambda *refs: force_kernel(slots, width, *refs),
        [("s", neighbours), ("s", counts), ("v", halo), ("v", first), ("v", second), ("v", states),
         ("v", density), ("v", ratio), ("v", first_ratio), ("v", second_ratio)],
        [(slots, floats, lanes), (slots, 5, lanes)],
        tables
        + [pltpu.VMEM((3 * slots + 1, 48, lanes), BF16), pltpu.VMEM((slots + 1, 16, lanes), F32)]
        + lists,
        30 * pair_terms,
        "force",
    )
    return updated, derived


def solution(mesh):
    tiles, slabs = mesh.shape["tile"], mesh.shape["slab"]
    in_specs = (
        P(("slab", "tile"), None, None),
        P(("slab", "tile")),
        P(("slab", "tile"), None),
        P(("slab", "tile")),
    )
    out_specs = (P(("slab", "tile"), None, None), P(("slab", "tile"), None, None))
    return jax.shard_map(
        lambda *args: body(tiles, slabs, *args), mesh=mesh, in_specs=in_specs, out_specs=out_specs, check_vma=False
    )
```

time: 75.8 us -> 67.3 us (0.89)
  other arithmetic: 40.6 us -> 0 us
  Pallas kernels: 0 us -> 40 us
  starting transfers between devices: 14.2 us -> 8.37 us
  waiting for transfers between devices: 12 us -> 16.4 us
  local copies, waits for them, and re-layouts: 6.13 us -> 2.34 us
  matrix products: 1.01 us -> 0 us
  loops' own time: 0.76 us -> 0 us
    pallas_call x0 -> x4, Pallas kernels: none -> 40 us  [kernel_call(): pl.pallas_call(kernel, out_shape=[jax.ShapeDtypeStruct(o, F32) for o in o...]
    reduce_sum x20 -> x0, other arithmetic: 27.2 us -> none  [the longest x4 9.27 us: slot_force(): accel = -jnp.sum(pairing[:, None] * offset, axis=(0, 3))]
    mul x15 -> x0, other arithmetic: 9.68 us -> none  [the longest x4 8.53 us: slot_force(): pairing = factor * (self_ratio[None, :, None] + picked[:, 8][:, None, :])]
    ppermute x4 -> x7, waiting for transfers between devices: 8.41 us -> 16.4 us  [the longest x2 9.72 us: both_sides(): second = lax.ppermute(array, 'slab', second_pairs)]
    all_to_all x1 -> x0, starting transfers between devices: 4.24 us -> none  [body(): lax.all_to_all(packed, 'tile', split_axis=0, concat_axis=0, tiled=True)]
    all_to_all x1 -> x0, waiting for transfers between devices: 3.62 us -> none  [body(): lax.all_to_all(packed, 'tile', split_axis=0, concat_axis=0, tiled=True)]
    ppermute x4 -> x7, starting transfers between devices: 10 us -> 8.37 us  [the longest x2 4.65 us: both_sides(): second = lax.ppermute(array, 'slab', second_pairs)]
    gather x2 -> x0, local copies, waits for them, and re-layouts: 1.52 us -> none  [the longest x1 0.76 us: body(): dense_pick = jnp.take(gathered, neighbours, axis=0)]
  transfers between devices with their start and end apart: 5 -> 7, of which waited for: 5 -> 5; matrix products, arithmetic and copies ran while one was open for 3% -> 0% of each run, Pallas kernels for 0% -> 0%
where the time goes in v1:
time: 67.3 us; the launch traced here: 67.8 us
  Pallas kernels  40 us (59%)
  waiting for transfers between devices  16.4 us (24%)
  starting transfers between devices  8.37 us (12%)
  local copies, waits for them, and re-layouts  2.34 us (3%)
    pallas_call x4, Pallas kernels, kernel_call(): pl.pallas_call(kernel, out_shape=[jax.ShapeDtypeStruct(o, F32) for o in o...  40 us
    ppermute x2, waiting for transfers between devices, both_sides(): second = lax.ppermute(array, 'slab', second_pairs)  9.72 us
    ppermute x2, starting transfers between devices, both_sides(): second = lax.ppermute(array, 'slab', second_pairs)  4.65 us
    ppermute x3, waiting for transfers between devices, body(): lax.ppermute(packed[k], 'tile', [(t, partner_tile(t, k, tiles)) for t in...  3.98 us
    ppermute x3, starting transfers between devices, body(): lax.ppermute(packed[k], 'tile', [(t, partner_tile(t, k, tiles)) for t in...  3.18 us
    ppermute x2, waiting for transfers between devices, both_sides(): first = lax.ppermute(array, 'slab', first_pairs)  2.71 us
    unnamed x9, local copies, waits for them, and re-layouts  1.69 us
  transfers between devices with their start and end apart: 7, of which 5 were waited for; matrix products, arithmetic and copies ran while one was open for 0% of the time, Pallas kernels for 0%

profile of v1, /device:TPU:0, one launch (start us, length us, event | category | flops | bytes accessed | tf_op | source)
XLA Modules:
  0.0 67.8 jit_solution(142395714376883611)
XLA Ops:
  0.6 0.0 copy-start
  0.6 0.9 %copy-done = f32[32,16,128]{2,1,0:T(8,128)S(1)} copy-done((f32[32,16,128]{2,1,0:T(8,128)S(1)}, f32[32,16,128]{2,1,0:T(8,128)}, u32[]{:S(2)}) %copy-start) | copy-done | bytes 262168
  1.6 0.0 copy-start.2
  1.6 0.7 copy-done.2
  2.2 0.7 %pack.1 = (f32[8,16,128]{2,1,0:T(8,128)S(1)}, f32[8,16,128]{2,1,0:T(8,128)S(1)}, f32[8,16,128]{2,1,0:T(8,128)S(1)}, f32[8,16,128]{2,1,0:T(8,128)S(1)}) custom-call(s32[32]{0:T(128)S(1)} %copy-done.2, f32[32,16,128]{2,1,0:T(8,128)S(1)} %copy-done), custom_call_target="tpu_custom_call" | custom-call | bytes 524416 | tf_op jit(solution)/shard_map/pack/pallas_call | solution.py:35
  3.0 0.5 collective-permute-start
  3.5 2.6 %collective-permute-start.1 = (f32[8,16,128]{2,1,0:T(8,128)S(1)}, f32[8,16,128]{2,1,0:T(8,128)S(1)}, u32[]{:S(2)}, u32[]{:S(2)}) collective-permute-start(f32[8,16,128]{2,1,0:T(8,128)S(1)} %get-tuple-element.12), channel_id=1, source_target_pairs={{0,2},{1,3},{2,0},{3,1},{4,6},{5,7},{6,4},{7,5},{8,10},{9,11},{10,... | collective-permute-start | bytes 196616 | tf_op jit(solution)/shard_map/ppermute | solution.py:357
  6.1 0.1 collective-permute-start.2
  6.2 0.0 collective-permute-done.refs_1_
  6.2 2.6 %collective-permute-done.1.refs_2_ = f32[8,16,128]{2,1,0:T(8,128)S(1)} collective-permute-done((f32[8,16,128]{2,1,0:T(8,128)S(1)}, f32[8,16,128]{2,1,0:T(8,128)S(1)}, u32[]{:S(2)}, u32[]{:S(2)}) %collective-permute-start.1) | collective-permute-done | bytes 65568 | tf_op jit(solution)/shard_map/ppermute | solution.py:357
  8.8 1.4 %collective-permute-done.2.refs_3_ = f32[8,16,128]{2,1,0:T(8,128)S(1)} collective-permute-done((f32[8,16,128]{2,1,0:T(8,128)S(1)}, f32[8,16,128]{2,1,0:T(8,128)S(1)}, u32[]{:S(2)}, u32[]{:S(2)}) %collective-permute-start.2) | collective-permute-done | bytes 65568 | tf_op jit(solution)/shard_map/ppermute | solution.py:357
  10.1 0.0 copy-start.3
  10.2 4.6 %collective-permute-start.4 = (f32[32,8,128]{2,1,0:T(8,128)S(1)}, f32[32,8,128]{2,1,0:T(8,128)S(1)}, u32[]{:S(2)}, u32[]{:S(2)}) collective-permute-start(f32[32,8,128]{2,1,0:T(8,128)S(1)} %get-tuple-element.14.refs_2_), channel_id=1, source_target_pairs={{0,28},{4,8},{8,4},{12,16},{16,12},{20,24},{24,20},{28,0},{1,29},{... | collective-permute-start | bytes 393224 | tf_op jit(solution)/shard_map/ppermute | solution.py:372
  14.8 0.0 collective-permute-start.3
  14.8 0.0 copy-done.3
  14.8 0.1 copy.7.refs_0_
  14.9 0.0 copy-start.1
  14.9 3.8 %collective-permute-done.4.refs_4_ = f32[32,8,128]{2,1,0:T(8,128)S(1)} collective-permute-done((f32[32,8,128]{2,1,0:T(8,128)S(1)}, f32[32,8,128]{2,1,0:T(8,128)S(1)}, u32[]{:S(2)}, u32[]{:S(2)}) %collective-permute-start.4) | collective-permute-done | bytes 131104 | tf_op jit(solution)/shard_map/ppermute | solution.py:372
  18.7 2.7 %collective-permute-done.3.refs_3_ = f32[32,8,128]{2,1,0:T(8,128)S(1)} collective-permute-done((f32[32,8,128]{2,1,0:T(8,128)S(1)}, f32[32,8,128]{2,1,0:T(8,128)S(1)}, u32[]{:S(2)}, u32[]{:S(2)}) %collective-permute-start.3) | collective-permute-done | bytes 131104 | tf_op jit(solution)/shard_map/ppermute | solution.py:373
  21.4 0.0 copy-done.1
  21.4 13.4 %density.1 = (f32[32,128]{1,0:T(8,128)S(1)}, f32[32,128]{1,0:T(8,128)S(1)}) custom-call(s32[32,4]{1,0:T(8,128)S(1)} %copy.7.refs_0_, s32[32]{0:T(128)S(1)} %copy-done.1, f32[32,8,128]{2,1,0:T(8,128)S(1)} %get-tuple-element.14.refs_2_, f32[32,8,128]{2,1,0:T(8,128)S(1)} %collective-permute-done.3.refs_3_, f32[32,8,128]{2,1,0:T(8,128)S(1)} %collective-permute-done.4.refs_4_, ...), custom_call_target="tpu_custom_call" | custom-call | flops 62914560 | bytes 688768 | tf_op jit(solution)/shard_map/density/pallas_call | solution.py:35
  34.8 0.1 collective-permute-start.6
  34.9 0.5 collective-permute-start.5
  35.4 5.9 %collective-permute-done.6.refs_9_ = f32[32,128]{1,0:T(8,128)S(1)} collective-permute-done((f32[32,128]{1,0:T(8,128)S(1)}, f32[32,128]{1,0:T(8,128)S(1)}, u32[]{:S(2)}, u32[]{:S(2)}) %collective-permute-start.6) | collective-permute-done | bytes 16416 | tf_op jit(solution)/shard_map/ppermute | solution.py:372
  41.3 0.0 collective-permute-done.5.refs_8_
  41.3 25.8 %force.1 = (f32[32,16,128]{2,1,0:T(8,128)}, f32[32,5,128]{2,1,0:T(8,128)S(1)}) custom-call(s32[32,4]{1,0:T(8,128)S(1)} %copy.7.refs_0_, s32[32]{0:T(128)S(1)} %copy-done.1, f32[32,8,128]{2,1,0:T(8,128)S(1)} %get-tuple-element.14.refs_2_, f32[32,8,128]{2,1,0:T(8,128)S(1)} %collective-permute-done.3.refs_3_, f32[32,8,128]{2,1,0:T(8,128)S(1)} %collective-permute-done.4.refs_4_, ...), custom_call_target="tpu_custom_call" | custom-call | flops 62914560 | bytes 1065600 | tf_op jit(solution)/shard_map/force/pallas_call | solution.py:35
  67.1 0.7 copy.8
  (1 shorter events, 0.0 us)
Async XLA Ops:
  0.6 1.0 %copy-start = (f32[32,16,128]{2,1,0:T(8,128)S(1)}, f32[32,16,128]{2,1,0:T(8,128)}, u32[]{:S(2)}) copy-start(f32[32,16,128]{2,1,0:T(8,128)} %refs_1_.3) | copy-start | bytes 786436
  1.6 0.7 copy-start.2
  3.0 3.2 %collective-permute-start = (f32[8,16,128]{2,1,0:T(8,128)S(1)}, f32[8,16,128]{2,1,0:T(8,128)S(1)}, u32[]{:S(2)}, u32[]{:S(2)}) collective-permute-start(f32[8,16,128]{2,1,0:T(8,128)S(1)} %get-tuple-element.11), channel_id=1, source_target_pairs={{0,1},{1,0},{2,3},{3,2},{4,5},{5,4},{6,7},{7,6},{8,9},{9,8},{10,11... | collective-permute-start | bytes 196616 | tf_op jit(solution)/shard_map/ppermute | solution.py:357
  3.5 5.3 %collective-permute-start.1 = (f32[8,16,128]{2,1,0:T(8,128)S(1)}, f32[8,16,128]{2,1,0:T(8,128)S(1)}, u32[]{:S(2)}, u32[]{:S(2)}) collective-permute-start(f32[8,16,128]{2,1,0:T(8,128)S(1)} %get-tuple-element.12), channel_id=1, source_target_pairs={{0,2},{1,3},{2,0},{3,1},{4,6},{5,7},{6,4},{7,5},{8,10},{9,11},{10,... | collective-permute-start | bytes 196616 | tf_op jit(solution)/shard_map/ppermute | solution.py:357
  6.1 4.0 %collective-permute-start.2 = (f32[8,16,128]{2,1,0:T(8,128)S(1)}, f32[8,16,128]{2,1,0:T(8,128)S(1)}, u32[]{:S(2)}, u32[]{:S(2)}) collective-permute-start(f32[8,16,128]{2,1,0:T(8,128)S(1)} %get-tuple-element.13), channel_id=1, source_target_pairs={{0,3},{1,2},{2,1},{3,0},{4,7},{5,6},{6,5},{7,4},{8,11},{9,10},{10,... | collective-permute-start | bytes 196616 | tf_op jit(solution)/shard_map/ppermute | solution.py:357
  10.1 4.6 %copy-start.3 = (s32[32,4]{0,1:T(4,128)S(1)}, s32[32,4]{0,1:T(4,128)}, u32[]{:S(2)}) copy-start(s32[32,4]{0,1:T(4,128)} %param.6) | copy-start | bytes 1540
  10.2 8.5 %collective-permute-start.4 = (f32[32,8,128]{2,1,0:T(8,128)S(1)}, f32[32,8,128]{2,1,0:T(8,128)S(1)}, u32[]{:S(2)}, u32[]{:S(2)}) collective-permute-start(f32[32,8,128]{2,1,0:T(8,128)S(1)} %get-tuple-element.14.refs_2_), channel_id=1, source_target_pairs={{0,28},{4,8},{8,4},{12,16},{16,12},{20,24},{24,20},{28,0},{1,29},{... | collective-permute-start | bytes 393224 | tf_op jit(solution)/shard_map/ppermute | solution.py:372
  14.8 6.6 %collective-permute-start.3 = (f32[32,8,128]{2,1,0:T(8,128)S(1)}, f32[32,8,128]{2,1,0:T(8,128)S(1)}, u32[]{:S(2)}, u32[]{:S(2)}) collective-permute-start(f32[32,8,128]{2,1,0:T(8,128)S(1)} %get-tuple-element.14.refs_2_), channel_id=1, source_target_pairs={{0,4},{4,0},{8,12},{12,8},{16,20},{20,16},{24,28},{28,24},{1,5},{5... | collective-permute-start | bytes 393224 | tf_op jit(solution)/shard_map/ppermute | solution.py:373
  14.9 6.5 %copy-start.1 = (s32[32]{0:T(128)S(1)}, s32[32]{0:T(128)}, u32[]{:S(2)}) copy-start(s32[32]{0:T(128)} %refs_1_.5) | copy-start | bytes 388
  34.8 6.5 %collective-permute-start.6 = (f32[32,128]{1,0:T(8,128)S(1)}, f32[32,128]{1,0:T(8,128)S(1)}, u32[]{:S(2)}, u32[]{:S(2)}) collective-permute-start(f32[32,128]{1,0:T(8,128)S(1)} %get-tuple-element.17.refs_7_), channel_id=1, source_target_pairs={{0,28},{4,8},{8,4},{12,16},{16,12},{20,24},{24,20},{28,0},{1,29},{... | collective-permute-start | bytes 49160 | tf_op jit(solution)/shard_map/ppermute | solution.py:372
  34.9 6.4 %collective-permute-start.5 = (f32[32,128]{1,0:T(8,128)S(1)}, f32[32,128]{1,0:T(8,128)S(1)}, u32[]{:S(2)}, u32[]{:S(2)}) collective-permute-start(f32[32,128]{1,0:T(8,128)S(1)} %get-tuple-element.17.refs_7_), channel_id=1, source_target_pairs={{0,4},{4,0},{8,12},{12,8},{16,20},{20,16},{24,28},{28,24},{1,5},{5... | collective-permute-start | bytes 49160 | tf_op jit(solution)/shard_map/ppermute | solution.py:373

commit v2 on v0

v2 whole, which is shorter than its diff:
```python
import math

import jax
import jax.numpy as jnp
from jax import lax
from jax.experimental import pallas as pl
from jax.experimental.pallas import tpu as pltpu
from jax.sharding import PartitionSpec as P

ADIABATIC = 5.0 / 3.0
TIMESTEP = 0.5
KERNEL_NORM = 21.0 / (16.0 * math.pi)
MASS_UNIT = 512.0
WEIGHT_FACTOR = 8.0 * KERNEL_NORM / MASS_UNIT
SLOPE_FACTOR = -5.0 * 32.0 * KERNEL_NORM / MASS_UNIT
CENTRE = 1.0
AWAY = 1.0e4
LANES = 128
GROUP = 16
DEPTH = 32
FIELD_ROWS = 40

F32 = jnp.float32
BF16 = jnp.bfloat16
I32 = jnp.int32


def vmem_spec():
    return pl.BlockSpec(memory_space=pltpu.VMEM)


def smem_spec():
    return pl.BlockSpec(memory_space=pltpu.SMEM)


def hbm_spec():
    return pl.BlockSpec(memory_space=pltpu.HBM)


def any_spec():
    return pl.BlockSpec(memory_space=pl.ANY)


SPECS = {"s": smem_spec, "v": vmem_spec, "h": hbm_spec, "a": any_spec}


def in_hbm(array):
    return pltpu.with_memory_space_constraint(array, pltpu.HBM)


def kernel_call(kernel, ins, outs, scratch, nanoseconds, name, aliases=None):
    return pl.pallas_call(
        kernel,
        out_shape=[jax.ShapeDtypeStruct(shape, dtype) for _, shape, dtype in outs],
        in_specs=[SPECS[memory]() for memory, _ in ins],
        out_specs=[SPECS[memory]() for memory, _, _ in outs],
        scratch_shapes=scratch,
        input_output_aliases=aliases or {},
        compiler_params=pltpu.CompilerParams(vmem_limit_bytes=32 * 1024 * 1024),
        cost_estimate=pl.CostEstimate(flops=0, bytes_accessed=3000 * nanoseconds, transcendentals=0),
        name=name,
    )(*[array for _, array in ins])


def is_power(count):
    return count & (count - 1) == 0


def partner_tile(index, step, count):
    return index ^ step if is_power(count) else (index + step) % count


def source_tile(index, step, count):
    return index ^ step if is_power(count) else lax.rem(index + count - step, count)


def rounded(value):
    return value.astype(BF16).astype(F32)


def split2(value):
    hi = rounded(value)
    return hi, rounded(value - hi)


def split3(value):
    hi = rounded(value)
    mid = rounded(value - hi)
    return hi, mid, rounded(value - hi - mid)


class Plan:
    def __init__(self, slots, width):
        self.slots, self.width = slots, width
        self.entry_bits = (width - 1).bit_length()
        self.cand_bits = (2 * slots).bit_length()
        self.length = slots * width + 2 * GROUP
        self.codes = (slots + 1) << self.entry_bits
        self.local, self.remote = 0, self.length
        self.counts = 2 * self.length
        self.size = 2 * self.length + 8
        self.stored = slots * width + 2 * GROUP

    def word(self, slot, entry, cand):
        return (((slot << self.entry_bits) + entry) << self.cand_bits) + cand

    def code(self, word):
        return word >> self.cand_bits

    def slot(self, word):
        return word >> (self.cand_bits + self.entry_bits)

    def cand(self, word):
        return word & ((1 << self.cand_bits) - 1)

    def groups(self, ref, which):
        return lax.div(ref[self.counts + which] + GROUP - 1, GROUP)

    def stored_base(self, ref, which):
        return self.groups(ref, 0) * GROUP if which else 0


def plan_kernel(plan, neighbours_ref, counts_ref, after_ref, plan_ref):
    slots = plan.slots
    upper_first = lax.rem(lax.axis_index("slab"), 2) == 0
    low_base = jnp.where(upper_first, slots, 0)
    high_base = jnp.where(upper_first, -2 * slots, -slots)

    def fill(i, totals):
        near, far = totals
        used = counts_ref[i]
        for k in range(plan.width):
            n = neighbours_ref[k, i]
            local = (n >= slots) & (n < 2 * slots)
            cand = jnp.where(n < slots, n + low_base, jnp.where(local, n - slots, n + high_base))
            word = plan.word(i, k, cand)
            plan_ref[plan.local + near] = word
            plan_ref[plan.remote + far] = word
            active = k < used
            near = near + (active & local).astype(I32)
            far = far + (active & jnp.logical_not(local)).astype(I32)
        return near, far

    near, far = lax.fori_loop(0, slots, fill, (jnp.int32(0), jnp.int32(0)))
    for k in range(GROUP):
        plan_ref[plan.local + near + k] = plan.word(slots, 0, slots)
        plan_ref[plan.remote + far + k] = plan.word(slots, 0, 2 * slots)
    plan_ref[plan.counts] = near
    plan_ref[plan.counts + 1] = far


def pack_kernel(tiles, cap, floats, dest_ref, particles_ref, *refs):
    outs, (packed, staged, dest, sems) = refs[:tiles], refs[tiles:]
    bring = [pltpu.make_async_copy(dest_ref, dest, sems.at[0]), pltpu.make_async_copy(particles_ref, staged, sems.at[1])]
    for copy in bring:
        copy.start()
    packed[...] = jnp.zeros_like(packed)
    me = lax.axis_index("tile")
    for copy in bring:
        copy.wait()

    def place(b, carry):
        target = dest[b]
        owner = lax.div(target, cap)
        step = owner ^ me if is_power(tiles) else lax.rem(owner + tiles - me, tiles)
        packed[step * cap + lax.rem(target, cap)] = staged[b]
        return carry

    lax.fori_loop(0, staged.shape[0], place, 0, unroll=4)
    for k in range(tiles):
        outs[k][...] = packed[k * cap : (k + 1) * cap].reshape(cap * floats, LANES)


def states_kernel(tiles, cap, floats, *refs):
    parts, (after_ref, own_ref, moving_ref) = refs[:tiles], refs[tiles:]
    me = lax.axis_index("tile")
    for k in range(tiles):
        base = pl.multiple_of(source_tile(me, k, tiles) * cap, cap)
        rows = pl.ds(base, cap)

        def field(f):
            return parts[k][pl.ds(f, cap, stride=floats), :]

        for f in range(8):
            own_ref[f, rows, :] = field(f)
        mass = field(6)
        present = mass > 0
        for f in range(3):
            moving_ref[f, rows, :] = field(f) - CENTRE
        moving_ref[3, rows, :] = jnp.where(present, field(8), 1.0)
        scaled = jnp.where(present, mass * MASS_UNIT, 1.0)
        root = jnp.exp(jnp.log(scaled) * (-1.0 / 3.0))
        for _ in range(2):
            root = root * (4.0 - scaled * (root * root * root)) * (1.0 / 3.0)
        moving_ref[4, rows, :] = jnp.where(present, root, 0.0)
        for f in range(3):
            moving_ref[5 + f, rows, :] = field(3 + f)


def store_far(far_ref, base, moving_ref, slots):
    def put(row, value):
        far_ref[pl.ds(base * DEPTH + row, slots, stride=DEPTH), :] = value

    place = [moving_ref[f] for f in range(3)]
    smooth, stretch = moving_ref[3], moving_ref[4]
    present = stretch > 0
    stretch = jnp.where(present, stretch, 1.0)
    square = stretch * stretch
    norm = 0.0
    for f in range(3):
        hi, mid, lo = split3(-2.0 * square * place[f])
        norm = norm + place[f] * place[f]
        put(f, hi)
        put(3 + f, hi)
        put(6 + f, hi)
        put(9 + f, mid)
        put(12 + f, lo)
    for row, value in enumerate(split3(jnp.where(present, square * norm, AWAY))):
        put(15 + row, value)
    s1, s2, s3 = split3(square)
    for row, value in enumerate((s1, s1, s1, s2, s2, s3)):
        put(18 + row, value)
    for row, value in enumerate(split3(stretch * smooth)):
        put(24 + row, value)
    u1, u2 = split2(stretch)
    for row, value in enumerate((u1, u1, u2, u2)):
        put(27 + row, value)
    put(31, jnp.zeros_like(stretch))


def store_far_dummy(far_ref, index):
    row = lax.broadcasted_iota(I32, (DEPTH, LANES), 0)
    far_ref[index * DEPTH : (index + 1) * DEPTH, :] = jnp.where(row == 15, AWAY, jnp.where(row == 24, 1.0, 0.0))


def store_near(near_ref, moving_ref, slots):
    near_ref[...] = jnp.zeros_like(near_ref)
    row = lax.broadcasted_iota(I32, (DEPTH, LANES), 0)
    start = 2 * slots * DEPTH
    near_ref[start : start + DEPTH, :] = jnp.where((row >= 15) & (row < 18), 1.0, 0.0)
    near_ref[start + DEPTH : start + 2 * DEPTH, :] = jnp.where((row >= 24) & (row < 27), 1.0, 0.0)

    def put(row, value, half=0):
        near_ref[pl.ds(half * DEPTH + row, slots, stride=2 * DEPTH), :] = value

    place = [moving_ref[f] for f in range(3)]
    norm = 0.0
    for f in range(3):
        hi, mid, lo = split3(place[f])
        norm = norm + place[f] * place[f]
        put(f, hi)
        put(3 + f, mid)
        put(6 + f, lo)
        put(9 + f, hi)
        put(12 + f, hi)
    ones = jnp.ones_like(norm)
    for row in range(3):
        put(15 + row, ones)
        put(24 + row, ones, 1)
    n1, n2, n3 = split3(norm)
    for row, value in enumerate((n1, n2, n3, n1, n2, n1)):
        put(18 + row, value)
    h1, h2 = split2(moving_ref[3])
    for row, value in enumerate((h1, h2, h1, h2)):
        put(27 + row, value, 1)


def pair_loop(plan, plan_ref, which, near_ref, far_ref, weight_ref, slope_ref):
    base = plan.remote if which else plan.local
    stored = plan.stored_base(plan_ref, which)

    def group(g, carry):
        for u in range(GROUP):
            word = plan_ref[base + g * GROUP + u]
            far = far_ref[pl.ds(pl.multiple_of(plan.cand(word) * DEPTH, DEPTH), DEPTH), :]
            near = near_ref[pl.ds(pl.multiple_of(plan.slot(word) * (2 * DEPTH), DEPTH), 2 * DEPTH), :]
            near = jnp.concatenate([near[0:DEPTH], near[DEPTH : 2 * DEPTH]], axis=1)
            both = lax.dot_general(far, near, (((0,), (0,)), ((), ())), preferred_element_type=F32)
            squared = jnp.maximum(both[:, 0:LANES], 1e-20)
            inverse = pltpu.reciprocal(both[:, LANES : 2 * LANES], approx=True)
            remain = jnp.maximum(1.0 - squared * lax.rsqrt(squared) * inverse, 0.0)
            scaled = inverse * remain
            cubed = scaled * scaled * scaled
            weight = cubed * (remain * (5.0 - 4.0 * remain))
            weight_ref[plan.code(word)] = jnp.sum(weight.reshape(LANES // 8, 8, LANES), axis=0)
            slope_ref[stored + g * GROUP + u] = cubed * (inverse * inverse)
        return carry

    lax.fori_loop(0, plan.groups(plan_ref, which), group, 0)


def local_kernel(plan, plan_ref, moving_ref, near_ref, weight_ref, slope_ref, far_ref):
    slots = plan.slots
    store_near(near_ref, moving_ref, slots)
    store_far(far_ref, 0, moving_ref, slots)
    store_far_dummy(far_ref, slots)
    weight_ref[...] = jnp.zeros_like(weight_ref)
    pair_loop(plan, plan_ref, 0, near_ref, far_ref, weight_ref, slope_ref)


def remote_kernel(plan, plan_ref, own_ref, first_ref, second_ref, near_ref, weight_ref, slope_in_ref,
                  density_ref, ratio_ref, slope_ref, far_ref, added_ref):
    slots = plan.slots
    store_far(far_ref, 0, first_ref, slots)
    store_far(far_ref, slots, second_ref, slots)
    store_far_dummy(far_ref, 2 * slots)
    added_ref[...] = jnp.zeros_like(added_ref)
    pair_loop(plan, plan_ref, 1, near_ref, far_ref, added_ref, slope_ref)
    entries = 1 << plan.entry_bits
    weight_rows = weight_ref.reshape(plan.codes * 8, LANES)
    added_rows = added_ref.reshape(plan.codes * 8, LANES)
    total = 0.0
    for row in range(8 * plan.width):
        picked = pl.ds(row, slots, stride=8 * entries)
        total = total + (weight_rows[picked, :] + added_rows[picked, :])
    density = WEIGHT_FACTOR * total
    safe = jnp.where(own_ref[6] > 0, density, 1.0)
    density_ref[...] = density
    ratio_ref[...] = (ADIABATIC - 1.0) * density * own_ref[7] / (safe * safe)


def store_fields(field_ref, base, moving_ref, ratio_ref, slots):
    def put(row, value):
        field_ref[pl.ds(base * FIELD_ROWS + row, slots, stride=FIELD_ROWS), :] = value

    stretch = moving_ref[4]
    square = stretch * stretch
    place = [moving_ref[f] for f in range(3)]
    speed = [moving_ref[5 + f] for f in range(3)]
    dotted = place[0] * speed[0] + place[1] * speed[1] + place[2] * speed[2]
    plain = [square] + [square * value for value in place + speed + [dotted]]
    heavy = [ratio_ref[...] * value for value in plain[0:4]]
    for row, value in enumerate(plain):
        for part, piece in enumerate(split3(value)):
            put(8 * part + row, piece)
    for row, value in enumerate(heavy):
        for part, piece in enumerate(split3(value)):
            put(24 + 4 * part + row, piece)
        put(36 + row, jnp.zeros_like(value))


def store_field_dummy(field_ref, index):
    field_ref[index * FIELD_ROWS : (index + 1) * FIELD_ROWS, :] = jnp.zeros((FIELD_ROWS, LANES), F32)


def field_loop(plan, plan_ref, which, field_ref, slope_ref, sum_ref):
    base = plan.remote if which else plan.local
    stored = plan.stored_base(plan_ref, which)

    def group(g, carry):
        for u in range(GROUP):
            word = plan_ref[base + g * GROUP + u]
            start = pl.multiple_of(plan.cand(word) * FIELD_ROWS, 8)
            field = field_ref[pl.ds(start, FIELD_ROWS), :].astype(BF16)
            slope = slope_ref[stored + g * GROUP + u]
            hi = slope.astype(BF16)
            lo = (slope - hi.astype(F32)).astype(BF16)
            both = jnp.dot(
                jnp.concatenate([field, field], axis=1),
                jnp.concatenate([hi, lo], axis=0),
                preferred_element_type=F32,
            )
            code = plan.code(word)
            sum_ref[code, 0:8, :] = both[0:8] + both[8:16] + both[16:24]
            sum_ref[code, 8:16, :] = both[24:32] + both[32:40]
        return carry

    lax.fori_loop(0, plan.groups(plan_ref, which), group, 0)


def local_field_kernel(plan, plan_ref, moving_ref, ratio_ref, slope_ref, sum_ref, field_ref):
    store_fields(field_ref, 0, moving_ref, ratio_ref, plan.slots)
    store_field_dummy(field_ref, plan.slots)
    sum_ref[...] = jnp.zeros_like(sum_ref)
    field_loop(plan, plan_ref, 0, field_ref, slope_ref, sum_ref)


def final_kernel(plan, tiles, cap, floats, plan_ref, own_ref, moving_ref, first_ref, second_ref, density_ref, ratio_ref,
                 first_ratio_ref, second_ratio_ref, slope_ref, local_sum_ref, *refs):
    parts, (updated_ref, derived_ref, field_ref, sum_ref) = refs[:tiles], refs[tiles:]
    slots = plan.slots
    store_fields(field_ref, 0, first_ref, first_ratio_ref, slots)
    store_fields(field_ref, slots, second_ref, second_ratio_ref, slots)
    store_field_dummy(field_ref, 2 * slots)
    sum_ref[...] = jnp.zeros_like(sum_ref)
    me = lax.axis_index("tile")
    for k in range(tiles):
        base = source_tile(me, k, tiles) * cap
        for j in range(cap):
            present = (parts[k][j * floats + 6 : j * floats + 7, :] > 0).astype(F32)
            start = pl.multiple_of((base + j) * floats + 8, 8)
            updated_ref[pl.ds(start, floats - 8), :] = parts[k][j * floats + 8 : (j + 1) * floats, :] * present
    field_loop(plan, plan_ref, 1, field_ref, slope_ref, sum_ref)
    local_rows = local_sum_ref.reshape(plan.codes * 16, LANES)
    remote_rows = sum_ref.reshape(plan.codes * 16, LANES)
    entries = 1 << plan.entry_bits

    def summed(row):
        total = 0.0
        for k in range(plan.width):
            picked = pl.ds(16 * k + row, slots, stride=16 * entries)
            total = total + (local_rows[picked, :] + remote_rows[picked, :])
        return SLOPE_FACTOR * total

    plain = [summed(row) for row in range(8)]
    heavy = [summed(8 + row) + summed(12 + row) for row in range(4)]
    place = [moving_ref[f] for f in range(3)]
    speed = [own_ref[3 + f] for f in range(3)]
    ratio, density = ratio_ref[...], density_ref[...]
    accel, heating = [], plain[7]
    for f in range(3):
        spread = place[f] * plain[0] - plain[1 + f]
        accel.append(-(ratio * spread + (place[f] * heavy[0] - heavy[1 + f])))
        heating = heating + place[f] * (speed[f] * plain[0] - plain[4 + f]) - speed[f] * plain[1 + f]
    heating = ratio * heating
    present = (own_ref[6] > 0).astype(F32)
    fresh = {}
    for f in range(3):
        fresh[3 + f] = speed[f] + TIMESTEP * accel[f]
        fresh[f] = own_ref[f] + TIMESTEP * fresh[3 + f]
    fresh[6] = own_ref[6]
    fresh[7] = own_ref[7] + TIMESTEP * heating
    for f in range(8):
        updated_ref[pl.ds(f, slots, stride=floats), :] = fresh[f] * present
    for f, value in enumerate([density] + accel + [heating]):
        derived_ref[f] = value * present


def body(tiles, slabs, particles, dest_slot, neighbours, counts):
    bins, floats, lanes = particles.shape
    slots, width = neighbours.shape
    cap = slots // tiles
    plan = Plan(slots, width)
    packed = kernel_call(
        lambda *refs: pack_kernel(tiles, cap, floats, *refs),
        [("h", in_hbm(dest_slot)), ("h", in_hbm(particles))],
        [("v", (cap * floats, lanes), F32)] * tiles,
        [
            pltpu.VMEM((slots, floats, lanes), F32),
            pltpu.VMEM((bins, floats, lanes), F32),
            pltpu.SMEM((bins,), I32),
            pltpu.SemaphoreType.DMA((2,)),
        ],
        1500,
        "pack",
    )
    parts = [packed[0]] + [
        lax.ppermute(packed[k], "tile", [(t, partner_tile(t, k, tiles)) for t in range(tiles)])
        for k in range(1, tiles)
    ]
    (lists,) = kernel_call(
        lambda *refs: plan_kernel(plan, *refs),
        [("s", in_hbm(neighbours.T)), ("s", in_hbm(counts)), ("a", packed[0])],
        [("s", (plan.size,), I32)],
        [],
        2000,
        "plan",
    )
    own, moving = kernel_call(
        lambda *refs: states_kernel(tiles, cap, floats, *refs),
        [("v", part) for part in parts] + [("a", lists)],
        [("v", (8, slots, lanes), F32)] * 2,
        [],
        200,
        "states",
    )
    first_pairs = [(s, s ^ 1) for s in range(slabs)]
    second_pairs = [(s, (((s + 1) ^ 1) - 1) % slabs) for s in range(slabs)]

    def both_sides(array):
        second = lax.ppermute(array, "slab", second_pairs)
        first = lax.ppermute(array, "slab", first_pairs)
        return first, second

    first, second = both_sides(moving)
    near, weights, slopes = kernel_call(
        lambda *refs: local_kernel(plan, *refs),
        [("s", lists), ("v", moving)],
        [
            ("v", ((slots + 1) * 2 * DEPTH, lanes), F32),
            ("v", (plan.codes, 8, lanes), F32),
            ("v", (plan.stored, lanes, lanes), F32),
        ],
        [pltpu.VMEM(((slots + 1) * DEPTH, lanes), F32)],
        3500,
        "local",
    )
    density, ratio, slopes = kernel_call(
        lambda *refs: remote_kernel(plan, *refs),
        [("s", lists), ("v", own), ("v", first), ("v", second), ("v", near), ("v", weights), ("v", slopes)],
        [("v", (slots, lanes), F32)] * 2 + [("v", (plan.stored, lanes, lanes), F32)],
        [pltpu.VMEM(((2 * slots + 1) * DEPTH, lanes), F32), pltpu.VMEM((plan.codes, 8, lanes), F32)],
        3500,
        "remote",
        {6: 2},
    )
    first_ratio, second_ratio = both_sides(ratio)
    (local_sums,) = kernel_call(
        lambda *refs: local_field_kernel(plan, *refs),
        [("s", lists), ("v", moving), ("v", ratio), ("v", slopes)],
        [("v", (plan.codes, 16, lanes), F32)],
        [pltpu.VMEM(((slots + 1) * FIELD_ROWS, lanes), F32)],
        2500,
        "fields",
    )
    updated, derived = kernel_call(
        lambda *refs: final_kernel(plan, tiles, cap, floats, *refs),
        [("s", lists), ("v", own), ("v", moving), ("v", first), ("v", second), ("v", density), ("v", ratio),
         ("v", first_ratio), ("v", second_ratio), ("v", slopes), ("v", local_sums)]
        + [("v", part) for part in parts],
        [("v", (slots * floats, lanes), F32), ("v", (5, slots, lanes), F32)],
        [pltpu.VMEM(((2 * slots + 1) * FIELD_ROWS, lanes), F32), pltpu.VMEM((plan.codes, 16, lanes), F32)],
        3000,
        "final",
    )
    return updated.reshape(slots, floats, lanes), derived.transpose(1, 0, 2)


def solution(mesh):
    tiles, slabs = mesh.shape["tile"], mesh.shape["slab"]
    in_specs = (
        P(("slab", "tile"), None, None),
        P(("slab", "tile")),
        P(("slab", "tile"), None),
        P(("slab", "tile")),
    )
    out_specs = (P(("slab", "tile"), None, None), P(("slab", "tile"), None, None))
    return jax.shard_map(
        lambda *args: body(tiles, slabs, *args), mesh=mesh, in_specs=in_specs, out_specs=out_specs, check_vma=False
    )
```

time: 75.8 us -> 35.3 us (0.47)
  other arithmetic: 40.6 us -> 0 us
  Pallas kernels: 0 us -> 18.8 us
  local copies, waits for them, and re-layouts: 6.13 us -> 0 us
  waiting for transfers between devices: 12 us -> 6.72 us
  starting transfers between devices: 14.2 us -> 8.99 us
  matrix products: 1.01 us -> 0 us
  loops' own time: 0.76 us -> 0 us
    reduce_sum x20 -> x0, other arithmetic: 27.2 us -> none  [the longest x4 9.27 us: slot_force(): accel = -jnp.sum(pairing[:, None] * offset, axis=(0, 3))]
    pallas_call x0 -> x7, Pallas kernels: none -> 18.8 us  [kernel_call(): pl.pallas_call(kernel, out_shape=[jax.ShapeDtypeStruct(shape, dtype) for...]
    mul x15 -> x0, other arithmetic: 9.68 us -> none  [the longest x4 8.53 us: slot_force(): pairing = factor * (self_ratio[None, :, None] + picked[:, 8][:, None, :])]
    all_to_all x1 -> x0, starting transfers between devices: 4.24 us -> none  [body(): lax.all_to_all(packed, 'tile', split_axis=0, concat_axis=0, tiled=True)]
    all_to_all x1 -> x0, waiting for transfers between devices: 3.62 us -> none  [body(): lax.all_to_all(packed, 'tile', split_axis=0, concat_axis=0, tiled=True)]
    ppermute x4 -> x7, waiting for transfers between devices: 8.41 us -> 6.72 us  [the longest x2 3.36 us: both_sides(): second = lax.ppermute(array, 'slab', second_pairs)]
    unnamed x3 -> x0, local copies, waits for them, and re-layouts: 1.6 us -> none
    gather x2 -> x0, local copies, waits for them, and re-layouts: 1.52 us -> none  [the longest x1 0.76 us: body(): dense_pick = jnp.take(gathered, neighbours, axis=0)]
  transfers between devices with their start and end apart: 5 -> 7, of which waited for: 5 -> 4; matrix products, arithmetic and copies ran while one was open for 3% -> 0% of each run, Pallas kernels for 0% -> 26%
where the time goes in v2:
time: 35.3 us; the launch traced here: 35.2 us
  Pallas kernels  18.8 us (53%)
  starting transfers between devices  8.99 us (25%)
  waiting for transfers between devices  6.72 us (19%)
  between operations  0.69 us (2%)
    pallas_call x7, Pallas kernels, kernel_call(): pl.pallas_call(kernel, out_shape=[jax.ShapeDtypeStruct(shape, dtype) for...  18.8 us
    ppermute x2, starting transfers between devices, both_sides(): second = lax.ppermute(array, 'slab', second_pairs)  5.62 us
    ppermute x2, waiting for transfers between devices, both_sides(): second = lax.ppermute(array, 'slab', second_pairs)  3.36 us
    ppermute x3, starting transfers between devices, body(): lax.ppermute(packed[k], 'tile', [(t, partner_tile(t, k, tiles)) for t in...  3.18 us
    ppermute x2, waiting for transfers between devices, both_sides(): first = lax.ppermute(array, 'slab', first_pairs)  1.81 us
    ppermute x3, waiting for transfers between devices, body(): lax.ppermute(packed[k], 'tile', [(t, partner_tile(t, k, tiles)) for t in...  1.55 us
  transfers between devices with their start and end apart: 7, of which 4 were waited for; matrix products, arithmetic and copies ran while one was open for 0% of the time, Pallas kernels for 26%

profile of v2, /device:TPU:0, one launch (start us, length us, event | category | flops | bytes accessed | tf_op | source)
XLA Modules:
  0.0 35.2 jit_solution(3940861467886242641)
XLA Ops:
  0.6 1.1 %pack.1 = (f32[128,128]{1,0:T(8,128)S(1)}, f32[128,128]{1,0:T(8,128)S(1)}, f32[128,128]{1,0:T(8,128)S(1)}, f32[128,128]{1,0:T(8,128)S(1)}) custom-call(s32[32]{0:T(128)} %refs_0_.1, f32[32,16,128]{2,1,0:T(8,128)} %refs_1_.2), custom_call_target="tpu_custom_call" | custom-call | bytes 4500000 | tf_op jit(solution)/shard_map/pack/pallas_call | solution.py:52
  1.7 0.5 %collective-permute-start = (f32[128,128]{1,0:T(8,128)S(1)}, f32[128,128]{1,0:T(8,128)S(1)}, u32[]{:S(2)}, u32[]{:S(2)}) collective-permute-start(f32[128,128]{1,0:T(8,128)S(1)} %get-tuple-element.17), channel_id=1, source_target_pairs={{0,1},{1,0},{2,3},{3,2},{4,5},{5,4},{6,7},{7,6},{8,9},{9,8},{10,11... | collective-permute-start | bytes 196616 | tf_op jit(solution)/shard_map/ppermute | solution.py:448
  2.3 2.6 %collective-permute-start.1 = (f32[128,128]{1,0:T(8,128)S(1)}, f32[128,128]{1,0:T(8,128)S(1)}, u32[]{:S(2)}, u32[]{:S(2)}) collective-permute-start(f32[128,128]{1,0:T(8,128)S(1)} %get-tuple-element.18), channel_id=1, source_target_pairs={{0,2},{1,3},{2,0},{3,1},{4,6},{5,7},{6,4},{7,5},{8,10},{9,11},{10,... | collective-permute-start | bytes 196616 | tf_op jit(solution)/shard_map/ppermute | solution.py:448
  4.9 0.1 collective-permute-start.2
  4.9 2.4 %plan.1.refs_4_.refs_0_ = s32[328]{0:T(512)S(1)} custom-call(s32[4,32]{1,0:T(4,128)} %bitcast.3, s32[32]{0:T(128)} %refs_1_.3, f32[128,128]{1,0:T(8,128)S(1)} %get-tuple-element.16.refs_2_.refs_0_.refs_11_), custom_call_target="tpu_custom_call" | custom-call | bytes 6000000 | tf_op jit(solution)/shard_map/plan/pallas_call | solution.py:52
  7.3 0.0 collective-permute-done.refs_1_.refs_12_
  7.4 0.2 collective-permute-done.1.refs_2_.refs_13_
  7.5 1.4 %collective-permute-done.2.refs_3_.refs_14_ = f32[128,128]{1,0:T(8,128)S(1)} collective-permute-done((f32[128,128]{1,0:T(8,128)S(1)}, f32[128,128]{1,0:T(8,128)S(1)}, u32[]{:S(2)}, u32[]{:S(2)}) %collective-permute-start.2) | collective-permute-done | bytes 65568 | tf_op jit(solution)/shard_map/ppermute | solution.py:448
  8.9 0.1 states.1
  9.0 4.6 %collective-permute-start.4 = (f32[8,32,128]{2,1,0:T(8,128)S(1)}, f32[8,32,128]{2,1,0:T(8,128)S(1)}, u32[]{:S(2)}, u32[]{:S(2)}) collective-permute-start(f32[8,32,128]{2,1,0:T(8,128)S(1)} %get-tuple-element.21.refs_1_.refs_2_), channel_id=1, source_target_pairs={{0,28},{4,8},{8,4},{12,16},{16,12},{20,24},{24,20},{28,0},{1,29},{... | collective-permute-start | bytes 393224 | tf_op jit(solution)/shard_map/ppermute | solution.py:471
  13.6 0.0 collective-permute-start.3
  13.6 4.8 %local.1 = (f32[2112,128]{1,0:T(8,128)S(1)}, f32[132,8,128]{2,1,0:T(8,128)S(1)}, f32[160,128,128]{2,1,0:T(8,128)S(1)}) custom-call(s32[328]{0:T(512)S(1)} %plan.1.refs_4_.refs_0_, f32[8,32,128]{2,1,0:T(8,128)S(1)} %get-tuple-element.21.refs_1_.refs_2_), custom_call_target="tpu_custom_call" | custom-call | bytes 10500000 | tf_op jit(solution)/shard_map/local/pallas_call | solution.py:52
  18.4 0.0 collective-permute-done.4.refs_3_.refs_4_
  18.4 1.8 %collective-permute-done.3.refs_2_.refs_3_ = f32[8,32,128]{2,1,0:T(8,128)S(1)} collective-permute-done((f32[8,32,128]{2,1,0:T(8,128)S(1)}, f32[8,32,128]{2,1,0:T(8,128)S(1)}, u32[]{:S(2)}, u32[]{:S(2)}) %collective-permute-start.3) | collective-permute-done | bytes 131104 | tf_op jit(solution)/shard_map/ppermute | solution.py:472
  20.2 4.5 %remote.1 = (f32[32,128]{1,0:T(8,128)S(1)}, f32[32,128]{1,0:T(8,128)S(1)}, f32[160,128,128]{2,1,0:T(8,128)S(1)}) custom-call(s32[328]{0:T(512)S(1)} %plan.1.refs_4_.refs_0_, f32[8,32,128]{2,1,0:T(8,128)S(1)} %get-tuple-element.20.refs_1_, f32[8,32,128]{2,1,0:T(8,128)S(1)} %collective-permute-done.3.refs_2_.refs_3_, ...), custom_call_target="tpu_custom_call", output_to_operand_aliasing={{2}: (6, {})} | custom-call | bytes 10500000 | tf_op jit(solution)/shard_map/remote/pallas_call | solution.py:52
  24.7 1.0 %collective-permute-start.6 = (f32[32,128]{1,0:T(8,128)S(1)}, f32[32,128]{1,0:T(8,128)S(1)}, u32[]{:S(2)}, u32[]{:S(2)}) collective-permute-start(f32[32,128]{1,0:T(8,128)S(1)} %get-tuple-element.26.refs_2_.refs_6_), channel_id=1, source_target_pairs={{0,28},{4,8},{8,4},{12,16},{16,12},{20,24},{24,20},{28,0},{1,29},{... | collective-permute-start | bytes 49160 | tf_op jit(solution)/shard_map/ppermute | solution.py:471
  25.7 0.2 collective-permute-start.5
  25.9 1.9 %fields.1.refs_10_ = f32[132,16,128]{2,1,0:T(8,128)S(1)} custom-call(s32[328]{0:T(512)S(1)} %plan.1.refs_4_.refs_0_, f32[8,32,128]{2,1,0:T(8,128)S(1)} %get-tuple-element.21.refs_1_.refs_2_, f32[32,128]{1,0:T(8,128)S(1)} %get-tuple-element.26.refs_2_.refs_6_, f32[160,128,128]{2,1,0:T(8,128)S(1)} %get-tuple-element.27.refs_3_.refs_9_), custom_call_target="tpu_custom_call" | custom-call | bytes 7500000 | tf_op jit(solution)/shard_map/fields/pallas_call | solution.py:52
  27.8 3.4 %collective-permute-done.6.refs_8_ = f32[32,128]{1,0:T(8,128)S(1)} collective-permute-done((f32[32,128]{1,0:T(8,128)S(1)}, f32[32,128]{1,0:T(8,128)S(1)}, u32[]{:S(2)}, u32[]{:S(2)}) %collective-permute-start.6) | collective-permute-done | bytes 16416 | tf_op jit(solution)/shard_map/ppermute | solution.py:471
  31.2 0.0 collective-permute-done.5.refs_7_
  31.2 4.0 %final.1 = (f32[512,128]{1,0:T(8,128)}, f32[5,32,128]{2,1,0:T(8,128)}) custom-call(s32[328]{0:T(512)S(1)} %plan.1.refs_4_.refs_0_, f32[8,32,128]{2,1,0:T(8,128)S(1)} %get-tuple-element.20.refs_1_, f32[8,32,128]{2,1,0:T(8,128)S(1)} %get-tuple-element.21.refs_1_.refs_2_, f32[8,32,128]{2,1,0:T(8,128)S(1)} %collective-permute-done.3.refs_2_.refs_3_, ...), custom_call_target="tpu_custom_call" | custom-call | bytes 9000000 | tf_op jit(solution)/shard_map/final/pallas_call | solution.py:52
Async XLA Ops:
  1.7 5.6 %collective-permute-start = (f32[128,128]{1,0:T(8,128)S(1)}, f32[128,128]{1,0:T(8,128)S(1)}, u32[]{:S(2)}, u32[]{:S(2)}) collective-permute-start(f32[128,128]{1,0:T(8,128)S(1)} %get-tuple-element.17), channel_id=1, source_target_pairs={{0,1},{1,0},{2,3},{3,2},{4,5},{5,4},{6,7},{7,6},{8,9},{9,8},{10,11... | collective-permute-start | bytes 196616 | tf_op jit(solution)/shard_map/ppermute | solution.py:448
  2.3 5.3 %collective-permute-start.1 = (f32[128,128]{1,0:T(8,128)S(1)}, f32[128,128]{1,0:T(8,128)S(1)}, u32[]{:S(2)}, u32[]{:S(2)}) collective-permute-start(f32[128,128]{1,0:T(8,128)S(1)} %get-tuple-element.18), channel_id=1, source_target_pairs={{0,2},{1,3},{2,0},{3,1},{4,6},{5,7},{6,4},{7,5},{8,10},{9,11},{10,... | collective-permute-start | bytes 196616 | tf_op jit(solution)/shard_map/ppermute | solution.py:448
  4.9 4.0 %collective-permute-start.2 = (f32[128,128]{1,0:T(8,128)S(1)}, f32[128,128]{1,0:T(8,128)S(1)}, u32[]{:S(2)}, u32[]{:S(2)}) collective-permute-start(f32[128,128]{1,0:T(8,128)S(1)} %get-tuple-element.19), channel_id=1, source_target_pairs={{0,3},{1,2},{2,1},{3,0},{4,7},{5,6},{6,5},{7,4},{8,11},{9,10},{10,... | collective-permute-start | bytes 196616 | tf_op jit(solution)/shard_map/ppermute | solution.py:448
  9.0 9.4 %collective-permute-start.4 = (f32[8,32,128]{2,1,0:T(8,128)S(1)}, f32[8,32,128]{2,1,0:T(8,128)S(1)}, u32[]{:S(2)}, u32[]{:S(2)}) collective-permute-start(f32[8,32,128]{2,1,0:T(8,128)S(1)} %get-tuple-element.21.refs_1_.refs_2_), channel_id=1, source_target_pairs={{0,28},{4,8},{8,4},{12,16},{16,12},{20,24},{24,20},{28,0},{1,29},{... | collective-permute-start | bytes 393224 | tf_op jit(solution)/shard_map/ppermute | solution.py:471
  13.6 6.6 %collective-permute-start.3 = (f32[8,32,128]{2,1,0:T(8,128)S(1)}, f32[8,32,128]{2,1,0:T(8,128)S(1)}, u32[]{:S(2)}, u32[]{:S(2)}) collective-permute-start(f32[8,32,128]{2,1,0:T(8,128)S(1)} %get-tuple-element.21.refs_1_.refs_2_), channel_id=1, source_target_pairs={{0,4},{4,0},{8,12},{12,8},{16,20},{20,16},{24,28},{28,24},{1,5},{5... | collective-permute-start | bytes 393224 | tf_op jit(solution)/shard_map/ppermute | solution.py:472
  24.7 6.5 %collective-permute-start.6 = (f32[32,128]{1,0:T(8,128)S(1)}, f32[32,128]{1,0:T(8,128)S(1)}, u32[]{:S(2)}, u32[]{:S(2)}) collective-permute-start(f32[32,128]{1,0:T(8,128)S(1)} %get-tuple-element.26.refs_2_.refs_6_), channel_id=1, source_target_pairs={{0,28},{4,8},{8,4},{12,16},{16,12},{20,24},{24,20},{28,0},{1,29},{... | collective-permute-start | bytes 49160 | tf_op jit(solution)/shard_map/ppermute | solution.py:471
  25.7 5.5 %collective-permute-start.5 = (f32[32,128]{1,0:T(8,128)S(1)}, f32[32,128]{1,0:T(8,128)S(1)}, u32[]{:S(2)}, u32[]{:S(2)}) collective-permute-start(f32[32,128]{1,0:T(8,128)S(1)} %get-tuple-element.26.refs_2_.refs_6_), channel_id=1, source_target_pairs={{0,4},{4,0},{8,12},{12,8},{16,20},{20,16},{24,28},{28,24},{1,5},{5... | collective-permute-start | bytes 49160 | tf_op jit(solution)/shard_map/ppermute | solution.py:472

commit v3 on v2

--- a/solution.py
+++ b/solution.py
@@ -11,12 +11,12 @@
 TIMESTEP = 0.5
 KERNEL_NORM = 21.0 / (16.0 * math.pi)
 MASS_UNIT = 512.0
-WEIGHT_FACTOR = 8.0 * KERNEL_NORM / MASS_UNIT
-SLOPE_FACTOR = -5.0 * 32.0 * KERNEL_NORM / MASS_UNIT
+WEIGHT_FACTOR = 8.0 * KERNEL_NORM / MASS_UNIT / 4.0**7
+SLOPE_FACTOR = -5.0 * 32.0 * KERNEL_NORM / MASS_UNIT / 4.0**8
 CENTRE = 1.0
 AWAY = 1.0e4
 LANES = 128
-GROUP = 16
+GROUPS = (24, 16, 8)
 DEPTH = 32
 FIELD_ROWS = 40
 
@@ -89,17 +89,23 @@
     return hi, mid, rounded(value - hi - mid)
 
 
+def sum_rows(tile):
+    tile = tile + pltpu.roll(tile, 4, 0)
+    tile = tile + pltpu.roll(tile, 2, 0)
+    return tile + pltpu.roll(tile, 1, 0)
+
+
 class Plan:
     def __init__(self, slots, width):
         self.slots, self.width = slots, width
         self.entry_bits = (width - 1).bit_length()
-        self.cand_bits = (2 * slots).bit_length()
-        self.length = slots * width + 2 * GROUP
+        self.cand_bits = slots.bit_length()
+        self.length = slots * width + GROUPS[0]
         self.codes = (slots + 1) << self.entry_bits
-        self.local, self.remote = 0, self.length
-        self.counts = 2 * self.length
-        self.size = 2 * self.length + 8
-        self.stored = slots * width + 2 * GROUP
+        self.counts = 3 * self.length
+        self.size = 3 * self.length + 8
+        self.stored = slots * width + 3 * GROUPS[-1]
+        self.dummy = self.word(slots, 0, slots)
 
     def word(self, slot, entry, cand):
         return (((slot << self.entry_bits) + entry) << self.cand_bits) + cand
@@ -113,40 +119,60 @@
     def cand(self, word):
         return word & ((1 << self.cand_bits) - 1)
 
-    def groups(self, ref, which):
-        return lax.div(ref[self.counts + which] + GROUP - 1, GROUP)
-
     def stored_base(self, ref, which):
-        return self.groups(ref, 0) * GROUP if which else 0
+        step = GROUPS[-1]
+        base = 0
+        for k in range(which):
+            base = base + lax.div(ref[self.counts + k] + step - 1, step) * step
+        return base
+
+
+def in_groups(plan, plan_ref, which, work):
+    count = plan_ref[plan.counts + which]
+    large, medium, small = GROUPS
+    full = lax.div(count + large - 1 - medium, large)
+
+    def step(g, carry):
+        work(g * large, large)
+        return carry
+
+    lax.fori_loop(0, full, step, 0)
+    rest = count - full * large
+
+    @pl.when(rest > small)
+    def _():
+        work(full * large, medium)
+
+    @pl.when((rest > 0) & (rest <= small))
+    def _():
+        work(full * large, small)
 
 
 def plan_kernel(plan, neighbours_ref, counts_ref, after_ref, plan_ref):
     slots = plan.slots
     upper_first = lax.rem(lax.axis_index("slab"), 2) == 0
-    low_base = jnp.where(upper_first, slots, 0)
-    high_base = jnp.where(upper_first, -2 * slots, -slots)
+    low = jnp.where(upper_first, 2, 1)
+    high = 3 - low
 
     def fill(i, totals):
-        near, far = totals
         used = counts_ref[i]
         for k in range(plan.width):
             n = neighbours_ref[k, i]
-            local = (n >= slots) & (n < 2 * slots)
-            cand = jnp.where(n < slots, n + low_base, jnp.where(local, n - slots, n + high_base))
-            word = plan.word(i, k, cand)
-            plan_ref[plan.local + near] = word
-            plan_ref[plan.remote + far] = word
-            active = k < used
-            near = near + (active & local).astype(I32)
-            far = far + (active & jnp.logical_not(local)).astype(I32)
-        return near, far
-
-    near, far = lax.fori_loop(0, slots, fill, (jnp.int32(0), jnp.int32(0)))
-    for k in range(GROUP):
-        plan_ref[plan.local + near + k] = plan.word(slots, 0, slots)
-        plan_ref[plan.remote + far + k] = plan.word(slots, 0, 2 * slots)
-    plan_ref[plan.counts] = near
-    plan_ref[plan.counts + 1] = far
+            region = lax.div(n, slots)
+            which = jnp.where(region == 1, 0, jnp.where(region == 0, low, high))
+            word = plan.word(i, k, n - region * slots)
+            kept = []
+            for w in range(3):
+                plan_ref[w * plan.length + totals[w]] = word
+                kept.append(totals[w] + ((k < used) & (which == w)).astype(I32))
+            totals = tuple(kept)
+        return totals
+
+    totals = lax.fori_loop(0, slots, fill, (jnp.int32(0),) * 3)
+    for w in range(3):
+        for k in range(GROUPS[0]):
+            plan_ref[w * plan.length + totals[w] + k] = plan.dummy
+        plan_ref[plan.counts + w] = totals[w]
 
 
 def pack_kernel(tiles, cap, floats, dest_ref, particles_ref, *refs):
@@ -193,8 +219,6 @@
         for _ in range(2):
             root = root * (4.0 - scaled * (root * root * root)) * (1.0 / 3.0)
         moving_ref[4, rows, :] = jnp.where(present, root, 0.0)
-        for f in range(3):
-            moving_ref[5 + f, rows, :] = field(3 + f)
 
 
 def store_far(far_ref, base, moving_ref, slots):
@@ -220,9 +244,9 @@
     s1, s2, s3 = split3(square)
     for row, value in enumerate((s1, s1, s1, s2, s2, s3)):
         put(18 + row, value)
-    for row, value in enumerate(split3(stretch * smooth)):
+    for row, value in enumerate(split3(0.25 * stretch * smooth)):
         put(24 + row, value)
-    u1, u2 = split2(stretch)
+    u1, u2 = split2(0.25 * stretch)
     for row, value in enumerate((u1, u1, u2, u2)):
         put(27 + row, value)
     put(31, jnp.zeros_like(stretch))
@@ -266,27 +290,28 @@
 
 
 def pair_loop(plan, plan_ref, which, near_ref, far_ref, weight_ref, slope_ref):
-    base = plan.remote if which else plan.local
+    base = which * plan.length
     stored = plan.stored_base(plan_ref, which)
 
-    def group(g, carry):
-        for u in range(GROUP):
-            word = plan_ref[base + g * GROUP + u]
+    def work(start, size):
+        for u in range(size):
+            word = plan_ref[base + start + u]
             far = far_ref[pl.ds(pl.multiple_of(plan.cand(word) * DEPTH, DEPTH), DEPTH), :]
             near = near_ref[pl.ds(pl.multiple_of(plan.slot(word) * (2 * DEPTH), DEPTH), 2 * DEPTH), :]
             near = jnp.concatenate([near[0:DEPTH], near[DEPTH : 2 * DEPTH]], axis=1)
-            both = lax.dot_general(far, near, (((0,), (0,)), ((), ())), preferred_element_type=F32)
+            both = lax.dot_general(
+                far.astype(BF16), near.astype(BF16), (((0,), (0,)), ((), ())), preferred_element_type=F32
+            )
             squared = jnp.maximum(both[:, 0:LANES], 1e-20)
             inverse = pltpu.reciprocal(both[:, LANES : 2 * LANES], approx=True)
-            remain = jnp.maximum(1.0 - squared * lax.rsqrt(squared) * inverse, 0.0)
+            remain = jnp.maximum(4.0 - squared * lax.rsqrt(squared) * inverse, 0.0)
             scaled = inverse * remain
             cubed = scaled * scaled * scaled
-            weight = cubed * (remain * (5.0 - 4.0 * remain))
+            weight = cubed * (remain * (5.0 - remain))
             weight_ref[plan.code(word)] = jnp.sum(weight.reshape(LANES // 8, 8, LANES), axis=0)
-            slope_ref[stored + g * GROUP + u] = cubed * (inverse * inverse)
-        return carry
-
-    lax.fori_loop(0, plan.groups(plan_ref, which), group, 0)
+            slope_ref[stored + start + u] = cubed * (inverse * inverse)
+
+    in_groups(plan, plan_ref, which, work)
 
 
 def local_kernel(plan, plan_ref, moving_ref, near_ref, weight_ref, slope_ref, far_ref):
@@ -298,38 +323,42 @@
     pair_loop(plan, plan_ref, 0, near_ref, far_ref, weight_ref, slope_ref)
 
 
-def remote_kernel(plan, plan_ref, own_ref, first_ref, second_ref, near_ref, weight_ref, slope_in_ref,
-                  density_ref, ratio_ref, slope_ref, far_ref, added_ref):
-    slots = plan.slots
-    store_far(far_ref, 0, first_ref, slots)
-    store_far(far_ref, slots, second_ref, slots)
-    store_far_dummy(far_ref, 2 * slots)
-    added_ref[...] = jnp.zeros_like(added_ref)
-    pair_loop(plan, plan_ref, 1, near_ref, far_ref, added_ref, slope_ref)
-    entries = 1 << plan.entry_bits
-    weight_rows = weight_ref.reshape(plan.codes * 8, LANES)
-    added_rows = added_ref.reshape(plan.codes * 8, LANES)
-    total = 0.0
-    for row in range(8 * plan.width):
-        picked = pl.ds(row, slots, stride=8 * entries)
-        total = total + (weight_rows[picked, :] + added_rows[picked, :])
-    density = WEIGHT_FACTOR * total
+def first_kernel(plan, plan_ref, moving_ref, near_ref, weight_in_ref, slope_in_ref, weight_ref, slope_ref, far_ref):
+    store_far(far_ref, 0, moving_ref, plan.slots)
+    store_far_dummy(far_ref, plan.slots)
+    pair_loop(plan, plan_ref, 1, near_ref, far_ref, weight_ref, slope_ref)
+
+
+def second_kernel(plan, plan_ref, own_ref, moving_ref, near_ref, weight_in_ref, slope_in_ref,
+                  density_ref, thermal_ref, weight_ref, slope_ref, far_ref):
+    store_far(far_ref, 0, moving_ref, plan.slots)
+    store_far_dummy(far_ref, plan.slots)
+    pair_loop(plan, plan_ref, 2, near_ref, far_ref, weight_ref, slope_ref)
+    for i in range(plan.slots):
+        first = i << plan.entry_bits
+        tile = weight_ref[first]
+        for k in range(1, plan.width):
+            tile = tile + weight_ref[first + k]
+        density_ref[i : i + 1, :] = sum_rows(tile)[0:1, :]
+    density = WEIGHT_FACTOR * density_ref[...]
+    density_ref[...] = density
     safe = jnp.where(own_ref[6] > 0, density, 1.0)
-    density_ref[...] = density
-    ratio_ref[...] = (ADIABATIC - 1.0) * density * own_ref[7] / (safe * safe)
-
-
-def store_fields(field_ref, base, moving_ref, ratio_ref, slots):
+    thermal_ref[0] = (ADIABATIC - 1.0) * density * own_ref[7] / (safe * safe)
+    for f in range(3):
+        thermal_ref[1 + f] = own_ref[3 + f]
+
+
+def store_fields(field_ref, base, moving_ref, thermal_ref, slots):
     def put(row, value):
         field_ref[pl.ds(base * FIELD_ROWS + row, slots, stride=FIELD_ROWS), :] = value
 
     stretch = moving_ref[4]
     square = stretch * stretch
     place = [moving_ref[f] for f in range(3)]
-    speed = [moving_ref[5 + f] for f in range(3)]
+    speed = [thermal_ref[1 + f] for f in range(3)]
     dotted = place[0] * speed[0] + place[1] * speed[1] + place[2] * speed[2]
     plain = [square] + [square * value for value in place + speed + [dotted]]
-    heavy = [ratio_ref[...] * value for value in plain[0:4]]
+    heavy = [thermal_ref[0] * value for value in plain[0:4]]
     for row, value in enumerate(plain):
         for part, piece in enumerate(split3(value)):
             put(8 * part + row, piece)
@@ -344,15 +373,14 @@
 
 
 def field_loop(plan, plan_ref, which, field_ref, slope_ref, sum_ref):
-    base = plan.remote if which else plan.local
+    base = which * plan.length
     stored = plan.stored_base(plan_ref, which)
 
-    def group(g, carry):
-        for u in range(GROUP):
-            word = plan_ref[base + g * GROUP + u]
-            start = pl.multiple_of(plan.cand(word) * FIELD_ROWS, 8)
-            field = field_ref[pl.ds(start, FIELD_ROWS), :].astype(BF16)
-            slope = slope_ref[stored + g * GROUP + u]
+    def work(start, size):
+        for u in range(size):
+            word = plan_ref[base + start + u]
+            field = field_ref[pl.ds(pl.multiple_of(plan.cand(word) * FIELD_ROWS, 8), FIELD_ROWS), :].astype(BF16)
+            slope = slope_ref[stored + start + u]
             hi = slope.astype(BF16)
             lo = (slope - hi.astype(F32)).astype(BF16)
             both = jnp.dot(
@@ -363,26 +391,29 @@
             code = plan.code(word)
             sum_ref[code, 0:8, :] = both[0:8] + both[8:16] + both[16:24]
             sum_ref[code, 8:16, :] = both[24:32] + both[32:40]
-        return carry
-
-    lax.fori_loop(0, plan.groups(plan_ref, which), group, 0)
-
-
-def local_field_kernel(plan, plan_ref, moving_ref, ratio_ref, slope_ref, sum_ref, field_ref):
-    store_fields(field_ref, 0, moving_ref, ratio_ref, plan.slots)
+
+    in_groups(plan, plan_ref, which, work)
+
+
+def local_field_kernel(plan, plan_ref, moving_ref, thermal_ref, slope_ref, sum_ref, field_ref):
+    store_fields(field_ref, 0, moving_ref, thermal_ref, plan.slots)
     store_field_dummy(field_ref, plan.slots)
     sum_ref[...] = jnp.zeros_like(sum_ref)
     field_loop(plan, plan_ref, 0, field_ref, slope_ref, sum_ref)
 
 
-def final_kernel(plan, tiles, cap, floats, plan_ref, own_ref, moving_ref, first_ref, second_ref, density_ref, ratio_ref,
-                 first_ratio_ref, second_ratio_ref, slope_ref, local_sum_ref, *refs):
-    parts, (updated_ref, derived_ref, field_ref, sum_ref) = refs[:tiles], refs[tiles:]
+def first_field_kernel(plan, plan_ref, moving_ref, thermal_ref, slope_ref, sum_in_ref, sum_ref, field_ref):
+    store_fields(field_ref, 0, moving_ref, thermal_ref, plan.slots)
+    store_field_dummy(field_ref, plan.slots)
+    field_loop(plan, plan_ref, 1, field_ref, slope_ref, sum_ref)
+
+
+def final_kernel(plan, tiles, cap, floats, plan_ref, own_ref, moving_ref, second_ref, density_ref, thermal_ref,
+                 second_thermal_ref, slope_ref, sum_in_ref, *refs):
+    parts, (updated_ref, derived_ref, sum_ref, field_ref, total_ref) = refs[:tiles], refs[tiles:]
     slots = plan.slots
-    store_fields(field_ref, 0, first_ref, first_ratio_ref, slots)
-    store_fields(field_ref, slots, second_ref, second_ratio_ref, slots)
-    store_field_dummy(field_ref, 2 * slots)
-    sum_ref[...] = jnp.zeros_like(sum_ref)
+    store_fields(field_ref, 0, second_ref, second_thermal_ref, slots)
+    store_field_dummy(field_ref, slots)
     me = lax.axis_index("tile")
     for k in range(tiles):
         base = source_tile(me, k, tiles) * cap
@@ -390,23 +421,22 @@
             present = (parts[k][j * floats + 6 : j * floats + 7, :] > 0).astype(F32)
             start = pl.multiple_of((base + j) * floats + 8, 8)
             updated_ref[pl.ds(start, floats - 8), :] = parts[k][j * floats + 8 : (j + 1) * floats, :] * present
-    field_loop(plan, plan_ref, 1, field_ref, slope_ref, sum_ref)
-    local_rows = local_sum_ref.reshape(plan.codes * 16, LANES)
-    remote_rows = sum_ref.reshape(plan.codes * 16, LANES)
-    entries = 1 << plan.entry_bits
+    field_loop(plan, plan_ref, 2, field_ref, slope_ref, sum_ref)
+    for i in range(slots):
+        first = i << plan.entry_bits
+        tile = sum_ref[first]
+        for k in range(1, plan.width):
+            tile = tile + sum_ref[first + k]
+        total_ref[16 * i : 16 * (i + 1), :] = tile
 
     def summed(row):
-        total = 0.0
-        for k in range(plan.width):
-            picked = pl.ds(16 * k + row, slots, stride=16 * entries)
-            total = total + (local_rows[picked, :] + remote_rows[picked, :])
-        return SLOPE_FACTOR * total
+        return SLOPE_FACTOR * total_ref[pl.ds(row, slots, stride=16), :]
 
     plain = [summed(row) for row in range(8)]
     heavy = [summed(8 + row) + summed(12 + row) for row in range(4)]
     place = [moving_ref[f] for f in range(3)]
     speed = [own_ref[3 + f] for f in range(3)]
-    ratio, density = ratio_ref[...], density_ref[...]
+    ratio, density = thermal_ref[0], density_ref[...]
     accel, heating = [], plain[7]
     for f in range(3):
         spread = place[f] * plain[0] - plain[1 + f]
@@ -459,7 +489,7 @@
     own, moving = kernel_call(
         lambda *refs: states_kernel(tiles, cap, floats, *refs),
         [("v", part) for part in parts] + [("a", lists)],
-        [("v", (8, slots, lanes), F32)] * 2,
+        [("v", (8, slots, lanes), F32), ("v", (5, slots, lanes), F32)],
         [],
         200,
         "states",
@@ -473,45 +503,65 @@
         return first, second
 
     first, second = both_sides(moving)
+    weight_out = ("v", (plan.codes, 8, lanes), F32)
+    slope_out = ("v", (plan.stored, lanes, lanes), F32)
+    sum_out = ("v", (plan.codes, 16, lanes), F32)
+    far_table = [pltpu.VMEM(((slots + 1) * DEPTH, lanes), F32)]
+    field_table = [pltpu.VMEM(((slots + 1) * FIELD_ROWS, lanes), F32)]
     near, weights, slopes = kernel_call(
         lambda *refs: local_kernel(plan, *refs),
         [("s", lists), ("v", moving)],
-        [
-            ("v", ((slots + 1) * 2 * DEPTH, lanes), F32),
-            ("v", (plan.codes, 8, lanes), F32),
-            ("v", (plan.stored, lanes, lanes), F32),
-        ],
-        [pltpu.VMEM(((slots + 1) * DEPTH, lanes), F32)],
+        [("v", ((slots + 1) * 2 * DEPTH, lanes), F32), weight_out, slope_out],
+        far_table,
         3500,
         "local",
     )
-    density, ratio, slopes = kernel_call(
-        lambda *refs: remote_kernel(plan, *refs),
-        [("s", lists), ("v", own), ("v", first), ("v", second), ("v", near), ("v", weights), ("v", slopes)],
-        [("v", (slots, lanes), F32)] * 2 + [("v", (plan.stored, lanes, lanes), F32)],
-        [pltpu.VMEM(((2 * slots + 1) * DEPTH, lanes), F32), pltpu.VMEM((plan.codes, 8, lanes), F32)],
-        3500,
-        "remote",
-        {6: 2},
-    )
-    first_ratio, second_ratio = both_sides(ratio)
-    (local_sums,) = kernel_call(
+    weights, slopes = kernel_call(
+        lambda *refs: first_kernel(plan, *refs),
+        [("s", lists), ("v", first), ("v", near), ("v", weights), ("v", slopes)],
+        [weight_out, slope_out],
+        far_table,
+        1500,
+        "first",
+        {3: 0, 4: 1},
+    )
+    density, thermal, weights, slopes = kernel_call(
+        lambda *refs: second_kernel(plan, *refs),
+        [("s", lists), ("v", own), ("v", second), ("v", near), ("v", weights), ("v", slopes)],
+        [("v", (slots, lanes), F32), ("v", (4, slots, lanes), F32), weight_out, slope_out],
+        far_table,
+        2000,
+        "second",
+        {4: 2, 5: 3},
+    )
+    first_thermal, second_thermal = both_sides(thermal)
+    (sums,) = kernel_call(
         lambda *refs: local_field_kernel(plan, *refs),
-        [("s", lists), ("v", moving), ("v", ratio), ("v", slopes)],
-        [("v", (plan.codes, 16, lanes), F32)],
-        [pltpu.VMEM(((slots + 1) * FIELD_ROWS, lanes), F32)],
-        2500,
-        "fields",
-    )
-    updated, derived = kernel_call(
+        [("s", lists), ("v", moving), ("v", thermal), ("v", slopes)],
+        [sum_out],
+        field_table,
+        1700,
+        "local_fields",
+    )
+    (sums,) = kernel_call(
+        lambda *refs: first_field_kernel(plan, *refs),
+        [("s", lists), ("v", first), ("v", first_thermal), ("v", slopes), ("v", sums)],
+        [sum_out],
+        field_table,
+        1000,
+        "first_fields",
+        {4: 0},
+    )
+    updated, derived, _ = kernel_call(
         lambda *refs: final_kernel(plan, tiles, cap, floats, *refs),
-        [("s", lists), ("v", own), ("v", moving), ("v", first), ("v", second), ("v", density), ("v", ratio),
-         ("v", first_ratio), ("v", second_ratio), ("v", slopes), ("v", local_sums)]
+        [("s", lists), ("v", own), ("v", moving), ("v", second), ("v", density), ("v", thermal),
+         ("v", second_thermal), ("v", slopes), ("v", sums)]
         + [("v", part) for part in parts],
-        [("v", (slots * floats, lanes), F32), ("v", (5, slots, lanes), F32)],
-        [pltpu.VMEM(((2 * slots + 1) * FIELD_ROWS, lanes), F32), pltpu.VMEM((plan.codes, 16, lanes), F32)],
-        3000,
+        [("v", (slots * floats, lanes), F32), ("v", (5, slots, lanes), F32), sum_out],
+        field_table + [pltpu.VMEM((slots * 16, lanes), F32)],
+        2000,
         "final",
+        {8: 2},
     )
     return updated.reshape(slots, floats, lanes), derived.transpose(1, 0, 2)
 

time: 35.3 us -> 30.9 us (0.88)
  waiting for transfers between devices: 6.72 us -> 3.7 us
  Pallas kernels: 18.8 us -> 15.8 us
  starting transfers between devices: 8.99 us -> 10.4 us
    pallas_call x7 -> x9, Pallas kernels: 18.8 us -> 15.8 us  [kernel_call(): pl.pallas_call(kernel, out_shape=[jax.ShapeDtypeStruct(shape, dtype) for...]
    ppermute x2, waiting for transfers between devices: 3.36 us -> 1.8 us  [both_sides(): second = lax.ppermute(array, 'slab', second_pairs)]
    ppermute x2, starting transfers between devices: 0.19 us -> 1.62 us  [both_sides(): first = lax.ppermute(array, 'slab', first_pairs)]
    ppermute x2, waiting for transfers between devices: 1.81 us -> 0.91 us  [both_sides(): first = lax.ppermute(array, 'slab', first_pairs)]
    ppermute x3, waiting for transfers between devices: 1.55 us -> 0.99 us  [body(): lax.ppermute(packed[k], 'tile', [(t, partner_tile(t, k, tiles)) for t in...]
  transfers between devices with their start and end apart: 7 -> 7, of which waited for: 4 -> 3; matrix products, arithmetic and copies ran while one was open for 0% -> 0% of each run, Pallas kernels for 26% -> 35%
where the time goes in v3:
time: 30.9 us; the launch traced here: 30.6 us
  Pallas kernels  15.8 us (51%)
  starting transfers between devices  10.4 us (34%)
  waiting for transfers between devices  3.7 us (12%)
  between operations  0.72 us (2%)
    pallas_call x9, Pallas kernels, kernel_call(): pl.pallas_call(kernel, out_shape=[jax.ShapeDtypeStruct(shape, dtype) for...  15.8 us
    ppermute x2, starting transfers between devices, both_sides(): second = lax.ppermute(array, 'slab', second_pairs)  5.6 us
    ppermute x3, starting transfers between devices, body(): lax.ppermute(packed[k], 'tile', [(t, partner_tile(t, k, tiles)) for t in...  3.18 us
    ppermute x2, waiting for transfers between devices, both_sides(): second = lax.ppermute(array, 'slab', second_pairs)  1.8 us
    ppermute x2, starting transfers between devices, both_sides(): first = lax.ppermute(array, 'slab', first_pairs)  1.62 us
    ppermute x3, waiting for transfers between devices, body(): lax.ppermute(packed[k], 'tile', [(t, partner_tile(t, k, tiles)) for t in...  0.99 us
    ppermute x2, waiting for transfers between devices, both_sides(): first = lax.ppermute(array, 'slab', first_pairs)  0.91 us
  transfers between devices with their start and end apart: 7, of which 3 were waited for; matrix products, arithmetic and copies ran while one was open for 0% of the time, Pallas kernels for 35%

profile of v3, /device:TPU:0, one launch (start us, length us, event | category | flops | bytes accessed | tf_op | source)
XLA Modules:
  0.0 30.6 jit_solution(1874516607452125322)
XLA Ops:
  0.6 1.1 %pack.1 = (f32[128,128]{1,0:T(8,128)S(1)}, f32[128,128]{1,0:T(8,128)S(1)}, f32[128,128]{1,0:T(8,128)S(1)}, f32[128,128]{1,0:T(8,128)S(1)}) custom-call(s32[32]{0:T(128)} %refs_0_.1, f32[32,16,128]{2,1,0:T(8,128)} %refs_1_.2), custom_call_target="tpu_custom_call" | custom-call | bytes 4500000 | tf_op jit(solution)/shard_map/pack/pallas_call | solution.py:52
  1.7 0.5 %collective-permute-start = (f32[128,128]{1,0:T(8,128)S(1)}, f32[128,128]{1,0:T(8,128)S(1)}, u32[]{:S(2)}, u32[]{:S(2)}) collective-permute-start(f32[128,128]{1,0:T(8,128)S(1)} %get-tuple-element.19), channel_id=1, source_target_pairs={{0,1},{1,0},{2,3},{3,2},{4,5},{5,4},{6,7},{7,6},{8,9},{9,8},{10,11... | collective-permute-start | bytes 196616 | tf_op jit(solution)/shard_map/ppermute | solution.py:478
  2.3 2.6 %collective-permute-start.1 = (f32[128,128]{1,0:T(8,128)S(1)}, f32[128,128]{1,0:T(8,128)S(1)}, u32[]{:S(2)}, u32[]{:S(2)}) collective-permute-start(f32[128,128]{1,0:T(8,128)S(1)} %get-tuple-element.20), channel_id=1, source_target_pairs={{0,2},{1,3},{2,0},{3,1},{4,6},{5,7},{6,4},{7,5},{8,10},{9,11},{10,... | collective-permute-start | bytes 196616 | tf_op jit(solution)/shard_map/ppermute | solution.py:478
  4.9 0.1 collective-permute-start.2
  4.9 3.0 %plan.1.refs_4_.refs_0_ = s32[464]{0:T(512)S(1)} custom-call(s32[4,32]{1,0:T(4,128)} %bitcast.3, s32[32]{0:T(128)} %refs_1_.3, f32[128,128]{1,0:T(8,128)S(1)} %get-tuple-element.18.refs_2_.refs_0_.refs_9_), custom_call_target="tpu_custom_call" | custom-call | bytes 6000000 | tf_op jit(solution)/shard_map/plan/pallas_call | solution.py:52
  7.9 0.0 collective-permute-done.refs_1_.refs_10_
  7.9 0.0 collective-permute-done.1.refs_2_.refs_11_
  7.9 1.0 %collective-permute-done.2.refs_3_.refs_12_ = f32[128,128]{1,0:T(8,128)S(1)} collective-permute-done((f32[128,128]{1,0:T(8,128)S(1)}, f32[128,128]{1,0:T(8,128)S(1)}, u32[]{:S(2)}, u32[]{:S(2)}) %collective-permute-start.2) | collective-permute-done | bytes 65568 | tf_op jit(solution)/shard_map/ppermute | solution.py:478
  8.9 0.1 states.1
  9.0 1.6 %collective-permute-start.4 = (f32[5,32,128]{2,1,0:T(8,128)S(1)}, f32[5,32,128]{2,1,0:T(8,128)S(1)}, u32[]{:S(2)}, u32[]{:S(2)}) collective-permute-start(f32[5,32,128]{2,1,0:T(8,128)S(1)} %get-tuple-element.23.refs_1_.refs_2_), channel_id=1, source_target_pairs={{0,4},{4,0},{8,12},{12,8},{16,20},{20,16},{24,28},{28,24},{1,5},{5... | collective-permute-start | bytes 245768 | tf_op jit(solution)/shard_map/ppermute | solution.py:502
  10.5 3.6 %collective-permute-start.3 = (f32[5,32,128]{2,1,0:T(8,128)S(1)}, f32[5,32,128]{2,1,0:T(8,128)S(1)}, u32[]{:S(2)}, u32[]{:S(2)}) collective-permute-start(f32[5,32,128]{2,1,0:T(8,128)S(1)} %get-tuple-element.23.refs_1_.refs_2_), channel_id=1, source_target_pairs={{0,28},{4,8},{8,4},{12,16},{16,12},{20,24},{24,20},{28,0},{1,29},{... | collective-permute-start | bytes 245768 | tf_op jit(solution)/shard_map/ppermute | solution.py:501
  14.1 3.7 %local.1 = (f32[2112,128]{1,0:T(8,128)S(1)}, f32[132,8,128]{2,1,0:T(8,128)S(1)}, f32[152,128,128]{2,1,0:T(8,128)S(1)}) custom-call(s32[464]{0:T(512)S(1)} %plan.1.refs_4_.refs_0_, f32[5,32,128]{2,1,0:T(8,128)S(1)} %get-tuple-element.23.refs_1_.refs_2_), custom_call_target="tpu_custom_call" | custom-call | bytes 10500000 | tf_op jit(solution)/shard_map/local/pallas_call | solution.py:52
  17.8 0.0 collective-permute-done.4.refs_1_
  17.8 1.8 %first.1 = (f32[132,8,128]{2,1,0:T(8,128)S(1)}, f32[152,128,128]{2,1,0:T(8,128)S(1)}) custom-call(s32[464]{0:T(512)S(1)} %plan.1.refs_4_.refs_0_, f32[5,32,128]{2,1,0:T(8,128)S(1)} %collective-permute-done.4.refs_1_, f32[2112,128]{1,0:T(8,128)S(1)} %get-tuple-element.24.refs_2_.refs_3_, ...), custom_call_target="tpu_custom_call", output_to_operand_aliasing={{0}: (3, {}), {1}: (4, {})} | custom-call | bytes 4500000 | tf_op jit(solution)/shard_map/first/pallas_call | solution.py:52
  19.6 0.0 collective-permute-done.3.refs_2_.refs_3_
  19.6 1.8 %second.1 = (f32[32,128]{1,0:T(8,128)S(1)}, f32[4,32,128]{2,1,0:T(8,128)S(1)}, f32[132,8,128]{2,1,0:T(8,128)S(1)}, f32[152,128,128]{2,1,0:T(8,128)S(1)}) custom-call(s32[464]{0:T(512)S(1)} %plan.1.refs_4_.refs_0_, f32[8,32,128]{2,1,0:T(8,128)S(1)} %get-tuple-element.22.refs_1_, ...), custom_call_target="tpu_custom_call", output_to_operand_aliasing={{2}: (4, {}), {3}: (5, {})} | custom-call | bytes 6000000 | tf_op jit(solution)/shard_map/second/pallas_call | solution.py:52
  21.4 0.1 collective-permute-start.6
  21.5 2.0 %collective-permute-start.5 = (f32[4,32,128]{2,1,0:T(8,128)S(1)}, f32[4,32,128]{2,1,0:T(8,128)S(1)}, u32[]{:S(2)}, u32[]{:S(2)}) collective-permute-start(f32[4,32,128]{2,1,0:T(8,128)S(1)} %get-tuple-element.30.refs_2_.refs_5_), channel_id=1, source_target_pairs={{0,28},{4,8},{8,4},{12,16},{16,12},{20,24},{24,20},{28,0},{1,29},{... | collective-permute-start | bytes 196616 | tf_op jit(solution)/shard_map/ppermute | solution.py:501
  23.5 1.5 %local_fields.1.refs_4_ = f32[132,16,128]{2,1,0:T(8,128)S(1)} custom-call(s32[464]{0:T(512)S(1)} %plan.1.refs_4_.refs_0_, f32[5,32,128]{2,1,0:T(8,128)S(1)} %get-tuple-element.23.refs_1_.refs_2_, f32[4,32,128]{2,1,0:T(8,128)S(1)} %get-tuple-element.30.refs_2_.refs_5_, f32[152,128,128]{2,1,0:T(8,128)S(1)} %get-tuple-element.31.refs_3_.refs_7_), custom_call_target="tpu_custom_call" | custom-call | bytes 5100000 | tf_op jit(solution)/shard_map/local_fields/pallas_call | solution.py:52
  25.0 0.9 %collective-permute-done.6.refs_2_ = f32[4,32,128]{2,1,0:T(8,128)S(1)} collective-permute-done((f32[4,32,128]{2,1,0:T(8,128)S(1)}, f32[4,32,128]{2,1,0:T(8,128)S(1)}, u32[]{:S(2)}, u32[]{:S(2)}) %collective-permute-start.6) | collective-permute-done | bytes 65568 | tf_op jit(solution)/shard_map/ppermute | solution.py:502
  25.9 1.0 %first_fields.1.refs_8_ = f32[132,16,128]{2,1,0:T(8,128)S(1)} custom-call(s32[464]{0:T(512)S(1)} %plan.1.refs_4_.refs_0_, f32[5,32,128]{2,1,0:T(8,128)S(1)} %collective-permute-done.4.refs_1_, f32[4,32,128]{2,1,0:T(8,128)S(1)} %collective-permute-done.6.refs_2_, ...), custom_call_target="tpu_custom_call", output_to_operand_aliasing={{}: (4, {})} | custom-call | bytes 3000000 | tf_op jit(solution)/shard_map/first_fields/pallas_call | solution.py:52
  26.9 1.8 %collective-permute-done.5.refs_6_ = f32[4,32,128]{2,1,0:T(8,128)S(1)} collective-permute-done((f32[4,32,128]{2,1,0:T(8,128)S(1)}, f32[4,32,128]{2,1,0:T(8,128)S(1)}, u32[]{:S(2)}, u32[]{:S(2)}) %collective-permute-start.5) | collective-permute-done | bytes 65568 | tf_op jit(solution)/shard_map/ppermute | solution.py:501
  28.7 1.9 %final.1 = (f32[512,128]{1,0:T(8,128)}, f32[5,32,128]{2,1,0:T(8,128)}, f32[132,16,128]{2,1,0:T(8,128)S(1)}) custom-call(s32[464]{0:T(512)S(1)} %plan.1.refs_4_.refs_0_, f32[8,32,128]{2,1,0:T(8,128)S(1)} %get-tuple-element.22.refs_1_, f32[5,32,128]{2,1,0:T(8,128)S(1)} %get-tuple-element.23.refs_1_.refs_2_, ...), custom_call_target="tpu_custom_call", output_to_operand_aliasing={{2}: (8, {})} | custom-call | bytes 6000000 | tf_op jit(solution)/shard_map/final/pallas_call | solution.py:52
Async XLA Ops:
  1.7 6.2 %collective-permute-start = (f32[128,128]{1,0:T(8,128)S(1)}, f32[128,128]{1,0:T(8,128)S(1)}, u32[]{:S(2)}, u32[]{:S(2)}) collective-permute-start(f32[128,128]{1,0:T(8,128)S(1)} %get-tuple-element.19), channel_id=1, source_target_pairs={{0,1},{1,0},{2,3},{3,2},{4,5},{5,4},{6,7},{7,6},{8,9},{9,8},{10,11... | collective-permute-start | bytes 196616 | tf_op jit(solution)/shard_map/ppermute | solution.py:478
  2.3 5.7 %collective-permute-start.1 = (f32[128,128]{1,0:T(8,128)S(1)}, f32[128,128]{1,0:T(8,128)S(1)}, u32[]{:S(2)}, u32[]{:S(2)}) collective-permute-start(f32[128,128]{1,0:T(8,128)S(1)} %get-tuple-element.20), channel_id=1, source_target_pairs={{0,2},{1,3},{2,0},{3,1},{4,6},{5,7},{6,4},{7,5},{8,10},{9,11},{10,... | collective-permute-start | bytes 196616 | tf_op jit(solution)/shard_map/ppermute | solution.py:478
  4.9 4.0 %collective-permute-start.2 = (f32[128,128]{1,0:T(8,128)S(1)}, f32[128,128]{1,0:T(8,128)S(1)}, u32[]{:S(2)}, u32[]{:S(2)}) collective-permute-start(f32[128,128]{1,0:T(8,128)S(1)} %get-tuple-element.21), channel_id=1, source_target_pairs={{0,3},{1,2},{2,1},{3,0},{4,7},{5,6},{6,5},{7,4},{8,11},{9,10},{10,... | collective-permute-start | bytes 196616 | tf_op jit(solution)/shard_map/ppermute | solution.py:478
  9.0 8.8 %collective-permute-start.4 = (f32[5,32,128]{2,1,0:T(8,128)S(1)}, f32[5,32,128]{2,1,0:T(8,128)S(1)}, u32[]{:S(2)}, u32[]{:S(2)}) collective-permute-start(f32[5,32,128]{2,1,0:T(8,128)S(1)} %get-tuple-element.23.refs_1_.refs_2_), channel_id=1, source_target_pairs={{0,4},{4,0},{8,12},{12,8},{16,20},{20,16},{24,28},{28,24},{1,5},{5... | collective-permute-start | bytes 245768 | tf_op jit(solution)/shard_map/ppermute | solution.py:502
  10.5 9.0 %collective-permute-start.3 = (f32[5,32,128]{2,1,0:T(8,128)S(1)}, f32[5,32,128]{2,1,0:T(8,128)S(1)}, u32[]{:S(2)}, u32[]{:S(2)}) collective-permute-start(f32[5,32,128]{2,1,0:T(8,128)S(1)} %get-tuple-element.23.refs_1_.refs_2_), channel_id=1, source_target_pairs={{0,28},{4,8},{8,4},{12,16},{16,12},{20,24},{24,20},{28,0},{1,29},{... | collective-permute-start | bytes 245768 | tf_op jit(solution)/shard_map/ppermute | solution.py:501
  21.4 4.5 %collective-permute-start.6 = (f32[4,32,128]{2,1,0:T(8,128)S(1)}, f32[4,32,128]{2,1,0:T(8,128)S(1)}, u32[]{:S(2)}, u32[]{:S(2)}) collective-permute-start(f32[4,32,128]{2,1,0:T(8,128)S(1)} %get-tuple-element.30.refs_2_.refs_5_), channel_id=1, source_target_pairs={{0,4},{4,0},{8,12},{12,8},{16,20},{20,16},{24,28},{28,24},{1,5},{5... | collective-permute-start | bytes 196616 | tf_op jit(solution)/shard_map/ppermute | solution.py:502
  21.5 7.2 %collective-permute-start.5 = (f32[4,32,128]{2,1,0:T(8,128)S(1)}, f32[4,32,128]{2,1,0:T(8,128)S(1)}, u32[]{:S(2)}, u32[]{:S(2)}) collective-permute-start(f32[4,32,128]{2,1,0:T(8,128)S(1)} %get-tuple-element.30.refs_2_.refs_5_), channel_id=1, source_target_pairs={{0,28},{4,8},{8,4},{12,16},{16,12},{20,24},{24,20},{28,0},{1,29},{... | collective-permute-start | bytes 196616 | tf_op jit(solution)/shard_map/ppermute | solution.py:501

commit v4 on v3

--- a/solution.py
+++ b/solution.py
@@ -17,6 +17,8 @@
 AWAY = 1.0e4
 LANES = 128
 GROUPS = (24, 16, 8)
+EARLY = 1
+CORE = 9
 DEPTH = 32
 FIELD_ROWS = 40
 
@@ -51,7 +53,10 @@
 def kernel_call(kernel, ins, outs, scratch, nanoseconds, name, aliases=None):
     return pl.pallas_call(
         kernel,
-        out_shape=[jax.ShapeDtypeStruct(shape, dtype) for _, shape, dtype in outs],
+        out_shape=[
+            pltpu.SMEM(shape, dtype) if memory == "s" else jax.ShapeDtypeStruct(shape, dtype)
+            for memory, shape, dtype in outs
+        ],
         in_specs=[SPECS[memory]() for memory, _ in ins],
         out_specs=[SPECS[memory]() for memory, _, _ in outs],
         scratch_shapes=scratch,
@@ -168,7 +173,7 @@
             totals = tuple(kept)
         return totals
 
-    totals = lax.fori_loop(0, slots, fill, (jnp.int32(0),) * 3)
+    totals = lax.fori_loop(0, slots, fill, (jnp.int32(0),) * 3, unroll=4)
     for w in range(3):
         for k in range(GROUPS[0]):
             plan_ref[w * plan.length + totals[w] + k] = plan.dummy
@@ -176,7 +181,7 @@
 
 
 def pack_kernel(tiles, cap, floats, dest_ref, particles_ref, *refs):
-    outs, (packed, staged, dest, sems) = refs[:tiles], refs[tiles:]
+    cores, rests, (packed, staged, dest, sems) = refs[:tiles], refs[tiles : 2 * tiles], refs[2 * tiles :]
     bring = [pltpu.make_async_copy(dest_ref, dest, sems.at[0]), pltpu.make_async_copy(particles_ref, staged, sems.at[1])]
     for copy in bring:
         copy.start()
@@ -189,36 +194,40 @@
         target = dest[b]
         owner = lax.div(target, cap)
         step = owner ^ me if is_power(tiles) else lax.rem(owner + tiles - me, tiles)
-        packed[step * cap + lax.rem(target, cap)] = staged[b]
+        start = pl.multiple_of((step * cap + lax.rem(target, cap)) * floats, 8)
+        packed[pl.ds(start, floats), :] = staged[b]
         return carry
 
     lax.fori_loop(0, staged.shape[0], place, 0, unroll=4)
     for k in range(tiles):
-        outs[k][...] = packed[k * cap : (k + 1) * cap].reshape(cap * floats, LANES)
-
-
-def states_kernel(tiles, cap, floats, *refs):
-    parts, (after_ref, own_ref, moving_ref) = refs[:tiles], refs[tiles:]
+        for f in range(floats):
+            value = packed[pl.ds(k * cap * floats + f, cap, stride=floats), :]
+            if f < CORE:
+                cores[k][f] = value
+            else:
+                rests[k][f - CORE] = value
+
+
+def states_kernel(tiles, cap, steps, *refs):
+    parts, (own_ref, moving_ref) = dict(zip(steps, refs)), refs[-2:]
     me = lax.axis_index("tile")
-    for k in range(tiles):
-        base = pl.multiple_of(source_tile(me, k, tiles) * cap, cap)
-        rows = pl.ds(base, cap)
-
-        def field(f):
-            return parts[k][pl.ds(f, cap, stride=floats), :]
-
-        for f in range(8):
-            own_ref[f, rows, :] = field(f)
-        mass = field(6)
+    for k in steps:
+        rows = pl.ds(pl.multiple_of(source_tile(me, k, tiles) * cap, cap), cap)
+        field = parts[k]
+        for f in range(CORE):
+            own_ref[f, rows, :] = field[f]
+        mass = field[6]
         present = mass > 0
         for f in range(3):
-            moving_ref[f, rows, :] = field(f) - CENTRE
-        moving_ref[3, rows, :] = jnp.where(present, field(8), 1.0)
+            moving_ref[f, rows, :] = field[f] - CENTRE
+        moving_ref[3, rows, :] = jnp.where(present, field[8], 1.0)
         scaled = jnp.where(present, mass * MASS_UNIT, 1.0)
         root = jnp.exp(jnp.log(scaled) * (-1.0 / 3.0))
         for _ in range(2):
             root = root * (4.0 - scaled * (root * root * root)) * (1.0 / 3.0)
         moving_ref[4, rows, :] = jnp.where(present, root, 0.0)
+        for f in range(EARLY):
+            moving_ref[5 + f, rows, :] = field[3 + f]
 
 
 def store_far(far_ref, base, moving_ref, slots):
@@ -344,8 +353,8 @@
     density_ref[...] = density
     safe = jnp.where(own_ref[6] > 0, density, 1.0)
     thermal_ref[0] = (ADIABATIC - 1.0) * density * own_ref[7] / (safe * safe)
-    for f in range(3):
-        thermal_ref[1 + f] = own_ref[3 + f]
+    for f in range(EARLY, 3):
+        thermal_ref[1 + f - EARLY] = own_ref[3 + f]
 
 
 def store_fields(field_ref, base, moving_ref, thermal_ref, slots):
@@ -355,7 +364,7 @@
     stretch = moving_ref[4]
     square = stretch * stretch
     place = [moving_ref[f] for f in range(3)]
-    speed = [thermal_ref[1 + f] for f in range(3)]
+    speed = [moving_ref[5 + f] if f < EARLY else thermal_ref[1 + f - EARLY] for f in range(3)]
     dotted = place[0] * speed[0] + place[1] * speed[1] + place[2] * speed[2]
     plain = [square] + [square * value for value in place + speed + [dotted]]
     heavy = [thermal_ref[0] * value for value in plain[0:4]]
@@ -395,6 +404,10 @@
     in_groups(plan, plan_ref, which, work)
 
 
+def hold_kernel(*refs):
+    pass
+
+
 def local_field_kernel(plan, plan_ref, moving_ref, thermal_ref, slope_ref, sum_ref, field_ref):
     store_fields(field_ref, 0, moving_ref, thermal_ref, plan.slots)
     store_field_dummy(field_ref, plan.slots)
@@ -410,17 +423,16 @@
 
 def final_kernel(plan, tiles, cap, floats, plan_ref, own_ref, moving_ref, second_ref, density_ref, thermal_ref,
                  second_thermal_ref, slope_ref, sum_in_ref, *refs):
-    parts, (updated_ref, derived_ref, sum_ref, field_ref, total_ref) = refs[:tiles], refs[tiles:]
+    rests, (updated_ref, derived_ref, sum_ref, field_ref, total_ref) = refs[:tiles], refs[tiles:]
     slots = plan.slots
     store_fields(field_ref, 0, second_ref, second_thermal_ref, slots)
     store_field_dummy(field_ref, slots)
     me = lax.axis_index("tile")
     for k in range(tiles):
-        base = source_tile(me, k, tiles) * cap
-        for j in range(cap):
-            present = (parts[k][j * floats + 6 : j * floats + 7, :] > 0).astype(F32)
-            start = pl.multiple_of((base + j) * floats + 8, 8)
-            updated_ref[pl.ds(start, floats - 8), :] = parts[k][j * floats + 8 : (j + 1) * floats, :] * present
+        base = pl.multiple_of(source_tile(me, k, tiles) * cap, cap)
+        held = (own_ref[6, pl.ds(base, cap), :] > 0).astype(F32)
+        for f in range(floats - CORE):
+            updated_ref[pl.ds(base * floats + CORE + f, cap, stride=floats), :] = rests[k][f] * held
     field_loop(plan, plan_ref, 2, field_ref, slope_ref, sum_ref)
     for i in range(slots):
         first = i << plan.entry_bits
@@ -450,7 +462,8 @@
         fresh[f] = own_ref[f] + TIMESTEP * fresh[3 + f]
     fresh[6] = own_ref[6]
     fresh[7] = own_ref[7] + TIMESTEP * heating
-    for f in range(8):
+    fresh[8] = own_ref[8]
+    for f in range(CORE):
         updated_ref[pl.ds(f, slots, stride=floats), :] = fresh[f] * present
     for f, value in enumerate([density] + accel + [heating]):
         derived_ref[f] = value * present
@@ -464,9 +477,9 @@
     packed = kernel_call(
         lambda *refs: pack_kernel(tiles, cap, floats, *refs),
         [("h", in_hbm(dest_slot)), ("h", in_hbm(particles))],
-        [("v", (cap * floats, lanes), F32)] * tiles,
+        [("v", (CORE, cap, lanes), F32)] * tiles + [("v", (floats - CORE, cap, lanes), F32)] * tiles,
         [
-            pltpu.VMEM((slots, floats, lanes), F32),
+            pltpu.VMEM((slots * floats, lanes), F32),
             pltpu.VMEM((bins, floats, lanes), F32),
             pltpu.SMEM((bins,), I32),
             pltpu.SemaphoreType.DMA((2,)),
@@ -474,10 +487,11 @@
         1500,
         "pack",
     )
-    parts = [packed[0]] + [
-        lax.ppermute(packed[k], "tile", [(t, partner_tile(t, k, tiles)) for t in range(tiles)])
-        for k in range(1, tiles)
-    ]
+    packed, rests = packed[:tiles], packed[tiles:]
+
+    def to_partner(array, step):
+        return lax.ppermute(array, "tile", [(t, partner_tile(t, step, tiles)) for t in range(tiles)])
+
     (lists,) = kernel_call(
         lambda *refs: plan_kernel(plan, *refs),
         [("s", in_hbm(neighbours.T)), ("s", in_hbm(counts)), ("a", packed[0])],
@@ -486,14 +500,27 @@
         2000,
         "plan",
     )
+    parts = [packed[0]] + [to_partner(packed[k], k) for k in range(1, tiles)]
+    state_outs = [("v", (CORE, slots, lanes), F32), ("v", (5 + EARLY, slots, lanes), F32)]
+    far_steps = [k for k in range(tiles) if k != 1]
     own, moving = kernel_call(
-        lambda *refs: states_kernel(tiles, cap, floats, *refs),
-        [("v", part) for part in parts] + [("a", lists)],
-        [("v", (8, slots, lanes), F32), ("v", (5, slots, lanes), F32)],
+        lambda *refs: states_kernel(tiles, cap, far_steps, *refs),
+        [("v", parts[k]) for k in far_steps],
+        state_outs,
         [],
         200,
-        "states",
-    )
+        "far_states",
+    )
+    if tiles > 1:
+        own, moving = kernel_call(
+            lambda *refs: states_kernel(tiles, cap, [1], *refs),
+            [("v", parts[1]), ("v", own), ("v", moving), ("a", lists)],
+            state_outs,
+            [],
+            100,
+            "near_states",
+            {1: 0, 2: 1},
+        )
     first_pairs = [(s, s ^ 1) for s in range(slabs)]
     second_pairs = [(s, (((s + 1) ^ 1) - 1) % slabs) for s in range(slabs)]
 
@@ -528,13 +555,22 @@
     density, thermal, weights, slopes = kernel_call(
         lambda *refs: second_kernel(plan, *refs),
         [("s", lists), ("v", own), ("v", second), ("v", near), ("v", weights), ("v", slopes)],
-        [("v", (slots, lanes), F32), ("v", (4, slots, lanes), F32), weight_out, slope_out],
+        [("v", (slots, lanes), F32), ("v", (4 - EARLY, slots, lanes), F32), weight_out, slope_out],
         far_table,
         2000,
         "second",
         {4: 2, 5: 3},
     )
     first_thermal, second_thermal = both_sides(thermal)
+    later = kernel_call(
+        hold_kernel,
+        [("a", rest) for rest in rests[1:]] + [("a", thermal)],
+        [("a", (floats - CORE, cap, lanes), F32)] * (tiles - 1),
+        [],
+        10,
+        "hold",
+        {k: k for k in range(tiles - 1)},
+    )
     (sums,) = kernel_call(
         lambda *refs: local_field_kernel(plan, *refs),
         [("s", lists), ("v", moving), ("v", thermal), ("v", slopes)],
@@ -543,6 +579,7 @@
         1700,
         "local_fields",
     )
+    rests = [rests[0]] + [to_partner(later[k - 1], k) for k in range(1, tiles)]
     (sums,) = kernel_call(
         lambda *refs: first_field_kernel(plan, *refs),
         [("s", lists), ("v", first), ("v", first_thermal), ("v", slopes), ("v", sums)],
@@ -556,7 +593,7 @@
         lambda *refs: final_kernel(plan, tiles, cap, floats, *refs),
         [("s", lists), ("v", own), ("v", moving), ("v", second), ("v", density), ("v", thermal),
          ("v", second_thermal), ("v", slopes), ("v", sums)]
-        + [("v", part) for part in parts],
+        + [("v", rest) for rest in rests],
         [("v", (slots * floats, lanes), F32), ("v", (5, slots, lanes), F32), sum_out],
         field_table + [pltpu.VMEM((slots * 16, lanes), F32)],
         2000,

time: 30.9 us -> 28.2 us (0.913); the launches traced: 30.6 us -> 28.3 us
  Pallas kernels: 15.8 us -> 12.1 us
  starting transfers between devices: 10.4 us -> 13.3 us
  waiting for transfers between devices: 3.7 us -> 2.09 us
    pallas_call x9 -> x11, Pallas kernels: 15.8 us -> 12.1 us  [kernel_call(): pl.pallas_call(kernel, out_shape=[pltpu.SMEM(shape, dtype) if memory == '...]
    ppermute x3 -> x6, starting transfers between devices: 3.18 us -> 5.09 us  [to_partner(): lax.ppermute(array, 'tile', [(t, partner_tile(t, step, tiles)) for t in r...]
    ppermute x2, waiting for transfers between devices: 1.8 us -> 0.01 us  [both_sides(): second = lax.ppermute(array, 'slab', second_pairs)]
    ppermute x3 -> x6, waiting for transfers between devices: 0.99 us -> 2.08 us  [to_partner(): lax.ppermute(array, 'tile', [(t, partner_tile(t, step, tiles)) for t in r...]
    ppermute x2, starting transfers between devices: 5.6 us -> 6.61 us  [both_sides(): second = lax.ppermute(array, 'slab', second_pairs)]
    ppermute x2, waiting for transfers between devices: 0.91 us -> 0.01 us  [both_sides(): first = lax.ppermute(array, 'slab', first_pairs)]
  transfers between devices with their start and end apart: 7 -> 10, of which waited for: 3 -> 3; matrix products, arithmetic and copies ran while one was open for 0% -> 0% of each run, Pallas kernels for 35% -> 29%
where the time goes in v4:
time: 28.2 us; the launch traced here: 28.3 us
  starting transfers between devices  13.3 us (47%)
  Pallas kernels  12.1 us (43%)
  waiting for transfers between devices  2.09 us (7%)
  between operations  0.74 us (3%)
    pallas_call x11, Pallas kernels, kernel_call(): pl.pallas_call(kernel, out_shape=[pltpu.SMEM(shape, dtype) if memory == '...  12.1 us
    ppermute x2, starting transfers between devices, both_sides(): second = lax.ppermute(array, 'slab', second_pairs)  6.61 us
    ppermute x6, starting transfers between devices, to_partner(): lax.ppermute(array, 'tile', [(t, partner_tile(t, step, tiles)) for t in r...  5.09 us
    ppermute x6, waiting for transfers between devices, to_partner(): lax.ppermute(array, 'tile', [(t, partner_tile(t, step, tiles)) for t in r...  2.08 us
    ppermute x2, starting transfers between devices, both_sides(): first = lax.ppermute(array, 'slab', first_pairs)  1.65 us
  transfers between devices with their start and end apart: 10, of which 3 were waited for; matrix products, arithmetic and copies ran while one was open for 0% of the time, Pallas kernels for 29%

profile of v4, /device:TPU:0, one launch (start us, length us, event | category | flops | bytes accessed | tf_op | source)
XLA Modules:
  0.0 28.3 jit_solution(3576429088314996013)
XLA Ops:
  0.6 1.2 %pack.1 = (f32[9,8,128]{2,1,0:T(8,128)S(1)}, f32[9,8,128]{2,1,0:T(8,128)S(1)}, f32[9,8,128]{2,1,0:T(8,128)S(1)}, f32[9,8,128]{2,1,0:T(8,128)S(1)}, f32[7,8,128]{...) custom-call(s32[32]{0:T(128)} %refs_0_.1, f32[32,16,128]{2,1,0:T(8,128)} %refs_1_.2), custom_call_target="tpu_custom_call" | custom-call | bytes 4500000 | tf_op jit(solution)/shard_map/pack/pallas_call | solution.py:54
  1.8 3.0 %collective-permute-start.1 = (f32[9,8,128]{2,1,0:T(8,128)S(1)}, f32[9,8,128]{2,1,0:T(8,128)S(1)}, u32[]{:S(2)}, u32[]{:S(2)}) collective-permute-start(f32[9,8,128]{2,1,0:T(8,128)S(1)} %get-tuple-element.29), channel_id=1, source_target_pairs={{0,2},{1,3},{2,0},{3,1},{4,6},{5,7},{6,4},{7,5},{8,10},{9,11},{10,... | collective-permute-start | bytes 110600 | tf_op jit(solution)/shard_map/ppermute | solution.py:493
  4.8 0.0 collective-permute-start.2
  4.8 0.2 collective-permute-start
  5.0 2.2 %plan.1.refs_3_.refs_0_ = s32[464]{0:T(512)S(4)} custom-call(s32[4,32]{1,0:T(4,128)} %bitcast.3, s32[32]{0:T(128)} %refs_1_.3, f32[9,8,128]{2,1,0:T(8,128)S(1)} %get-tuple-element.27.refs_2_.refs_0_), custom_call_target="tpu_custom_call" | custom-call | bytes 6000000 | tf_op jit(solution)/shard_map/plan/pallas_call | solution.py:54
  7.3 0.0 collective-permute-done.1.refs_1_
  7.3 1.1 %collective-permute-done.2.refs_2_ = f32[9,8,128]{2,1,0:T(8,128)S(1)} collective-permute-done((f32[9,8,128]{2,1,0:T(8,128)S(1)}, f32[9,8,128]{2,1,0:T(8,128)S(1)}, u32[]{:S(2)}, u32[]{:S(2)}) %collective-permute-start.2) | collective-permute-done | bytes 36896 | tf_op jit(solution)/shard_map/ppermute | solution.py:493
  8.4 0.0 collective-permute-done.refs_0_
  8.4 1.6 %collective-permute-start.4 = (f32[6,32,128]{2,1,0:T(8,128)S(1)}, f32[6,32,128]{2,1,0:T(8,128)S(1)}, u32[]{:S(2)}, u32[]{:S(2)}) collective-permute-start(f32[6,32,128]{2,1,0:T(8,128)S(1)} %get-tuple-element.34.refs_1_.refs_2_), channel_id=1, source_target_pairs={{0,4},{4,0},{8,12},{12,8},{16,20},{20,16},{24,28},{28,24},{1,5},{5... | collective-permute-start | bytes 294920 | tf_op jit(solution)/shard_map/ppermute | solution.py:529
  10.0 3.6 %collective-permute-start.3 = (f32[6,32,128]{2,1,0:T(8,128)S(1)}, f32[6,32,128]{2,1,0:T(8,128)S(1)}, u32[]{:S(2)}, u32[]{:S(2)}) collective-permute-start(f32[6,32,128]{2,1,0:T(8,128)S(1)} %get-tuple-element.34.refs_1_.refs_2_), channel_id=1, source_target_pairs={{0,28},{4,8},{8,4},{12,16},{16,12},{20,24},{24,20},{28,0},{1,29},{... | collective-permute-start | bytes 294920 | tf_op jit(solution)/shard_map/ppermute | solution.py:528
  13.6 3.1 %local.1 = (f32[2112,128]{1,0:T(8,128)S(1)}, f32[132,8,128]{2,1,0:T(8,128)S(1)}, f32[152,128,128]{2,1,0:T(8,128)S(1)}) custom-call(s32[464]{0:T(512)S(4)} %plan.1.refs_3_.refs_0_, f32[6,32,128]{2,1,0:T(8,128)S(1)} %get-tuple-element.34.refs_1_.refs_2_), custom_call_target="tpu_custom_call" | custom-call | bytes 10500000 | tf_op jit(solution)/shard_map/local/pallas_call | solution.py:54
  16.7 0.0 collective-permute-done.4.refs_1_
  16.7 1.5 %first.1 = (f32[132,8,128]{2,1,0:T(8,128)S(1)}, f32[152,128,128]{2,1,0:T(8,128)S(1)}) custom-call(s32[464]{0:T(512)S(4)} %plan.1.refs_3_.refs_0_, f32[6,32,128]{2,1,0:T(8,128)S(1)} %collective-permute-done.4.refs_1_, f32[2112,128]{1,0:T(8,128)S(1)} %get-tuple-element.35.refs_2_.refs_3_, ...), custom_call_target="tpu_custom_call", output_to_operand_aliasing={{0}: (3, {}), {1}: (4, {})} | custom-call | bytes 4500000 | tf_op jit(solution)/shard_map/first/pallas_call | solution.py:54
  18.2 0.0 collective-permute-done.3.refs_2_.refs_3_
  18.2 1.2 %second.1 = (f32[32,128]{1,0:T(8,128)S(1)}, f32[3,32,128]{2,1,0:T(8,128)S(1)}, f32[132,8,128]{2,1,0:T(8,128)S(1)}, f32[152,128,128]{2,1,0:T(8,128)S(1)}) custom-call(s32[464]{0:T(512)S(4)} %plan.1.refs_3_.refs_0_, f32[9,32,128]{2,1,0:T(8,128)S(1)} %get-tuple-element.33.refs_1_, ...), custom_call_target="tpu_custom_call", output_to_operand_aliasing={{2}: (4, {}), {3}: (5, {})} | custom-call | bytes 6000000 | tf_op jit(solution)/shard_map/second/pallas_call | solution.py:54
  19.4 0.1 collective-permute-start.6
  19.5 3.0 %collective-permute-start.5 = (f32[3,32,128]{2,1,0:T(8,128)S(1)}, f32[3,32,128]{2,1,0:T(8,128)S(1)}, u32[]{:S(2)}, u32[]{:S(2)}) collective-permute-start(f32[3,32,128]{2,1,0:T(8,128)S(1)} %get-tuple-element.41.refs_2_.refs_3_.refs_5_), channel_id=1, source_target_pairs={{0,28},{4,8},{8,4},{12,16},{16,12},{20,24},{24,20},{28,0},{1,29},{... | collective-permute-start | bytes 147464 | tf_op jit(solution)/shard_map/ppermute | solution.py:528
  22.6 0.0 collective-permute-start.7
  22.6 1.0 %collective-permute-start.8 = (f32[7,8,128]{2,1,0:T(8,128)S(1)}, f32[7,8,128]{2,1,0:T(8,128)S(1)}, u32[]{:S(2)}, u32[]{:S(2)}) collective-permute-start(f32[7,8,128]{2,1,0:T(8,128)S(1)} %get-tuple-element.48), channel_id=1, source_target_pairs={{0,2},{1,3},{2,0},{3,1},{4,6},{5,7},{6,4},{7,5},{8,10},{9,11},{10,... | collective-permute-start | bytes 86024 | tf_op jit(solution)/shard_map/ppermute | solution.py:493
  23.6 0.9 %collective-permute-start.9 = (f32[7,8,128]{2,1,0:T(8,128)S(1)}, f32[7,8,128]{2,1,0:T(8,128)S(1)}, u32[]{:S(2)}, u32[]{:S(2)}) collective-permute-start(f32[7,8,128]{2,1,0:T(8,128)S(1)} %get-tuple-element.49), channel_id=1, source_target_pairs={{0,3},{1,2},{2,1},{3,0},{4,7},{5,6},{6,5},{7,4},{8,11},{9,10},{10,... | collective-permute-start | bytes 86024 | tf_op jit(solution)/shard_map/ppermute | solution.py:493
  24.4 0.9 %local_fields.1.refs_4_ = f32[132,16,128]{2,1,0:T(8,128)S(1)} custom-call(s32[464]{0:T(512)S(4)} %plan.1.refs_3_.refs_0_, f32[6,32,128]{2,1,0:T(8,128)S(1)} %get-tuple-element.34.refs_1_.refs_2_, f32[3,32,128]{2,1,0:T(8,128)S(1)} %get-tuple-element.41.refs_2_.refs_3_.refs_5_, f32[152,128,128]{2,1,0:T(8,128)S(1)} %get-tuple-element.42.refs_3_.refs_7_), custom_call_target="tpu_custom_call" | custom-call | bytes 5100000 | tf_op jit(solution)/shard_map/local_fields/pallas_call | solution.py:54
  25.4 0.0 collective-permute-done.6.refs_2_
  25.4 0.5 %first_fields.1.refs_8_ = f32[132,16,128]{2,1,0:T(8,128)S(1)} custom-call(s32[464]{0:T(512)S(4)} %plan.1.refs_3_.refs_0_, f32[6,32,128]{2,1,0:T(8,128)S(1)} %collective-permute-done.4.refs_1_, f32[3,32,128]{2,1,0:T(8,128)S(1)} %collective-permute-done.6.refs_2_, ...), custom_call_target="tpu_custom_call", output_to_operand_aliasing={{}: (4, {})} | custom-call | bytes 3000000 | tf_op jit(solution)/shard_map/first_fields/pallas_call | solution.py:54
  25.9 0.0 collective-permute-done.7.refs_10_
  25.9 0.6 %collective-permute-done.8.refs_11_ = f32[7,8,128]{2,1,0:T(8,128)S(1)} collective-permute-done((f32[7,8,128]{2,1,0:T(8,128)S(1)}, f32[7,8,128]{2,1,0:T(8,128)S(1)}, u32[]{:S(2)}, u32[]{:S(2)}) %collective-permute-start.8) | collective-permute-done | bytes 28704 | tf_op jit(solution)/shard_map/ppermute | solution.py:493
  26.4 0.4 %collective-permute-done.9.refs_12_ = f32[7,8,128]{2,1,0:T(8,128)S(1)} collective-permute-done((f32[7,8,128]{2,1,0:T(8,128)S(1)}, f32[7,8,128]{2,1,0:T(8,128)S(1)}, u32[]{:S(2)}, u32[]{:S(2)}) %collective-permute-start.9) | collective-permute-done | bytes 28704 | tf_op jit(solution)/shard_map/ppermute | solution.py:493
  26.9 0.0 collective-permute-done.5.refs_6_
  26.9 1.4 %final.1 = (f32[512,128]{1,0:T(8,128)}, f32[5,32,128]{2,1,0:T(8,128)}, f32[132,16,128]{2,1,0:T(8,128)S(1)}) custom-call(s32[464]{0:T(512)S(4)} %plan.1.refs_3_.refs_0_, f32[9,32,128]{2,1,0:T(8,128)S(1)} %get-tuple-element.33.refs_1_, f32[6,32,128]{2,1,0:T(8,128)S(1)} %get-tuple-element.34.refs_1_.refs_2_, ...), custom_call_target="tpu_custom_call", output_to_operand_aliasing={{2}: (8, {})} | custom-call | bytes 6000000 | tf_op jit(solution)/shard_map/final/pallas_call | solution.py:54
  (3 shorter events, 0.1 us)
Async XLA Ops:
  1.8 5.5 %collective-permute-start.1 = (f32[9,8,128]{2,1,0:T(8,128)S(1)}, f32[9,8,128]{2,1,0:T(8,128)S(1)}, u32[]{:S(2)}, u32[]{:S(2)}) collective-permute-start(f32[9,8,128]{2,1,0:T(8,128)S(1)} %get-tuple-element.29), channel_id=1, source_target_pairs={{0,2},{1,3},{2,0},{3,1},{4,6},{5,7},{6,4},{7,5},{8,10},{9,11},{10,... | collective-permute-start | bytes 110600 | tf_op jit(solution)/shard_map/ppermute | solution.py:493
  4.8 3.5 %collective-permute-start.2 = (f32[9,8,128]{2,1,0:T(8,128)S(1)}, f32[9,8,128]{2,1,0:T(8,128)S(1)}, u32[]{:S(2)}, u32[]{:S(2)}) collective-permute-start(f32[9,8,128]{2,1,0:T(8,128)S(1)} %get-tuple-element.30), channel_id=1, source_target_pairs={{0,3},{1,2},{2,1},{3,0},{4,7},{5,6},{6,5},{7,4},{8,11},{9,10},{10,... | collective-permute-start | bytes 110600 | tf_op jit(solution)/shard_map/ppermute | solution.py:493
  4.8 3.6 %collective-permute-start = (f32[9,8,128]{2,1,0:T(8,128)S(1)}, f32[9,8,128]{2,1,0:T(8,128)S(1)}, u32[]{:S(2)}, u32[]{:S(2)}) collective-permute-start(f32[9,8,128]{2,1,0:T(8,128)S(1)} %get-tuple-element.28), channel_id=1, source_target_pairs={{0,1},{1,0},{2,3},{3,2},{4,5},{5,4},{6,7},{7,6},{8,9},{9,8},{10,11... | collective-permute-start | bytes 110600 | tf_op jit(solution)/shard_map/ppermute | solution.py:493
  8.4 8.2 %collective-permute-start.4 = (f32[6,32,128]{2,1,0:T(8,128)S(1)}, f32[6,32,128]{2,1,0:T(8,128)S(1)}, u32[]{:S(2)}, u32[]{:S(2)}) collective-permute-start(f32[6,32,128]{2,1,0:T(8,128)S(1)} %get-tuple-element.34.refs_1_.refs_2_), channel_id=1, source_target_pairs={{0,4},{4,0},{8,12},{12,8},{16,20},{20,16},{24,28},{28,24},{1,5},{5... | collective-permute-start | bytes 294920 | tf_op jit(solution)/shard_map/ppermute | solution.py:529
  10.0 8.2 %collective-permute-start.3 = (f32[6,32,128]{2,1,0:T(8,128)S(1)}, f32[6,32,128]{2,1,0:T(8,128)S(1)}, u32[]{:S(2)}, u32[]{:S(2)}) collective-permute-start(f32[6,32,128]{2,1,0:T(8,128)S(1)} %get-tuple-element.34.refs_1_.refs_2_), channel_id=1, source_target_pairs={{0,28},{4,8},{8,4},{12,16},{16,12},{20,24},{24,20},{28,0},{1,29},{... | collective-permute-start | bytes 294920 | tf_op jit(solution)/shard_map/ppermute | solution.py:528
  19.4 5.9 %collective-permute-start.6 = (f32[3,32,128]{2,1,0:T(8,128)S(1)}, f32[3,32,128]{2,1,0:T(8,128)S(1)}, u32[]{:S(2)}, u32[]{:S(2)}) collective-permute-start(f32[3,32,128]{2,1,0:T(8,128)S(1)} %get-tuple-element.41.refs_2_.refs_3_.refs_5_), channel_id=1, source_target_pairs={{0,4},{4,0},{8,12},{12,8},{16,20},{20,16},{24,28},{28,24},{1,5},{5... | collective-permute-start | bytes 147464 | tf_op jit(solution)/shard_map/ppermute | solution.py:529
  19.5 7.3 %collective-permute-start.5 = (f32[3,32,128]{2,1,0:T(8,128)S(1)}, f32[3,32,128]{2,1,0:T(8,128)S(1)}, u32[]{:S(2)}, u32[]{:S(2)}) collective-permute-start(f32[3,32,128]{2,1,0:T(8,128)S(1)} %get-tuple-element.41.refs_2_.refs_3_.refs_5_), channel_id=1, source_target_pairs={{0,28},{4,8},{8,4},{12,16},{16,12},{20,24},{24,20},{28,0},{1,29},{... | collective-permute-start | bytes 147464 | tf_op jit(solution)/shard_map/ppermute | solution.py:528
  22.6 3.3 %collective-permute-start.7 = (f32[7,8,128]{2,1,0:T(8,128)S(1)}, f32[7,8,128]{2,1,0:T(8,128)S(1)}, u32[]{:S(2)}, u32[]{:S(2)}) collective-permute-start(f32[7,8,128]{2,1,0:T(8,128)S(1)} %get-tuple-element.47), channel_id=1, source_target_pairs={{0,1},{1,0},{2,3},{3,2},{4,5},{5,4},{6,7},{7,6},{8,9},{9,8},{10,11... | collective-permute-start | bytes 86024 | tf_op jit(solution)/shard_map/ppermute | solution.py:493
  22.6 3.9 %collective-permute-start.8 = (f32[7,8,128]{2,1,0:T(8,128)S(1)}, f32[7,8,128]{2,1,0:T(8,128)S(1)}, u32[]{:S(2)}, u32[]{:S(2)}) collective-permute-start(f32[7,8,128]{2,1,0:T(8,128)S(1)} %get-tuple-element.48), channel_id=1, source_target_pairs={{0,2},{1,3},{2,0},{3,1},{4,6},{5,7},{6,4},{7,5},{8,10},{9,11},{10,... | collective-permute-start | bytes 86024 | tf_op jit(solution)/shard_map/ppermute | solution.py:493
  23.6 3.3 %collective-permute-start.9 = (f32[7,8,128]{2,1,0:T(8,128)S(1)}, f32[7,8,128]{2,1,0:T(8,128)S(1)}, u32[]{:S(2)}, u32[]{:S(2)}) collective-permute-start(f32[7,8,128]{2,1,0:T(8,128)S(1)} %get-tuple-element.49), channel_id=1, source_target_pairs={{0,3},{1,2},{2,1},{3,0},{4,7},{5,6},{6,5},{7,4},{8,11},{9,10},{10,... | collective-permute-start | bytes 86024 | tf_op jit(solution)/shard_map/ppermute | solution.py:493

commit v5 on v4

--- a/solution.py
+++ b/solution.py
@@ -16,7 +16,9 @@
 CENTRE = 1.0
 AWAY = 1.0e4
 LANES = 128
-GROUPS = (24, 16, 8)
+LARGE_GROUPS = (((48, 40), (24, 16)), 16, 8)
+GROUPS = (((24, 16),), 16, 8)
+STEP = 8
 EARLY = 1
 CORE = 9
 DEPTH = 32
@@ -105,11 +107,11 @@
         self.slots, self.width = slots, width
         self.entry_bits = (width - 1).bit_length()
         self.cand_bits = slots.bit_length()
-        self.length = slots * width + GROUPS[0]
+        self.length = slots * width + STEP
         self.codes = (slots + 1) << self.entry_bits
         self.counts = 3 * self.length
         self.size = 3 * self.length + 8
-        self.stored = slots * width + 3 * GROUPS[-1]
+        self.stored = slots * width + 4 * STEP
         self.dummy = self.word(slots, 0, slots)
 
     def word(self, slot, entry, cand):
@@ -125,36 +127,36 @@
         return word & ((1 << self.cand_bits) - 1)
 
     def stored_base(self, ref, which):
-        step = GROUPS[-1]
         base = 0
         for k in range(which):
-            base = base + lax.div(ref[self.counts + k] + step - 1, step) * step
+            base = base + lax.div(ref[self.counts + k] + STEP - 1, STEP) * STEP
         return base
 
 
-def in_groups(plan, plan_ref, which, work):
-    count = plan_ref[plan.counts + which]
-    large, medium, small = GROUPS
-    full = lax.div(count + large - 1 - medium, large)
-
-    def step(g, carry):
-        work(g * large, large)
-        return carry
-
-    lax.fori_loop(0, full, step, 0)
-    rest = count - full * large
-
-    @pl.when(rest > small)
+def in_groups(plan, plan_ref, which, groups, work):
+    loops, medium, small = groups
+    start, count = 0, plan_ref[plan.counts + which]
+    for size, left in loops:
+
+        def step(g, first, size=size):
+            work(first, size)
+            return first + size
+
+        number = lax.div(jnp.maximum(count - start - left + size - 1, 0), size)
+        start = lax.fori_loop(0, number, step, start)
+
+    @pl.when(count - start > small)
     def _():
-        work(full * large, medium)
-
-    @pl.when((rest > 0) & (rest <= small))
+        work(start, medium)
+
+    @pl.when((count > start) & (count - start <= small))
     def _():
-        work(full * large, small)
-
-
-def plan_kernel(plan, neighbours_ref, counts_ref, after_ref, plan_ref):
+        work(start, small)
+
+
+def plan_kernel(plan, neighbours_ref, counts_ref, after_ref, plan_ref, near_ref, weight_ref):
     slots = plan.slots
+    entries = 1 << plan.entry_bits
     upper_first = lax.rem(lax.axis_index("slab"), 2) == 0
     low = jnp.where(upper_first, 2, 1)
     high = 3 - low
@@ -171,18 +173,26 @@
                 plan_ref[w * plan.length + totals[w]] = word
                 kept.append(totals[w] + ((k < used) & (which == w)).astype(I32))
             totals = tuple(kept)
+        rows = pl.ds(pl.multiple_of(i * (2 * DEPTH), 2 * DEPTH), 2 * DEPTH)
+        near_ref[rows, :] = jnp.zeros((2 * DEPTH, LANES), F32)
+        weight_ref[pl.ds(i * entries, entries)] = jnp.zeros((entries, 8, LANES), F32)
         return totals
 
     totals = lax.fori_loop(0, slots, fill, (jnp.int32(0),) * 3, unroll=4)
     for w in range(3):
-        for k in range(GROUPS[0]):
+        for k in range(STEP):
             plan_ref[w * plan.length + totals[w] + k] = plan.dummy
         plan_ref[plan.counts + w] = totals[w]
 
 
 def pack_kernel(tiles, cap, floats, dest_ref, particles_ref, *refs):
     cores, rests, (packed, staged, dest, sems) = refs[:tiles], refs[tiles : 2 * tiles], refs[2 * tiles :]
-    bring = [pltpu.make_async_copy(dest_ref, dest, sems.at[0]), pltpu.make_async_copy(particles_ref, staged, sems.at[1])]
+    pieces = sems.shape[0] - 1
+    bins = staged.shape[0] // pieces
+    bring = [pltpu.make_async_copy(dest_ref, dest, sems.at[pieces])]
+    for p in range(pieces):
+        part = pl.ds(p * bins, bins)
+        bring.append(pltpu.make_async_copy(particles_ref.at[part], staged.at[part], sems.at[p]))
     for copy in bring:
         copy.start()
     packed[...] = jnp.zeros_like(packed)
@@ -267,7 +277,6 @@
 
 
 def store_near(near_ref, moving_ref, slots):
-    near_ref[...] = jnp.zeros_like(near_ref)
     row = lax.broadcasted_iota(I32, (DEPTH, LANES), 0)
     start = 2 * slots * DEPTH
     near_ref[start : start + DEPTH, :] = jnp.where((row >= 15) & (row < 18), 1.0, 0.0)
@@ -298,7 +307,7 @@
         put(27 + row, value, 1)
 
 
-def pair_loop(plan, plan_ref, which, near_ref, far_ref, weight_ref, slope_ref):
+def pair_loop(plan, plan_ref, which, groups, near_ref, far_ref, weight_ref, slope_ref):
     base = which * plan.length
     stored = plan.stored_base(plan_ref, which)
 
@@ -320,29 +329,28 @@
             weight_ref[plan.code(word)] = jnp.sum(weight.reshape(LANES // 8, 8, LANES), axis=0)
             slope_ref[stored + start + u] = cubed * (inverse * inverse)
 
-    in_groups(plan, plan_ref, which, work)
-
-
-def local_kernel(plan, plan_ref, moving_ref, near_ref, weight_ref, slope_ref, far_ref):
+    in_groups(plan, plan_ref, which, groups, work)
+
+
+def local_kernel(plan, plan_ref, moving_ref, near_in_ref, weight_in_ref, near_ref, weight_ref, slope_ref, far_ref):
     slots = plan.slots
     store_near(near_ref, moving_ref, slots)
     store_far(far_ref, 0, moving_ref, slots)
     store_far_dummy(far_ref, slots)
-    weight_ref[...] = jnp.zeros_like(weight_ref)
-    pair_loop(plan, plan_ref, 0, near_ref, far_ref, weight_ref, slope_ref)
+    pair_loop(plan, plan_ref, 0, LARGE_GROUPS, near_ref, far_ref, weight_ref, slope_ref)
 
 
 def first_kernel(plan, plan_ref, moving_ref, near_ref, weight_in_ref, slope_in_ref, weight_ref, slope_ref, far_ref):
     store_far(far_ref, 0, moving_ref, plan.slots)
     store_far_dummy(far_ref, plan.slots)
-    pair_loop(plan, plan_ref, 1, near_ref, far_ref, weight_ref, slope_ref)
+    pair_loop(plan, plan_ref, 1, GROUPS, near_ref, far_ref, weight_ref, slope_ref)
 
 
 def second_kernel(plan, plan_ref, own_ref, moving_ref, near_ref, weight_in_ref, slope_in_ref,
                   density_ref, thermal_ref, weight_ref, slope_ref, far_ref):
     store_far(far_ref, 0, moving_ref, plan.slots)
     store_far_dummy(far_ref, plan.slots)
-    pair_loop(plan, plan_ref, 2, near_ref, far_ref, weight_ref, slope_ref)
+    pair_loop(plan, plan_ref, 2, GROUPS, near_ref, far_ref, weight_ref, slope_ref)
     for i in range(plan.slots):
         first = i << plan.entry_bits
         tile = weight_ref[first]
@@ -401,7 +409,7 @@
             sum_ref[code, 0:8, :] = both[0:8] + both[8:16] + both[16:24]
             sum_ref[code, 8:16, :] = both[24:32] + both[32:40]
 
-    in_groups(plan, plan_ref, which, work)
+    in_groups(plan, plan_ref, which, GROUPS, work)
 
 
 def hold_kernel(*refs):
@@ -482,7 +490,7 @@
             pltpu.VMEM((slots * floats, lanes), F32),
             pltpu.VMEM((bins, floats, lanes), F32),
             pltpu.SMEM((bins,), I32),
-            pltpu.SemaphoreType.DMA((2,)),
+            pltpu.SemaphoreType.DMA((9 if bins % 8 == 0 else 2,)),
         ],
         1500,
         "pack",
@@ -492,10 +500,12 @@
     def to_partner(array, step):
         return lax.ppermute(array, "tile", [(t, partner_tile(t, step, tiles)) for t in range(tiles)])
 
-    (lists,) = kernel_call(
+    near_out = ("v", ((slots + 1) * 2 * DEPTH, lanes), F32)
+    weight_out = ("v", (plan.codes, 8, lanes), F32)
+    lists, near, weights = kernel_call(
         lambda *refs: plan_kernel(plan, *refs),
         [("s", in_hbm(neighbours.T)), ("s", in_hbm(counts)), ("a", packed[0])],
-        [("s", (plan.size,), I32)],
+        [("s", (plan.size,), I32), near_out, weight_out],
         [],
         2000,
         "plan",
@@ -530,18 +540,18 @@
         return first, second
 
     first, second = both_sides(moving)
-    weight_out = ("v", (plan.codes, 8, lanes), F32)
     slope_out = ("v", (plan.stored, lanes, lanes), F32)
     sum_out = ("v", (plan.codes, 16, lanes), F32)
     far_table = [pltpu.VMEM(((slots + 1) * DEPTH, lanes), F32)]
     field_table = [pltpu.VMEM(((slots + 1) * FIELD_ROWS, lanes), F32)]
     near, weights, slopes = kernel_call(
         lambda *refs: local_kernel(plan, *refs),
-        [("s", lists), ("v", moving)],
-        [("v", ((slots + 1) * 2 * DEPTH, lanes), F32), weight_out, slope_out],
+        [("s", lists), ("v", moving), ("v", near), ("v", weights)],
+        [near_out, weight_out, slope_out],
         far_table,
         3500,
         "local",
+        {2: 0, 3: 1},
     )
     weights, slopes = kernel_call(
         lambda *refs: first_kernel(plan, *refs),

time: 28.2 us -> 28.4 us (level); the launches traced: 28.3 us -> 28.1 us
  Pallas kernels: 12.1 us -> 11.4 us
  starting transfers between devices: 13.3 us -> 13.6 us
    pallas_call x11, Pallas kernels: 12.1 us -> 11.4 us  [kernel_call(): pl.pallas_call(kernel, out_shape=[pltpu.SMEM(shape, dtype) if memory == '...]
    ppermute x2, starting transfers between devices: 1.65 us -> 2.24 us  [both_sides(): first = lax.ppermute(array, 'slab', first_pairs)]
    ppermute x2, starting transfers between devices: 6.61 us -> 6.3 us  [both_sides(): second = lax.ppermute(array, 'slab', second_pairs)]
  transfers between devices with their start and end apart: 10 -> 10, of which waited for: 3 -> 3; matrix products, arithmetic and copies ran while one was open for 0% -> 0% of each run, Pallas kernels for 29% -> 27%
where the time goes in v5:
time: 28.4 us; the launch traced here: 28.1 us
  starting transfers between devices  13.6 us (48%)
  Pallas kernels  11.4 us (40%)
  waiting for transfers between devices  2.35 us (8%)
  between operations  0.74 us (3%)
    pallas_call x11, Pallas kernels, kernel_call(): pl.pallas_call(kernel, out_shape=[pltpu.SMEM(shape, dtype) if memory == '...  11.4 us
    ppermute x2, starting transfers between devices, both_sides(): second = lax.ppermute(array, 'slab', second_pairs)  6.3 us
    ppermute x6, starting transfers between devices, to_partner(): lax.ppermute(array, 'tile', [(t, partner_tile(t, step, tiles)) for t in r...  5.09 us
    ppermute x6, waiting for transfers between devices, to_partner(): lax.ppermute(array, 'tile', [(t, partner_tile(t, step, tiles)) for t in r...  2.34 us
    ppermute x2, starting transfers between devices, both_sides(): first = lax.ppermute(array, 'slab', first_pairs)  2.24 us
  transfers between devices with their start and end apart: 10, of which 3 were waited for; matrix products, arithmetic and copies ran while one was open for 0% of the time, Pallas kernels for 27%

profile of v5, /device:TPU:0, one launch (start us, length us, event | category | flops | bytes accessed | tf_op | source)
XLA Modules:
  0.0 28.1 jit_solution(11735809442196537880)
XLA Ops:
  0.6 1.2 %pack.1 = (f32[9,8,128]{2,1,0:T(8,128)S(1)}, f32[9,8,128]{2,1,0:T(8,128)S(1)}, f32[9,8,128]{2,1,0:T(8,128)S(1)}, f32[9,8,128]{2,1,0:T(8,128)S(1)}, f32[7,8,128]{...) custom-call(s32[32]{0:T(128)} %refs_0_.1, f32[32,16,128]{2,1,0:T(8,128)} %refs_1_.2), custom_call_target="tpu_custom_call" | custom-call | bytes 4500000 | tf_op jit(solution)/shard_map/pack/pallas_call | solution.py:56
  1.8 3.0 %collective-permute-start.1 = (f32[9,8,128]{2,1,0:T(8,128)S(1)}, f32[9,8,128]{2,1,0:T(8,128)S(1)}, u32[]{:S(2)}, u32[]{:S(2)}) collective-permute-start(f32[9,8,128]{2,1,0:T(8,128)S(1)} %get-tuple-element.33), channel_id=1, source_target_pairs={{0,2},{1,3},{2,0},{3,1},{4,6},{5,7},{6,4},{7,5},{8,10},{9,11},{10,... | collective-permute-start | bytes 110600 | tf_op jit(solution)/shard_map/ppermute | solution.py:501
  4.8 0.0 collective-permute-start.2
  4.8 0.2 collective-permute-start
  5.0 2.2 %plan.1 = (s32[416]{0:T(512)S(4)}, f32[2112,128]{1,0:T(8,128)S(1)}, f32[132,8,128]{2,1,0:T(8,128)S(1)}) custom-call(s32[4,32]{1,0:T(4,128)} %bitcast.3, s32[32]{0:T(128)} %refs_1_.3, f32[9,8,128]{2,1,0:T(8,128)S(1)} %get-tuple-element.30.refs_2_.refs_0_), custom_call_target="tpu_custom_call" | custom-call | bytes 6000000 | tf_op jit(solution)/shard_map/plan/pallas_call | solution.py:56
  7.2 0.0 collective-permute-done.1.refs_1_
  7.3 1.1 %collective-permute-done.2.refs_2_ = f32[9,8,128]{2,1,0:T(8,128)S(1)} collective-permute-done((f32[9,8,128]{2,1,0:T(8,128)S(1)}, f32[9,8,128]{2,1,0:T(8,128)S(1)}, u32[]{:S(2)}, u32[]{:S(2)}) %collective-permute-start.2) | collective-permute-done | bytes 36896 | tf_op jit(solution)/shard_map/ppermute | solution.py:501
  8.4 0.0 collective-permute-done.refs_0_
  8.4 1.6 %collective-permute-start.4 = (f32[6,32,128]{2,1,0:T(8,128)S(1)}, f32[6,32,128]{2,1,0:T(8,128)S(1)}, u32[]{:S(2)}, u32[]{:S(2)}) collective-permute-start(f32[6,32,128]{2,1,0:T(8,128)S(1)} %get-tuple-element.38.refs_1_.refs_2_), channel_id=1, source_target_pairs={{0,4},{4,0},{8,12},{12,8},{16,20},{20,16},{24,28},{28,24},{1,5},{5... | collective-permute-start | bytes 294920 | tf_op jit(solution)/shard_map/ppermute | solution.py:539
  10.0 3.6 %collective-permute-start.3 = (f32[6,32,128]{2,1,0:T(8,128)S(1)}, f32[6,32,128]{2,1,0:T(8,128)S(1)}, u32[]{:S(2)}, u32[]{:S(2)}) collective-permute-start(f32[6,32,128]{2,1,0:T(8,128)S(1)} %get-tuple-element.38.refs_1_.refs_2_), channel_id=1, source_target_pairs={{0,28},{4,8},{8,4},{12,16},{16,12},{20,24},{24,20},{28,0},{1,29},{... | collective-permute-start | bytes 294920 | tf_op jit(solution)/shard_map/ppermute | solution.py:538
  13.6 2.8 %local.1 = (f32[2112,128]{1,0:T(8,128)S(1)}, f32[132,8,128]{2,1,0:T(8,128)S(1)}, f32[160,128,128]{2,1,0:T(8,128)S(1)}) custom-call(s32[416]{0:T(512)S(4)} %get-tuple-element.31.refs_3_.refs_0_, f32[6,32,128]{2,1,0:T(8,128)S(1)} %get-tuple-element.38.refs_1_.refs_2_, ...), custom_call_target="tpu_custom_call", output_to_operand_aliasing={{0}: (2, {}), {1}: (3, {})} | custom-call | bytes 10500000 | tf_op jit(solution)/shard_map/local/pallas_call | solution.py:56
  16.4 0.0 collective-permute-done.4.refs_1_
  16.4 1.2 %first.1 = (f32[132,8,128]{2,1,0:T(8,128)S(1)}, f32[160,128,128]{2,1,0:T(8,128)S(1)}) custom-call(s32[416]{0:T(512)S(4)} %get-tuple-element.31.refs_3_.refs_0_, f32[6,32,128]{2,1,0:T(8,128)S(1)} %collective-permute-done.4.refs_1_, f32[2112,128]{1,0:T(8,128)S(1)} %get-tuple-element.41.refs_2_.refs_3_, ...), custom_call_target="tpu_custom_call", output_to_operand_aliasing={{0}: (3, {}), {1}: (4, {})} | custom-call | bytes 4500000 | tf_op jit(solution)/shard_map/first/pallas_call | solution.py:56
  17.6 0.0 collective-permute-done.3.refs_2_.refs_3_
  17.6 1.2 %second.1 = (f32[32,128]{1,0:T(8,128)S(1)}, f32[3,32,128]{2,1,0:T(8,128)S(1)}, f32[132,8,128]{2,1,0:T(8,128)S(1)}, f32[160,128,128]{2,1,0:T(8,128)S(1)}) custom-call(s32[416]{0:T(512)S(4)} %get-tuple-element.31.refs_3_.refs_0_, f32[9,32,128]{2,1,0:T(8,128)S(1)} %get-tuple-element.37.refs_1_, ...), custom_call_target="tpu_custom_call", output_to_operand_aliasing={{2}: (4, {}), {3}: (5, {})} | custom-call | bytes 6000000 | tf_op jit(solution)/shard_map/second/pallas_call | solution.py:56
  18.8 0.7 %collective-permute-start.6 = (f32[3,32,128]{2,1,0:T(8,128)S(1)}, f32[3,32,128]{2,1,0:T(8,128)S(1)}, u32[]{:S(2)}, u32[]{:S(2)}) collective-permute-start(f32[3,32,128]{2,1,0:T(8,128)S(1)} %get-tuple-element.47.refs_2_.refs_3_.refs_5_), channel_id=1, source_target_pairs={{0,4},{4,0},{8,12},{12,8},{16,20},{20,16},{24,28},{28,24},{1,5},{5... | collective-permute-start | bytes 147464 | tf_op jit(solution)/shard_map/ppermute | solution.py:539
  19.5 2.7 %collective-permute-start.5 = (f32[3,32,128]{2,1,0:T(8,128)S(1)}, f32[3,32,128]{2,1,0:T(8,128)S(1)}, u32[]{:S(2)}, u32[]{:S(2)}) collective-permute-start(f32[3,32,128]{2,1,0:T(8,128)S(1)} %get-tuple-element.47.refs_2_.refs_3_.refs_5_), channel_id=1, source_target_pairs={{0,28},{4,8},{8,4},{12,16},{16,12},{20,24},{24,20},{28,0},{1,29},{... | collective-permute-start | bytes 147464 | tf_op jit(solution)/shard_map/ppermute | solution.py:538
  22.2 0.0 collective-permute-start.7
  22.3 1.2 %collective-permute-start.8 = (f32[7,8,128]{2,1,0:T(8,128)S(1)}, f32[7,8,128]{2,1,0:T(8,128)S(1)}, u32[]{:S(2)}, u32[]{:S(2)}) collective-permute-start(f32[7,8,128]{2,1,0:T(8,128)S(1)} %get-tuple-element.54), channel_id=1, source_target_pairs={{0,2},{1,3},{2,0},{3,1},{4,6},{5,7},{6,4},{7,5},{8,10},{9,11},{10,... | collective-permute-start | bytes 86024 | tf_op jit(solution)/shard_map/ppermute | solution.py:501
  23.4 0.7 %collective-permute-start.9 = (f32[7,8,128]{2,1,0:T(8,128)S(1)}, f32[7,8,128]{2,1,0:T(8,128)S(1)}, u32[]{:S(2)}, u32[]{:S(2)}) collective-permute-start(f32[7,8,128]{2,1,0:T(8,128)S(1)} %get-tuple-element.55), channel_id=1, source_target_pairs={{0,3},{1,2},{2,1},{3,0},{4,7},{5,6},{6,5},{7,4},{8,11},{9,10},{10,... | collective-permute-start | bytes 86024 | tf_op jit(solution)/shard_map/ppermute | solution.py:501
  24.1 0.9 %local_fields.1.refs_4_ = f32[132,16,128]{2,1,0:T(8,128)S(1)} custom-call(s32[416]{0:T(512)S(4)} %get-tuple-element.31.refs_3_.refs_0_, f32[6,32,128]{2,1,0:T(8,128)S(1)} %get-tuple-element.38.refs_1_.refs_2_, f32[3,32,128]{2,1,0:T(8,128)S(1)} %get-tuple-element.47.refs_2_.refs_3_.refs_5_, f32[160,128,128]{2,1,0:T(8,128)S(1)} %get-tuple-element.48.refs_3_.refs_7_), custom_call_target="tpu_custom_call" | custom-call | bytes 5100000 | tf_op jit(solution)/shard_map/local_fields/pallas_call | solution.py:56
  25.0 0.0 collective-permute-done.6.refs_2_
  25.0 0.4 %first_fields.1.refs_8_ = f32[132,16,128]{2,1,0:T(8,128)S(1)} custom-call(s32[416]{0:T(512)S(4)} %get-tuple-element.31.refs_3_.refs_0_, f32[6,32,128]{2,1,0:T(8,128)S(1)} %collective-permute-done.4.refs_1_, f32[3,32,128]{2,1,0:T(8,128)S(1)} %collective-permute-done.6.refs_2_, ...), custom_call_target="tpu_custom_call", output_to_operand_aliasing={{}: (4, {})} | custom-call | bytes 3000000 | tf_op jit(solution)/shard_map/first_fields/pallas_call | solution.py:56
  25.5 0.0 collective-permute-done.7.refs_10_
  25.5 0.6 %collective-permute-done.8.refs_11_ = f32[7,8,128]{2,1,0:T(8,128)S(1)} collective-permute-done((f32[7,8,128]{2,1,0:T(8,128)S(1)}, f32[7,8,128]{2,1,0:T(8,128)S(1)}, u32[]{:S(2)}, u32[]{:S(2)}) %collective-permute-start.8) | collective-permute-done | bytes 28704 | tf_op jit(solution)/shard_map/ppermute | solution.py:501
  26.1 0.6 %collective-permute-done.9.refs_12_ = f32[7,8,128]{2,1,0:T(8,128)S(1)} collective-permute-done((f32[7,8,128]{2,1,0:T(8,128)S(1)}, f32[7,8,128]{2,1,0:T(8,128)S(1)}, u32[]{:S(2)}, u32[]{:S(2)}) %collective-permute-start.9) | collective-permute-done | bytes 28704 | tf_op jit(solution)/shard_map/ppermute | solution.py:501
  26.7 0.0 collective-permute-done.5.refs_6_
  26.7 1.4 %final.1 = (f32[512,128]{1,0:T(8,128)}, f32[5,32,128]{2,1,0:T(8,128)}, f32[132,16,128]{2,1,0:T(8,128)S(1)}) custom-call(s32[416]{0:T(512)S(4)} %get-tuple-element.31.refs_3_.refs_0_, f32[9,32,128]{2,1,0:T(8,128)S(1)} %get-tuple-element.37.refs_1_, f32[6,32,128]{2,1,0:T(8,128)S(1)} %get-tuple-element.38.refs_1_.refs_2_, ...), custom_call_target="tpu_custom_call", output_to_operand_aliasing={{2}: (8, {})} | custom-call | bytes 6000000 | tf_op jit(solution)/shard_map/final/pallas_call | solution.py:56
  (3 shorter events, 0.1 us)
Async XLA Ops:
  1.8 5.5 %collective-permute-start.1 = (f32[9,8,128]{2,1,0:T(8,128)S(1)}, f32[9,8,128]{2,1,0:T(8,128)S(1)}, u32[]{:S(2)}, u32[]{:S(2)}) collective-permute-start(f32[9,8,128]{2,1,0:T(8,128)S(1)} %get-tuple-element.33), channel_id=1, source_target_pairs={{0,2},{1,3},{2,0},{3,1},{4,6},{5,7},{6,4},{7,5},{8,10},{9,11},{10,... | collective-permute-start | bytes 110600 | tf_op jit(solution)/shard_map/ppermute | solution.py:501
  4.8 3.5 %collective-permute-start.2 = (f32[9,8,128]{2,1,0:T(8,128)S(1)}, f32[9,8,128]{2,1,0:T(8,128)S(1)}, u32[]{:S(2)}, u32[]{:S(2)}) collective-permute-start(f32[9,8,128]{2,1,0:T(8,128)S(1)} %get-tuple-element.34), channel_id=1, source_target_pairs={{0,3},{1,2},{2,1},{3,0},{4,7},{5,6},{6,5},{7,4},{8,11},{9,10},{10,... | collective-permute-start | bytes 110600 | tf_op jit(solution)/shard_map/ppermute | solution.py:501
  4.8 3.6 %collective-permute-start = (f32[9,8,128]{2,1,0:T(8,128)S(1)}, f32[9,8,128]{2,1,0:T(8,128)S(1)}, u32[]{:S(2)}, u32[]{:S(2)}) collective-permute-start(f32[9,8,128]{2,1,0:T(8,128)S(1)} %get-tuple-element.32), channel_id=1, source_target_pairs={{0,1},{1,0},{2,3},{3,2},{4,5},{5,4},{6,7},{7,6},{8,9},{9,8},{10,11... | collective-permute-start | bytes 110600 | tf_op jit(solution)/shard_map/ppermute | solution.py:501
  8.4 8.0 %collective-permute-start.4 = (f32[6,32,128]{2,1,0:T(8,128)S(1)}, f32[6,32,128]{2,1,0:T(8,128)S(1)}, u32[]{:S(2)}, u32[]{:S(2)}) collective-permute-start(f32[6,32,128]{2,1,0:T(8,128)S(1)} %get-tuple-element.38.refs_1_.refs_2_), channel_id=1, source_target_pairs={{0,4},{4,0},{8,12},{12,8},{16,20},{20,16},{24,28},{28,24},{1,5},{5... | collective-permute-start | bytes 294920 | tf_op jit(solution)/shard_map/ppermute | solution.py:539
  10.0 7.6 %collective-permute-start.3 = (f32[6,32,128]{2,1,0:T(8,128)S(1)}, f32[6,32,128]{2,1,0:T(8,128)S(1)}, u32[]{:S(2)}, u32[]{:S(2)}) collective-permute-start(f32[6,32,128]{2,1,0:T(8,128)S(1)} %get-tuple-element.38.refs_1_.refs_2_), channel_id=1, source_target_pairs={{0,28},{4,8},{8,4},{12,16},{16,12},{20,24},{24,20},{28,0},{1,29},{... | collective-permute-start | bytes 294920 | tf_op jit(solution)/shard_map/ppermute | solution.py:538
  18.8 6.2 %collective-permute-start.6 = (f32[3,32,128]{2,1,0:T(8,128)S(1)}, f32[3,32,128]{2,1,0:T(8,128)S(1)}, u32[]{:S(2)}, u32[]{:S(2)}) collective-permute-start(f32[3,32,128]{2,1,0:T(8,128)S(1)} %get-tuple-element.47.refs_2_.refs_3_.refs_5_), channel_id=1, source_target_pairs={{0,4},{4,0},{8,12},{12,8},{16,20},{20,16},{24,28},{28,24},{1,5},{5... | collective-permute-start | bytes 147464 | tf_op jit(solution)/shard_map/ppermute | solution.py:539
  19.5 7.2 %collective-permute-start.5 = (f32[3,32,128]{2,1,0:T(8,128)S(1)}, f32[3,32,128]{2,1,0:T(8,128)S(1)}, u32[]{:S(2)}, u32[]{:S(2)}) collective-permute-start(f32[3,32,128]{2,1,0:T(8,128)S(1)} %get-tuple-element.47.refs_2_.refs_3_.refs_5_), channel_id=1, source_target_pairs={{0,28},{4,8},{8,4},{12,16},{16,12},{20,24},{24,20},{28,0},{1,29},{... | collective-permute-start | bytes 147464 | tf_op jit(solution)/shard_map/ppermute | solution.py:538
  22.2 3.2 %collective-permute-start.7 = (f32[7,8,128]{2,1,0:T(8,128)S(1)}, f32[7,8,128]{2,1,0:T(8,128)S(1)}, u32[]{:S(2)}, u32[]{:S(2)}) collective-permute-start(f32[7,8,128]{2,1,0:T(8,128)S(1)} %get-tuple-element.53), channel_id=1, source_target_pairs={{0,1},{1,0},{2,3},{3,2},{4,5},{5,4},{6,7},{7,6},{8,9},{9,8},{10,11... | collective-permute-start | bytes 86024 | tf_op jit(solution)/shard_map/ppermute | solution.py:501
  22.3 3.9 %collective-permute-start.8 = (f32[7,8,128]{2,1,0:T(8,128)S(1)}, f32[7,8,128]{2,1,0:T(8,128)S(1)}, u32[]{:S(2)}, u32[]{:S(2)}) collective-permute-start(f32[7,8,128]{2,1,0:T(8,128)S(1)} %get-tuple-element.54), channel_id=1, source_target_pairs={{0,2},{1,3},{2,0},{3,1},{4,6},{5,7},{6,4},{7,5},{8,10},{9,11},{10,... | collective-permute-start | bytes 86024 | tf_op jit(solution)/shard_map/ppermute | solution.py:501
  23.4 3.3 %collective-permute-start.9 = (f32[7,8,128]{2,1,0:T(8,128)S(1)}, f32[7,8,128]{2,1,0:T(8,128)S(1)}, u32[]{:S(2)}, u32[]{:S(2)}) collective-permute-start(f32[7,8,128]{2,1,0:T(8,128)S(1)} %get-tuple-element.55), channel_id=1, source_target_pairs={{0,3},{1,2},{2,1},{3,0},{4,7},{5,6},{6,5},{7,4},{8,11},{9,10},{10,... | collective-permute-start | bytes 86024 | tf_op jit(solution)/shard_map/ppermute | solution.py:501

commit v6 on v5

--- a/solution.py
+++ b/solution.py
@@ -16,8 +16,8 @@
 CENTRE = 1.0
 AWAY = 1.0e4
 LANES = 128
-LARGE_GROUPS = (((48, 40), (24, 16)), 16, 8)
-GROUPS = (((24, 16),), 16, 8)
+LARGE_GROUPS = (((48, 40), (24, 16)), (16, 8))
+GROUPS = (((24, 16),), (16, 8))
 STEP = 8
 EARLY = 1
 CORE = 9
@@ -134,7 +134,7 @@
 
 
 def in_groups(plan, plan_ref, which, groups, work):
-    loops, medium, small = groups
+    loops, tails = groups
     start, count = 0, plan_ref[plan.counts + which]
     for size, left in loops:
 
@@ -144,17 +144,15 @@
 
         number = lax.div(jnp.maximum(count - start - left + size - 1, 0), size)
         start = lax.fori_loop(0, number, step, start)
-
-    @pl.when(count - start > small)
-    def _():
-        work(start, medium)
-
-    @pl.when((count > start) & (count - start <= small))
-    def _():
-        work(start, small)
-
-
-def plan_kernel(plan, neighbours_ref, counts_ref, after_ref, plan_ref, near_ref, weight_ref):
+    rest = count - start
+    for size, below in zip(tails, tails[1:] + (0,)):
+
+        @pl.when((rest <= size) & (rest > below))
+        def _(size=size):
+            work(start, size)
+
+
+def plan_kernel(plan, neighbours_ref, counts_ref, after_ref, plan_ref, weight_ref):
     slots = plan.slots
     entries = 1 << plan.entry_bits
     upper_first = lax.rem(lax.axis_index("slab"), 2) == 0
@@ -173,8 +171,6 @@
                 plan_ref[w * plan.length + totals[w]] = word
                 kept.append(totals[w] + ((k < used) & (which == w)).astype(I32))
             totals = tuple(kept)
-        rows = pl.ds(pl.multiple_of(i * (2 * DEPTH), 2 * DEPTH), 2 * DEPTH)
-        near_ref[rows, :] = jnp.zeros((2 * DEPTH, LANES), F32)
         weight_ref[pl.ds(i * entries, entries)] = jnp.zeros((entries, 8, LANES), F32)
         return totals
 
@@ -240,35 +236,30 @@
             moving_ref[5 + f, rows, :] = field[3 + f]
 
 
-def store_far(far_ref, base, moving_ref, slots):
-    def put(row, value):
-        far_ref[pl.ds(base * DEPTH + row, slots, stride=DEPTH), :] = value
-
+def slot_major(rows):
+    slots, lanes = rows[0].shape
+    return jnp.swapaxes(jnp.stack(rows, axis=0), 0, 1).reshape(slots * len(rows), lanes)
+
+
+def store_far(far_ref, moving_ref, slots):
     place = [moving_ref[f] for f in range(3)]
     smooth, stretch = moving_ref[3], moving_ref[4]
     present = stretch > 0
     stretch = jnp.where(present, stretch, 1.0)
     square = stretch * stretch
     norm = 0.0
+    rows = [None] * DEPTH
     for f in range(3):
         hi, mid, lo = split3(-2.0 * square * place[f])
         norm = norm + place[f] * place[f]
-        put(f, hi)
-        put(3 + f, hi)
-        put(6 + f, hi)
-        put(9 + f, mid)
-        put(12 + f, lo)
-    for row, value in enumerate(split3(jnp.where(present, square * norm, AWAY))):
-        put(15 + row, value)
+        rows[f : 15 : 3] = [hi, hi, hi, mid, lo]
+    rows[15:18] = split3(jnp.where(present, square * norm, AWAY))
     s1, s2, s3 = split3(square)
-    for row, value in enumerate((s1, s1, s1, s2, s2, s3)):
-        put(18 + row, value)
-    for row, value in enumerate(split3(0.25 * stretch * smooth)):
-        put(24 + row, value)
+    rows[18:24] = [s1, s1, s1, s2, s2, s3]
+    rows[24:27] = split3(0.25 * stretch * smooth)
     u1, u2 = split2(0.25 * stretch)
-    for row, value in enumerate((u1, u1, u2, u2)):
-        put(27 + row, value)
-    put(31, jnp.zeros_like(stretch))
+    rows[27:32] = [u1, u1, u2, u2, jnp.zeros_like(u1)]
+    far_ref[0 : slots * DEPTH, :] = slot_major(rows)
 
 
 def store_far_dummy(far_ref, index):
@@ -281,30 +272,20 @@
     start = 2 * slots * DEPTH
     near_ref[start : start + DEPTH, :] = jnp.where((row >= 15) & (row < 18), 1.0, 0.0)
     near_ref[start + DEPTH : start + 2 * DEPTH, :] = jnp.where((row >= 24) & (row < 27), 1.0, 0.0)
-
-    def put(row, value, half=0):
-        near_ref[pl.ds(half * DEPTH + row, slots, stride=2 * DEPTH), :] = value
-
     place = [moving_ref[f] for f in range(3)]
+    zeros, ones = jnp.zeros_like(place[0]), jnp.ones_like(place[0])
     norm = 0.0
+    rows = [zeros] * (2 * DEPTH)
     for f in range(3):
         hi, mid, lo = split3(place[f])
         norm = norm + place[f] * place[f]
-        put(f, hi)
-        put(3 + f, mid)
-        put(6 + f, lo)
-        put(9 + f, hi)
-        put(12 + f, hi)
-    ones = jnp.ones_like(norm)
-    for row in range(3):
-        put(15 + row, ones)
-        put(24 + row, ones, 1)
+        rows[f : 15 : 3] = [hi, mid, lo, hi, hi]
+    rows[15:18] = [ones] * 3
     n1, n2, n3 = split3(norm)
-    for row, value in enumerate((n1, n2, n3, n1, n2, n1)):
-        put(18 + row, value)
+    rows[18:24] = [n1, n2, n3, n1, n2, n1]
     h1, h2 = split2(moving_ref[3])
-    for row, value in enumerate((h1, h2, h1, h2)):
-        put(27 + row, value, 1)
+    rows[DEPTH + 24 : DEPTH + 31] = [ones] * 3 + [h1, h2, h1, h2]
+    near_ref[0:start, :] = slot_major(rows)
 
 
 def pair_loop(plan, plan_ref, which, groups, near_ref, far_ref, weight_ref, slope_ref):
@@ -332,23 +313,23 @@
     in_groups(plan, plan_ref, which, groups, work)
 
 
-def local_kernel(plan, plan_ref, moving_ref, near_in_ref, weight_in_ref, near_ref, weight_ref, slope_ref, far_ref):
+def local_kernel(plan, plan_ref, moving_ref, weight_in_ref, near_ref, weight_ref, slope_ref, far_ref):
     slots = plan.slots
     store_near(near_ref, moving_ref, slots)
-    store_far(far_ref, 0, moving_ref, slots)
+    store_far(far_ref, moving_ref, slots)
     store_far_dummy(far_ref, slots)
     pair_loop(plan, plan_ref, 0, LARGE_GROUPS, near_ref, far_ref, weight_ref, slope_ref)
 
 
 def first_kernel(plan, plan_ref, moving_ref, near_ref, weight_in_ref, slope_in_ref, weight_ref, slope_ref, far_ref):
-    store_far(far_ref, 0, moving_ref, plan.slots)
+    store_far(far_ref, moving_ref, plan.slots)
     store_far_dummy(far_ref, plan.slots)
     pair_loop(plan, plan_ref, 1, GROUPS, near_ref, far_ref, weight_ref, slope_ref)
 
 
 def second_kernel(plan, plan_ref, own_ref, moving_ref, near_ref, weight_in_ref, slope_in_ref,
                   density_ref, thermal_ref, weight_ref, slope_ref, far_ref):
-    store_far(far_ref, 0, moving_ref, plan.slots)
+    store_far(far_ref, moving_ref, plan.slots)
     store_far_dummy(far_ref, plan.slots)
     pair_loop(plan, plan_ref, 2, GROUPS, near_ref, far_ref, weight_ref, slope_ref)
     for i in range(plan.slots):
@@ -365,9 +346,9 @@
         thermal_ref[1 + f - EARLY] = own_ref[3 + f]
 
 
-def store_fields(field_ref, base, moving_ref, thermal_ref, slots):
+def store_fields(field_ref, moving_ref, thermal_ref, slots):
     def put(row, value):
-        field_ref[pl.ds(base * FIELD_ROWS + row, slots, stride=FIELD_ROWS), :] = value
+        field_ref[pl.ds(row, slots, stride=FIELD_ROWS), :] = value
 
     stretch = moving_ref[4]
     square = stretch * stretch
@@ -412,19 +393,15 @@
     in_groups(plan, plan_ref, which, GROUPS, work)
 
 
-def hold_kernel(*refs):
-    pass
-
-
 def local_field_kernel(plan, plan_ref, moving_ref, thermal_ref, slope_ref, sum_ref, field_ref):
-    store_fields(field_ref, 0, moving_ref, thermal_ref, plan.slots)
+    store_fields(field_ref, moving_ref, thermal_ref, plan.slots)
     store_field_dummy(field_ref, plan.slots)
     sum_ref[...] = jnp.zeros_like(sum_ref)
     field_loop(plan, plan_ref, 0, field_ref, slope_ref, sum_ref)
 
 
 def first_field_kernel(plan, plan_ref, moving_ref, thermal_ref, slope_ref, sum_in_ref, sum_ref, field_ref):
-    store_fields(field_ref, 0, moving_ref, thermal_ref, plan.slots)
+    store_fields(field_ref, moving_ref, thermal_ref, plan.slots)
     store_field_dummy(field_ref, plan.slots)
     field_loop(plan, plan_ref, 1, field_ref, slope_ref, sum_ref)
 
@@ -433,7 +410,7 @@
                  second_thermal_ref, slope_ref, sum_in_ref, *refs):
     rests, (updated_ref, derived_ref, sum_ref, field_ref, total_ref) = refs[:tiles], refs[tiles:]
     slots = plan.slots
-    store_fields(field_ref, 0, second_ref, second_thermal_ref, slots)
+    store_fields(field_ref, second_ref, second_thermal_ref, slots)
     store_field_dummy(field_ref, slots)
     me = lax.axis_index("tile")
     for k in range(tiles):
@@ -502,10 +479,10 @@
 
     near_out = ("v", ((slots + 1) * 2 * DEPTH, lanes), F32)
     weight_out = ("v", (plan.codes, 8, lanes), F32)
-    lists, near, weights = kernel_call(
+    lists, weights = kernel_call(
         lambda *refs: plan_kernel(plan, *refs),
         [("s", in_hbm(neighbours.T)), ("s", in_hbm(counts)), ("a", packed[0])],
-        [("s", (plan.size,), I32), near_out, weight_out],
+        [("s", (plan.size,), I32), weight_out],
         [],
         2000,
         "plan",
@@ -546,12 +523,12 @@
     field_table = [pltpu.VMEM(((slots + 1) * FIELD_ROWS, lanes), F32)]
     near, weights, slopes = kernel_call(
         lambda *refs: local_kernel(plan, *refs),
-        [("s", lists), ("v", moving), ("v", near), ("v", weights)],
+        [("s", lists), ("v", moving), ("v", weights)],
         [near_out, weight_out, slope_out],
         far_table,
         3500,
         "local",
-        {2: 0, 3: 1},
+        {2: 1},
     )
     weights, slopes = kernel_call(
         lambda *refs: first_kernel(plan, *refs),
@@ -572,15 +549,7 @@
         {4: 2, 5: 3},
     )
     first_thermal, second_thermal = both_sides(thermal)
-    later = kernel_call(
-        hold_kernel,
-        [("a", rest) for rest in rests[1:]] + [("a", thermal)],
-        [("a", (floats - CORE, cap, lanes), F32)] * (tiles - 1),
-        [],
-        10,
-        "hold",
-        {k: k for k in range(tiles - 1)},
-    )
+    later = rests[1:]
     (sums,) = kernel_call(
         lambda *refs: local_field_kernel(plan, *refs),
         [("s", lists), ("v", moving), ("v", thermal), ("v", slopes)],

time: 28.4 us -> 28.2 us (level)
  starting transfers between devices: 13.6 us -> 13.9 us
    ppermute x2, starting transfers between devices: 6.3 us -> 7.16 us  [both_sides(): second = lax.ppermute(array, 'slab', second_pairs)]
    ppermute x2, starting transfers between devices: 2.24 us -> 1.69 us  [both_sides(): first = lax.ppermute(array, 'slab', first_pairs)]
    ppermute x6, waiting for transfers between devices: 2.34 us -> 1.96 us  [to_partner(): lax.ppermute(array, 'tile', [(t, partner_tile(t, step, tiles)) for t in r...]
    pallas_call x11 -> x10, Pallas kernels: 11.4 us -> 11.2 us  [kernel_call(): pl.pallas_call(kernel, out_shape=[pltpu.SMEM(shape, dtype) if memory == '...]
  transfers between devices with their start and end apart: 10 -> 10, of which waited for: 3 -> 3; matrix products, arithmetic and copies ran while one was open for 0% -> 0% of each run, Pallas kernels for 27% -> 26%
where the time goes in v6:
time: 28.2 us; the launch traced here: 28 us
  starting transfers between devices  13.9 us (49%)
  Pallas kernels  11.2 us (40%)
  waiting for transfers between devices  2.13 us (8%)
  between operations  0.73 us (3%)
    pallas_call x10, Pallas kernels, kernel_call(): pl.pallas_call(kernel, out_shape=[pltpu.SMEM(shape, dtype) if memory == '...  11.2 us
    ppermute x2, starting transfers between devices, both_sides(): second = lax.ppermute(array, 'slab', second_pairs)  7.16 us
    ppermute x6, starting transfers between devices, to_partner(): lax.ppermute(array, 'tile', [(t, partner_tile(t, step, tiles)) for t in r...  5.09 us
    ppermute x6, waiting for transfers between devices, to_partner(): lax.ppermute(array, 'tile', [(t, partner_tile(t, step, tiles)) for t in r...  1.96 us
    ppermute x2, starting transfers between devices, both_sides(): first = lax.ppermute(array, 'slab', first_pairs)  1.69 us
  transfers between devices with their start and end apart: 10, of which 3 were waited for; matrix products, arithmetic and copies ran while one was open for 0% of the time, Pallas kernels for 26%

profile of v6, /device:TPU:0, one launch (start us, length us, event | category | flops | bytes accessed | tf_op | source)
XLA Modules:
  0.0 28.0 jit_solution(17288424537677334594)
XLA Ops:
  0.6 1.2 %pack.1 = (f32[9,8,128]{2,1,0:T(8,128)S(1)}, f32[9,8,128]{2,1,0:T(8,128)S(1)}, f32[9,8,128]{2,1,0:T(8,128)S(1)}, f32[9,8,128]{2,1,0:T(8,128)S(1)}, f32[7,8,128]{...) custom-call(s32[32]{0:T(128)} %refs_0_.1, f32[32,16,128]{2,1,0:T(8,128)} %refs_1_.2), custom_call_target="tpu_custom_call" | custom-call | bytes 4500000 | tf_op jit(solution)/shard_map/pack/pallas_call | solution.py:56
  1.8 3.0 %collective-permute-start.1 = (f32[9,8,128]{2,1,0:T(8,128)S(1)}, f32[9,8,128]{2,1,0:T(8,128)S(1)}, u32[]{:S(2)}, u32[]{:S(2)}) collective-permute-start(f32[9,8,128]{2,1,0:T(8,128)S(1)} %get-tuple-element.29), channel_id=1, source_target_pairs={{0,2},{1,3},{2,0},{3,1},{4,6},{5,7},{6,4},{7,5},{8,10},{9,11},{10,... | collective-permute-start | bytes 110600 | tf_op jit(solution)/shard_map/ppermute | solution.py:478
  4.8 0.0 collective-permute-start.2
  4.8 0.2 collective-permute-start
  5.0 2.2 %plan.1 = (s32[416]{0:T(512)S(4)}, f32[132,8,128]{2,1,0:T(8,128)S(1)}) custom-call(s32[4,32]{1,0:T(4,128)} %bitcast.3, s32[32]{0:T(128)} %refs_1_.3, f32[9,8,128]{2,1,0:T(8,128)S(1)} %get-tuple-element.26.refs_2_.refs_0_), custom_call_target="tpu_custom_call" | custom-call | bytes 6000000 | tf_op jit(solution)/shard_map/plan/pallas_call | solution.py:56
  7.2 0.0 collective-permute-done.1.refs_1_
  7.2 1.1 %collective-permute-done.2.refs_2_ = f32[9,8,128]{2,1,0:T(8,128)S(1)} collective-permute-done((f32[9,8,128]{2,1,0:T(8,128)S(1)}, f32[9,8,128]{2,1,0:T(8,128)S(1)}, u32[]{:S(2)}, u32[]{:S(2)}) %collective-permute-start.2) | collective-permute-done | bytes 36896 | tf_op jit(solution)/shard_map/ppermute | solution.py:478
  8.4 0.0 collective-permute-done.refs_0_
  8.4 1.6 %collective-permute-start.4 = (f32[6,32,128]{2,1,0:T(8,128)S(1)}, f32[6,32,128]{2,1,0:T(8,128)S(1)}, u32[]{:S(2)}, u32[]{:S(2)}) collective-permute-start(f32[6,32,128]{2,1,0:T(8,128)S(1)} %get-tuple-element.34.refs_1_.refs_2_), channel_id=1, source_target_pairs={{0,4},{4,0},{8,12},{12,8},{16,20},{20,16},{24,28},{28,24},{1,5},{5... | collective-permute-start | bytes 294920 | tf_op jit(solution)/shard_map/ppermute | solution.py:516
  10.0 3.6 %collective-permute-start.3 = (f32[6,32,128]{2,1,0:T(8,128)S(1)}, f32[6,32,128]{2,1,0:T(8,128)S(1)}, u32[]{:S(2)}, u32[]{:S(2)}) collective-permute-start(f32[6,32,128]{2,1,0:T(8,128)S(1)} %get-tuple-element.34.refs_1_.refs_2_), channel_id=1, source_target_pairs={{0,28},{4,8},{8,4},{12,16},{16,12},{20,24},{24,20},{28,0},{1,29},{... | collective-permute-start | bytes 294920 | tf_op jit(solution)/shard_map/ppermute | solution.py:515
  13.6 2.3 %local.1 = (f32[2112,128]{1,0:T(8,128)S(1)}, f32[132,8,128]{2,1,0:T(8,128)S(1)}, f32[160,128,128]{2,1,0:T(8,128)S(1)}) custom-call(s32[416]{0:T(512)S(4)} %get-tuple-element.27.refs_3_.refs_0_, f32[6,32,128]{2,1,0:T(8,128)S(1)} %get-tuple-element.34.refs_1_.refs_2_, f32[132,8,128]{2,1,0:T(8,128)S(1)} %get-tuple-element.35.refs_2_), custom_call_target="tpu_custom_call", output_to_operand_aliasing={{1}: (2, {})} | custom-call | bytes 10500000 | tf_op jit(solution)/shard_map/local/pallas_call | solution.py:56
  15.9 0.0 collective-permute-done.4.refs_1_
  15.9 1.2 %first.1 = (f32[132,8,128]{2,1,0:T(8,128)S(1)}, f32[160,128,128]{2,1,0:T(8,128)S(1)}) custom-call(s32[416]{0:T(512)S(4)} %get-tuple-element.27.refs_3_.refs_0_, f32[6,32,128]{2,1,0:T(8,128)S(1)} %collective-permute-done.4.refs_1_, f32[2112,128]{1,0:T(8,128)S(1)} %get-tuple-element.36.refs_2_.refs_3_, ...), custom_call_target="tpu_custom_call", output_to_operand_aliasing={{0}: (3, {}), {1}: (4, {})} | custom-call | bytes 4500000 | tf_op jit(solution)/shard_map/first/pallas_call | solution.py:56
  17.1 0.2 collective-permute-done.3.refs_2_.refs_3_
  17.3 1.3 %second.1 = (f32[32,128]{1,0:T(8,128)S(1)}, f32[3,32,128]{2,1,0:T(8,128)S(1)}, f32[132,8,128]{2,1,0:T(8,128)S(1)}, f32[160,128,128]{2,1,0:T(8,128)S(1)}) custom-call(s32[416]{0:T(512)S(4)} %get-tuple-element.27.refs_3_.refs_0_, f32[9,32,128]{2,1,0:T(8,128)S(1)} %get-tuple-element.33.refs_1_, ...), custom_call_target="tpu_custom_call", output_to_operand_aliasing={{2}: (4, {}), {3}: (5, {})} | custom-call | bytes 6000000 | tf_op jit(solution)/shard_map/second/pallas_call | solution.py:56
  18.6 0.1 collective-permute-start.6
  18.7 3.6 %collective-permute-start.5 = (f32[3,32,128]{2,1,0:T(8,128)S(1)}, f32[3,32,128]{2,1,0:T(8,128)S(1)}, u32[]{:S(2)}, u32[]{:S(2)}) collective-permute-start(f32[3,32,128]{2,1,0:T(8,128)S(1)} %get-tuple-element.42.refs_2_.refs_5_), channel_id=1, source_target_pairs={{0,28},{4,8},{8,4},{12,16},{16,12},{20,24},{24,20},{28,0},{1,29},{... | collective-permute-start | bytes 147464 | tf_op jit(solution)/shard_map/ppermute | solution.py:515
  22.3 0.0 collective-permute-start.7
  22.3 0.6 %collective-permute-start.8 = (f32[7,8,128]{2,1,0:T(8,128)S(1)}, f32[7,8,128]{2,1,0:T(8,128)S(1)}, u32[]{:S(2)}, u32[]{:S(2)}) collective-permute-start(f32[7,8,128]{2,1,0:T(8,128)S(1)} %get-tuple-element.46), channel_id=1, source_target_pairs={{0,2},{1,3},{2,0},{3,1},{4,6},{5,7},{6,4},{7,5},{8,10},{9,11},{10,... | collective-permute-start | bytes 86024 | tf_op jit(solution)/shard_map/ppermute | solution.py:478
  22.9 1.3 %collective-permute-start.9 = (f32[7,8,128]{2,1,0:T(8,128)S(1)}, f32[7,8,128]{2,1,0:T(8,128)S(1)}, u32[]{:S(2)}, u32[]{:S(2)}) collective-permute-start(f32[7,8,128]{2,1,0:T(8,128)S(1)} %get-tuple-element.47), channel_id=1, source_target_pairs={{0,3},{1,2},{2,1},{3,0},{4,7},{5,6},{6,5},{7,4},{8,11},{9,10},{10,... | collective-permute-start | bytes 86024 | tf_op jit(solution)/shard_map/ppermute | solution.py:478
  24.2 0.9 %local_fields.1.refs_4_ = f32[132,16,128]{2,1,0:T(8,128)S(1)} custom-call(s32[416]{0:T(512)S(4)} %get-tuple-element.27.refs_3_.refs_0_, f32[6,32,128]{2,1,0:T(8,128)S(1)} %get-tuple-element.34.refs_1_.refs_2_, f32[3,32,128]{2,1,0:T(8,128)S(1)} %get-tuple-element.42.refs_2_.refs_5_, f32[160,128,128]{2,1,0:T(8,128)S(1)} %get-tuple-element.43.refs_3_.refs_7_), custom_call_target="tpu_custom_call" | custom-call | bytes 5100000 | tf_op jit(solution)/shard_map/local_fields/pallas_call | solution.py:56
  25.1 0.0 collective-permute-done.6.refs_2_
  25.1 0.5 %first_fields.1.refs_8_ = f32[132,16,128]{2,1,0:T(8,128)S(1)} custom-call(s32[416]{0:T(512)S(4)} %get-tuple-element.27.refs_3_.refs_0_, f32[6,32,128]{2,1,0:T(8,128)S(1)} %collective-permute-done.4.refs_1_, f32[3,32,128]{2,1,0:T(8,128)S(1)} %collective-permute-done.6.refs_2_, ...), custom_call_target="tpu_custom_call", output_to_operand_aliasing={{}: (4, {})} | custom-call | bytes 3000000 | tf_op jit(solution)/shard_map/first_fields/pallas_call | solution.py:56
  25.6 0.0 collective-permute-done.7.refs_10_
  25.6 0.9 %collective-permute-done.8.refs_11_ = f32[7,8,128]{2,1,0:T(8,128)S(1)} collective-permute-done((f32[7,8,128]{2,1,0:T(8,128)S(1)}, f32[7,8,128]{2,1,0:T(8,128)S(1)}, u32[]{:S(2)}, u32[]{:S(2)}) %collective-permute-start.8) | collective-permute-done | bytes 28704 | tf_op jit(solution)/shard_map/ppermute | solution.py:478
  26.5 0.0 collective-permute-done.9.refs_12_
  26.5 0.0 collective-permute-done.5.refs_6_
  26.5 1.5 %final.1 = (f32[512,128]{1,0:T(8,128)}, f32[5,32,128]{2,1,0:T(8,128)}, f32[132,16,128]{2,1,0:T(8,128)S(1)}) custom-call(s32[416]{0:T(512)S(4)} %get-tuple-element.27.refs_3_.refs_0_, f32[9,32,128]{2,1,0:T(8,128)S(1)} %get-tuple-element.33.refs_1_, f32[6,32,128]{2,1,0:T(8,128)S(1)} %get-tuple-element.34.refs_1_.refs_2_, ...), custom_call_target="tpu_custom_call", output_to_operand_aliasing={{2}: (8, {})} | custom-call | bytes 6000000 | tf_op jit(solution)/shard_map/final/pallas_call | solution.py:56
  (2 shorter events, 0.1 us)
Async XLA Ops:
  1.8 5.4 %collective-permute-start.1 = (f32[9,8,128]{2,1,0:T(8,128)S(1)}, f32[9,8,128]{2,1,0:T(8,128)S(1)}, u32[]{:S(2)}, u32[]{:S(2)}) collective-permute-start(f32[9,8,128]{2,1,0:T(8,128)S(1)} %get-tuple-element.29), channel_id=1, source_target_pairs={{0,2},{1,3},{2,0},{3,1},{4,6},{5,7},{6,4},{7,5},{8,10},{9,11},{10,... | collective-permute-start | bytes 110600 | tf_op jit(solution)/shard_map/ppermute | solution.py:478
  4.8 3.5 %collective-permute-start.2 = (f32[9,8,128]{2,1,0:T(8,128)S(1)}, f32[9,8,128]{2,1,0:T(8,128)S(1)}, u32[]{:S(2)}, u32[]{:S(2)}) collective-permute-start(f32[9,8,128]{2,1,0:T(8,128)S(1)} %get-tuple-element.30), channel_id=1, source_target_pairs={{0,3},{1,2},{2,1},{3,0},{4,7},{5,6},{6,5},{7,4},{8,11},{9,10},{10,... | collective-permute-start | bytes 110600 | tf_op jit(solution)/shard_map/ppermute | solution.py:478
  4.8 3.6 %collective-permute-start = (f32[9,8,128]{2,1,0:T(8,128)S(1)}, f32[9,8,128]{2,1,0:T(8,128)S(1)}, u32[]{:S(2)}, u32[]{:S(2)}) collective-permute-start(f32[9,8,128]{2,1,0:T(8,128)S(1)} %get-tuple-element.28), channel_id=1, source_target_pairs={{0,1},{1,0},{2,3},{3,2},{4,5},{5,4},{6,7},{7,6},{8,9},{9,8},{10,11... | collective-permute-start | bytes 110600 | tf_op jit(solution)/shard_map/ppermute | solution.py:478
  8.4 7.5 %collective-permute-start.4 = (f32[6,32,128]{2,1,0:T(8,128)S(1)}, f32[6,32,128]{2,1,0:T(8,128)S(1)}, u32[]{:S(2)}, u32[]{:S(2)}) collective-permute-start(f32[6,32,128]{2,1,0:T(8,128)S(1)} %get-tuple-element.34.refs_1_.refs_2_), channel_id=1, source_target_pairs={{0,4},{4,0},{8,12},{12,8},{16,20},{20,16},{24,28},{28,24},{1,5},{5... | collective-permute-start | bytes 294920 | tf_op jit(solution)/shard_map/ppermute | solution.py:516
  10.0 7.3 %collective-permute-start.3 = (f32[6,32,128]{2,1,0:T(8,128)S(1)}, f32[6,32,128]{2,1,0:T(8,128)S(1)}, u32[]{:S(2)}, u32[]{:S(2)}) collective-permute-start(f32[6,32,128]{2,1,0:T(8,128)S(1)} %get-tuple-element.34.refs_1_.refs_2_), channel_id=1, source_target_pairs={{0,28},{4,8},{8,4},{12,16},{16,12},{20,24},{24,20},{28,0},{1,29},{... | collective-permute-start | bytes 294920 | tf_op jit(solution)/shard_map/ppermute | solution.py:515
  18.6 6.5 %collective-permute-start.6 = (f32[3,32,128]{2,1,0:T(8,128)S(1)}, f32[3,32,128]{2,1,0:T(8,128)S(1)}, u32[]{:S(2)}, u32[]{:S(2)}) collective-permute-start(f32[3,32,128]{2,1,0:T(8,128)S(1)} %get-tuple-element.42.refs_2_.refs_5_), channel_id=1, source_target_pairs={{0,4},{4,0},{8,12},{12,8},{16,20},{20,16},{24,28},{28,24},{1,5},{5... | collective-permute-start | bytes 147464 | tf_op jit(solution)/shard_map/ppermute | solution.py:516
  18.7 7.8 %collective-permute-start.5 = (f32[3,32,128]{2,1,0:T(8,128)S(1)}, f32[3,32,128]{2,1,0:T(8,128)S(1)}, u32[]{:S(2)}, u32[]{:S(2)}) collective-permute-start(f32[3,32,128]{2,1,0:T(8,128)S(1)} %get-tuple-element.42.refs_2_.refs_5_), channel_id=1, source_target_pairs={{0,28},{4,8},{8,4},{12,16},{16,12},{20,24},{24,20},{28,0},{1,29},{... | collective-permute-start | bytes 147464 | tf_op jit(solution)/shard_map/ppermute | solution.py:515
  22.3 3.3 %collective-permute-start.7 = (f32[7,8,128]{2,1,0:T(8,128)S(1)}, f32[7,8,128]{2,1,0:T(8,128)S(1)}, u32[]{:S(2)}, u32[]{:S(2)}) collective-permute-start(f32[7,8,128]{2,1,0:T(8,128)S(1)} %get-tuple-element.45), channel_id=1, source_target_pairs={{0,1},{1,0},{2,3},{3,2},{4,5},{5,4},{6,7},{7,6},{8,9},{9,8},{10,11... | collective-permute-start | bytes 86024 | tf_op jit(solution)/shard_map/ppermute | solution.py:478
  22.3 4.2 %collective-permute-start.8 = (f32[7,8,128]{2,1,0:T(8,128)S(1)}, f32[7,8,128]{2,1,0:T(8,128)S(1)}, u32[]{:S(2)}, u32[]{:S(2)}) collective-permute-start(f32[7,8,128]{2,1,0:T(8,128)S(1)} %get-tuple-element.46), channel_id=1, source_target_pairs={{0,2},{1,3},{2,0},{3,1},{4,6},{5,7},{6,4},{7,5},{8,10},{9,11},{10,... | collective-permute-start | bytes 86024 | tf_op jit(solution)/shard_map/ppermute | solution.py:478
  22.9 3.6 %collective-permute-start.9 = (f32[7,8,128]{2,1,0:T(8,128)S(1)}, f32[7,8,128]{2,1,0:T(8,128)S(1)}, u32[]{:S(2)}, u32[]{:S(2)}) collective-permute-start(f32[7,8,128]{2,1,0:T(8,128)S(1)} %get-tuple-element.47), channel_id=1, source_target_pairs={{0,3},{1,2},{2,1},{3,0},{4,7},{5,6},{6,5},{7,4},{8,11},{9,10},{10,... | collective-permute-start | bytes 86024 | tf_op jit(solution)/shard_map/ppermute | solution.py:478

commit v7 on v6

--- a/solution.py
+++ b/solution.py
@@ -19,7 +19,7 @@
 LARGE_GROUPS = (((48, 40), (24, 16)), (16, 8))
 GROUPS = (((24, 16),), (16, 8))
 STEP = 8
-EARLY = 1
+EARLY = 0
 CORE = 9
 DEPTH = 32
 FIELD_ROWS = 40
@@ -182,7 +182,7 @@
 
 
 def pack_kernel(tiles, cap, floats, dest_ref, particles_ref, *refs):
-    cores, rests, (packed, staged, dest, sems) = refs[:tiles], refs[tiles : 2 * tiles], refs[2 * tiles :]
+    cores, rests, (packed, staged, dest, sems) = refs[:tiles], refs[tiles:-4], refs[-4:]
     pieces = sems.shape[0] - 1
     bins = staged.shape[0] // pieces
     bring = [pltpu.make_async_copy(dest_ref, dest, sems.at[pieces])]
@@ -211,7 +211,10 @@
             if f < CORE:
                 cores[k][f] = value
             else:
-                rests[k][f - CORE] = value
+                if k % 2 == 0:
+                    rests[k // 2][f - CORE] = value
+                else:
+                    cores[1][f + (k // 2) * (floats - CORE)] = value
 
 
 def states_kernel(tiles, cap, steps, *refs):
@@ -236,6 +239,16 @@
             moving_ref[5 + f, rows, :] = field[3 + f]
 
 
+def near_states_kernel(tiles, cap, floats, *refs):
+    nearest, rests, refs = refs[0], refs[1 : 1 + tiles // 2], refs[1 + tiles // 2 :]
+    bundles, (own_ref, moving_ref) = refs[-2 - tiles // 2 : -2], refs[-2:]
+    states_kernel(tiles, cap, [1], nearest, own_ref, moving_ref)
+    extra = floats - CORE
+    for q in range(tiles // 2):
+        bundles[q][0:extra] = rests[q][...]
+        bundles[q][extra : 2 * extra] = nearest[CORE + q * extra : CORE + (q + 1) * extra]
+
+
 def slot_major(rows):
     slots, lanes = rows[0].shape
     return jnp.swapaxes(jnp.stack(rows, axis=0), 0, 1).reshape(slots * len(rows), lanes)
@@ -408,7 +421,7 @@
 
 def final_kernel(plan, tiles, cap, floats, plan_ref, own_ref, moving_ref, second_ref, density_ref, thermal_ref,
                  second_thermal_ref, slope_ref, sum_in_ref, *refs):
-    rests, (updated_ref, derived_ref, sum_ref, field_ref, total_ref) = refs[:tiles], refs[tiles:]
+    bundles, (updated_ref, derived_ref, sum_ref, field_ref, total_ref) = refs[: tiles // 2], refs[tiles // 2 :]
     slots = plan.slots
     store_fields(field_ref, second_ref, second_thermal_ref, slots)
     store_field_dummy(field_ref, slots)
@@ -417,7 +430,8 @@
         base = pl.multiple_of(source_tile(me, k, tiles) * cap, cap)
         held = (own_ref[6, pl.ds(base, cap), :] > 0).astype(F32)
         for f in range(floats - CORE):
-            updated_ref[pl.ds(base * floats + CORE + f, cap, stride=floats), :] = rests[k][f] * held
+            value = bundles[k // 2][(k % 2) * (floats - CORE) + f]
+            updated_ref[pl.ds(base * floats + CORE + f, cap, stride=floats), :] = value * held
     field_loop(plan, plan_ref, 2, field_ref, slope_ref, sum_ref)
     for i in range(slots):
         first = i << plan.entry_bits
@@ -459,10 +473,12 @@
     slots, width = neighbours.shape
     cap = slots // tiles
     plan = Plan(slots, width)
+    half, extra = tiles // 2, floats - CORE
     packed = kernel_call(
         lambda *refs: pack_kernel(tiles, cap, floats, *refs),
         [("h", in_hbm(dest_slot)), ("h", in_hbm(particles))],
-        [("v", (CORE, cap, lanes), F32)] * tiles + [("v", (floats - CORE, cap, lanes), F32)] * tiles,
+        [("v", (CORE + (extra * half if k == 1 else 0), cap, lanes), F32) for k in range(tiles)]
+        + [("v", (extra, cap, lanes), F32)] * half,
         [
             pltpu.VMEM((slots * floats, lanes), F32),
             pltpu.VMEM((bins, floats, lanes), F32),
@@ -498,16 +514,15 @@
         200,
         "far_states",
     )
-    if tiles > 1:
-        own, moving = kernel_call(
-            lambda *refs: states_kernel(tiles, cap, [1], *refs),
-            [("v", parts[1]), ("v", own), ("v", moving), ("a", lists)],
-            state_outs,
-            [],
-            100,
-            "near_states",
-            {1: 0, 2: 1},
-        )
+    *bundles, own, moving = kernel_call(
+        lambda *refs: near_states_kernel(tiles, cap, floats, *refs),
+        [("v", parts[1])] + [("v", rest) for rest in rests] + [("v", own), ("v", moving), ("a", lists)],
+        [("v", (2 * extra, cap, lanes), F32)] * half + state_outs,
+        [],
+        100,
+        "near_states",
+        {1 + half: half, 2 + half: half + 1},
+    )
     first_pairs = [(s, s ^ 1) for s in range(slabs)]
     second_pairs = [(s, (((s + 1) ^ 1) - 1) % slabs) for s in range(slabs)]
 
@@ -549,7 +564,6 @@
         {4: 2, 5: 3},
     )
     first_thermal, second_thermal = both_sides(thermal)
-    later = rests[1:]
     (sums,) = kernel_call(
         lambda *refs: local_field_kernel(plan, *refs),
         [("s", lists), ("v", moving), ("v", thermal), ("v", slopes)],
@@ -558,7 +572,7 @@
         1700,
         "local_fields",
     )
-    rests = [rests[0]] + [to_partner(later[k - 1], k) for k in range(1, tiles)]
+    bundles = [bundles[0]] + [to_partner(bundles[q], 2 * q) for q in range(1, half)]
     (sums,) = kernel_call(
         lambda *refs: first_field_kernel(plan, *refs),
         [("s", lists), ("v", first), ("v", first_thermal), ("v", slopes), ("v", sums)],
@@ -572,7 +586,7 @@
         lambda *refs: final_kernel(plan, tiles, cap, floats, *refs),
         [("s", lists), ("v", own), ("v", moving), ("v", second), ("v", density), ("v", thermal),
          ("v", second_thermal), ("v", slopes), ("v", sums)]
-        + [("v", rest) for rest in rests],
+        + [("v", bundle) for bundle in bundles],
         [("v", (slots * floats, lanes), F32), ("v", (5, slots, lanes), F32), sum_out],
         field_table + [pltpu.VMEM((slots * 16, lanes), F32)],
         2000,

time: 28.2 us -> 27.6 us (0.979)
  starting transfers between devices: 13.9 us -> 12.6 us
  waiting for transfers between devices: 2.13 us -> 2.53 us
  Pallas kernels: 11.2 us -> 11.5 us
    ppermute x6 -> x4, starting transfers between devices: 5.09 us -> 4.34 us  [to_partner(): lax.ppermute(array, 'tile', [(t, partner_tile(t, step, tiles)) for t in r...]
    ppermute x6 -> x4, waiting for transfers between devices: 1.96 us -> 2.52 us  [to_partner(): lax.ppermute(array, 'tile', [(t, partner_tile(t, step, tiles)) for t in r...]
    ppermute x2, starting transfers between devices: 7.16 us -> 6.68 us  [both_sides(): second = lax.ppermute(array, 'slab', second_pairs)]
    pallas_call x10, Pallas kernels: 11.2 us -> 11.5 us  [kernel_call(): pl.pallas_call(kernel, out_shape=[pltpu.SMEM(shape, dtype) if memory == '...]
  transfers between devices with their start and end apart: 10 -> 8, of which waited for: 3 -> 2; matrix products, arithmetic and copies ran while one was open for 0% -> 0% of each run, Pallas kernels for 26% -> 29%
where the time goes in v7:
time: 27.6 us; the launch traced here: 27.4 us
  starting transfers between devices  12.6 us (46%)
  Pallas kernels  11.5 us (42%)
  waiting for transfers between devices  2.53 us (9%)
  between operations  0.74 us (3%)
    pallas_call x10, Pallas kernels, kernel_call(): pl.pallas_call(kernel, out_shape=[pltpu.SMEM(shape, dtype) if memory == '...  11.5 us
    ppermute x2, starting transfers between devices, both_sides(): second = lax.ppermute(array, 'slab', second_pairs)  6.68 us
    ppermute x4, starting transfers between devices, to_partner(): lax.ppermute(array, 'tile', [(t, partner_tile(t, step, tiles)) for t in r...  4.34 us
    ppermute x4, waiting for transfers between devices, to_partner(): lax.ppermute(array, 'tile', [(t, partner_tile(t, step, tiles)) for t in r...  2.52 us
    ppermute x2, starting transfers between devices, both_sides(): first = lax.ppermute(array, 'slab', first_pairs)  1.63 us
  transfers between devices with their start and end apart: 8, of which 2 were waited for; matrix products, arithmetic and copies ran while one was open for 0% of the time, Pallas kernels for 29%

profile of v7, /device:TPU:0, one launch (start us, length us, event | category | flops | bytes accessed | tf_op | source)
XLA Modules:
  0.0 27.4 jit_solution(11692697311097323008)
XLA Ops:
  0.6 1.2 %pack.1 = (f32[9,8,128]{2,1,0:T(8,128)S(1)}, f32[23,8,128]{2,1,0:T(8,128)S(1)}, f32[9,8,128]{2,1,0:T(8,128)S(1)}, f32[9,8,128]{2,1,0:T(8,128)S(1)}, f32[7,8,128]{2,1,0:T(8,128)S(1)}, /*index=5*/f32[7,8,128]{2,1,0:T(8,128)S(1)}) custom-call(s32[32]{0:T(128)} %refs_0_.1, f32[32,16,128]{2,1,0:T(8,128)} %refs_1_.2), custom_call_target="tpu_custom_call" | custom-call | bytes 4500000 | tf_op jit(solution)/shard_map/pack/pallas_call | solution.py:56
  1.8 0.5 %collective-permute-start = (f32[23,8,128]{2,1,0:T(8,128)S(1)}, f32[23,8,128]{2,1,0:T(8,128)S(1)}, u32[]{:S(2)}, u32[]{:S(2)}) collective-permute-start(f32[23,8,128]{2,1,0:T(8,128)S(1)} %get-tuple-element.28), channel_id=1, source_target_pairs={{0,1},{1,0},{2,3},{3,2},{4,5},{5,4},{6,7},{7,6},{8,9},{9,8},{10,11... | collective-permute-start | bytes 282632 | tf_op jit(solution)/shard_map/ppermute | solution.py:494
  2.3 2.6 %collective-permute-start.1 = (f32[9,8,128]{2,1,0:T(8,128)S(1)}, f32[9,8,128]{2,1,0:T(8,128)S(1)}, u32[]{:S(2)}, u32[]{:S(2)}) collective-permute-start(f32[9,8,128]{2,1,0:T(8,128)S(1)} %get-tuple-element.31), channel_id=1, source_target_pairs={{0,2},{1,3},{2,0},{3,1},{4,6},{5,7},{6,4},{7,5},{8,10},{9,11},{10,... | collective-permute-start | bytes 110600 | tf_op jit(solution)/shard_map/ppermute | solution.py:494
  4.9 0.1 collective-permute-start.2
  5.0 2.2 %plan.1 = (s32[416]{0:T(512)S(4)}, f32[132,8,128]{2,1,0:T(8,128)S(1)}) custom-call(s32[4,32]{1,0:T(4,128)} %bitcast.3, s32[32]{0:T(128)} %refs_1_.3, f32[9,8,128]{2,1,0:T(8,128)S(1)} %get-tuple-element.26.refs_2_.refs_0_), custom_call_target="tpu_custom_call" | custom-call | bytes 6000000 | tf_op jit(solution)/shard_map/plan/pallas_call | solution.py:56
  7.2 0.0 collective-permute-done.1.refs_1_
  7.2 1.1 %collective-permute-done.2.refs_2_ = f32[9,8,128]{2,1,0:T(8,128)S(1)} collective-permute-done((f32[9,8,128]{2,1,0:T(8,128)S(1)}, f32[9,8,128]{2,1,0:T(8,128)S(1)}, u32[]{:S(2)}, u32[]{:S(2)}) %collective-permute-start.2) | collective-permute-done | bytes 36896 | tf_op jit(solution)/shard_map/ppermute | solution.py:494
  8.4 0.0 collective-permute-done.refs_0_
  8.4 1.6 %collective-permute-start.4 = (f32[5,32,128]{2,1,0:T(8,128)S(1)}, f32[5,32,128]{2,1,0:T(8,128)S(1)}, u32[]{:S(2)}, u32[]{:S(2)}) collective-permute-start(f32[5,32,128]{2,1,0:T(8,128)S(1)} %get-tuple-element.36.refs_1_.refs_2_), channel_id=1, source_target_pairs={{0,4},{4,0},{8,12},{12,8},{16,20},{20,16},{24,28},{28,24},{1,5},{5... | collective-permute-start | bytes 245768 | tf_op jit(solution)/shard_map/ppermute | solution.py:531
  10.0 3.6 %collective-permute-start.3 = (f32[5,32,128]{2,1,0:T(8,128)S(1)}, f32[5,32,128]{2,1,0:T(8,128)S(1)}, u32[]{:S(2)}, u32[]{:S(2)}) collective-permute-start(f32[5,32,128]{2,1,0:T(8,128)S(1)} %get-tuple-element.36.refs_1_.refs_2_), channel_id=1, source_target_pairs={{0,28},{4,8},{8,4},{12,16},{16,12},{20,24},{24,20},{28,0},{1,29},{... | collective-permute-start | bytes 245768 | tf_op jit(solution)/shard_map/ppermute | solution.py:530
  13.6 2.8 %local.1 = (f32[2112,128]{1,0:T(8,128)S(1)}, f32[132,8,128]{2,1,0:T(8,128)S(1)}, f32[160,128,128]{2,1,0:T(8,128)S(1)}) custom-call(s32[416]{0:T(512)S(4)} %get-tuple-element.27.refs_5_.refs_0_, f32[5,32,128]{2,1,0:T(8,128)S(1)} %get-tuple-element.36.refs_1_.refs_2_, f32[132,8,128]{2,1,0:T(8,128)S(1)} %get-tuple-element.37.refs_2_), custom_call_target="tpu_custom_call", output_to_operand_aliasing={{1}: (2, {})} | custom-call | bytes 10500000 | tf_op jit(solution)/shard_map/local/pallas_call | solution.py:56
  16.4 0.0 collective-permute-done.4.refs_1_
  16.4 1.2 %first.1 = (f32[132,8,128]{2,1,0:T(8,128)S(1)}, f32[160,128,128]{2,1,0:T(8,128)S(1)}) custom-call(s32[416]{0:T(512)S(4)} %get-tuple-element.27.refs_5_.refs_0_, f32[5,32,128]{2,1,0:T(8,128)S(1)} %collective-permute-done.4.refs_1_, f32[2112,128]{1,0:T(8,128)S(1)} %get-tuple-element.38.refs_2_.refs_3_, ...), custom_call_target="tpu_custom_call", output_to_operand_aliasing={{0}: (3, {}), {1}: (4, {})} | custom-call | bytes 4500000 | tf_op jit(solution)/shard_map/first/pallas_call | solution.py:56
  17.6 0.0 collective-permute-done.3.refs_2_.refs_3_
  17.6 1.0 %second.1 = (f32[32,128]{1,0:T(8,128)S(1)}, f32[4,32,128]{2,1,0:T(8,128)S(1)}, f32[132,8,128]{2,1,0:T(8,128)S(1)}, f32[160,128,128]{2,1,0:T(8,128)S(1)}) custom-call(s32[416]{0:T(512)S(4)} %get-tuple-element.27.refs_5_.refs_0_, f32[9,32,128]{2,1,0:T(8,128)S(1)} %get-tuple-element.35.refs_1_, ...), custom_call_target="tpu_custom_call", output_to_operand_aliasing={{2}: (4, {}), {3}: (5, {})} | custom-call | bytes 6000000 | tf_op jit(solution)/shard_map/second/pallas_call | solution.py:56
  18.6 0.1 collective-permute-start.6
  18.7 3.1 %collective-permute-start.5 = (f32[4,32,128]{2,1,0:T(8,128)S(1)}, f32[4,32,128]{2,1,0:T(8,128)S(1)}, u32[]{:S(2)}, u32[]{:S(2)}) collective-permute-start(f32[4,32,128]{2,1,0:T(8,128)S(1)} %get-tuple-element.44.refs_2_.refs_5_), channel_id=1, source_target_pairs={{0,28},{4,8},{8,4},{12,16},{16,12},{20,24},{24,20},{28,0},{1,29},{... | collective-permute-start | bytes 196616 | tf_op jit(solution)/shard_map/ppermute | solution.py:530
  21.8 1.2 %collective-permute-start.7 = (f32[14,8,128]{2,1,0:T(8,128)S(1)}, f32[14,8,128]{2,1,0:T(8,128)S(1)}, u32[]{:S(2)}, u32[]{:S(2)}) collective-permute-start(f32[14,8,128]{2,1,0:T(8,128)S(1)} %get-tuple-element.47), channel_id=1, source_target_pairs={{0,2},{1,3},{2,0},{3,1},{4,6},{5,7},{6,4},{7,5},{8,10},{9,11},{10,... | collective-permute-start | bytes 172040 | tf_op jit(solution)/shard_map/ppermute | solution.py:494
  23.0 1.1 %local_fields.1.refs_4_ = f32[132,16,128]{2,1,0:T(8,128)S(1)} custom-call(s32[416]{0:T(512)S(4)} %get-tuple-element.27.refs_5_.refs_0_, f32[5,32,128]{2,1,0:T(8,128)S(1)} %get-tuple-element.36.refs_1_.refs_2_, f32[4,32,128]{2,1,0:T(8,128)S(1)} %get-tuple-element.44.refs_2_.refs_5_, f32[160,128,128]{2,1,0:T(8,128)S(1)} %get-tuple-element.45.refs_3_.refs_7_), custom_call_target="tpu_custom_call" | custom-call | bytes 5100000 | tf_op jit(solution)/shard_map/local_fields/pallas_call | solution.py:56
  24.1 0.0 collective-permute-done.6.refs_2_
  24.1 0.5 %first_fields.1.refs_8_ = f32[132,16,128]{2,1,0:T(8,128)S(1)} custom-call(s32[416]{0:T(512)S(4)} %get-tuple-element.27.refs_5_.refs_0_, f32[5,32,128]{2,1,0:T(8,128)S(1)} %collective-permute-done.4.refs_1_, f32[4,32,128]{2,1,0:T(8,128)S(1)} %collective-permute-done.6.refs_2_, ...), custom_call_target="tpu_custom_call", output_to_operand_aliasing={{}: (4, {})} | custom-call | bytes 3000000 | tf_op jit(solution)/shard_map/first_fields/pallas_call | solution.py:56
  24.6 1.4 %collective-permute-done.7.refs_10_ = f32[14,8,128]{2,1,0:T(8,128)S(1)} collective-permute-done((f32[14,8,128]{2,1,0:T(8,128)S(1)}, f32[14,8,128]{2,1,0:T(8,128)S(1)}, u32[]{:S(2)}, u32[]{:S(2)}) %collective-permute-start.7) | collective-permute-done | bytes 57376 | tf_op jit(solution)/shard_map/ppermute | solution.py:494
  26.0 0.0 collective-permute-done.5.refs_6_
  26.0 1.4 %final.1 = (f32[512,128]{1,0:T(8,128)}, f32[5,32,128]{2,1,0:T(8,128)}, f32[132,16,128]{2,1,0:T(8,128)S(1)}) custom-call(s32[416]{0:T(512)S(4)} %get-tuple-element.27.refs_5_.refs_0_, f32[9,32,128]{2,1,0:T(8,128)S(1)} %get-tuple-element.35.refs_1_, f32[5,32,128]{2,1,0:T(8,128)S(1)} %get-tuple-element.36.refs_1_.refs_2_, ...), custom_call_target="tpu_custom_call", output_to_operand_aliasing={{2}: (8, {})} | custom-call | bytes 6000000 | tf_op jit(solution)/shard_map/final/pallas_call | solution.py:56
  (2 shorter events, 0.1 us)
Async XLA Ops:
  1.8 6.6 %collective-permute-start = (f32[23,8,128]{2,1,0:T(8,128)S(1)}, f32[23,8,128]{2,1,0:T(8,128)S(1)}, u32[]{:S(2)}, u32[]{:S(2)}) collective-permute-start(f32[23,8,128]{2,1,0:T(8,128)S(1)} %get-tuple-element.28), channel_id=1, source_target_pairs={{0,1},{1,0},{2,3},{3,2},{4,5},{5,4},{6,7},{7,6},{8,9},{9,8},{10,11... | collective-permute-start | bytes 282632 | tf_op jit(solution)/shard_map/ppermute | solution.py:494
  2.3 4.9 %collective-permute-start.1 = (f32[9,8,128]{2,1,0:T(8,128)S(1)}, f32[9,8,128]{2,1,0:T(8,128)S(1)}, u32[]{:S(2)}, u32[]{:S(2)}) collective-permute-start(f32[9,8,128]{2,1,0:T(8,128)S(1)} %get-tuple-element.31), channel_id=1, source_target_pairs={{0,2},{1,3},{2,0},{3,1},{4,6},{5,7},{6,4},{7,5},{8,10},{9,11},{10,... | collective-permute-start | bytes 110600 | tf_op jit(solution)/shard_map/ppermute | solution.py:494
  4.9 3.4 %collective-permute-start.2 = (f32[9,8,128]{2,1,0:T(8,128)S(1)}, f32[9,8,128]{2,1,0:T(8,128)S(1)}, u32[]{:S(2)}, u32[]{:S(2)}) collective-permute-start(f32[9,8,128]{2,1,0:T(8,128)S(1)} %get-tuple-element.32), channel_id=1, source_target_pairs={{0,3},{1,2},{2,1},{3,0},{4,7},{5,6},{6,5},{7,4},{8,11},{9,10},{10,... | collective-permute-start | bytes 110600 | tf_op jit(solution)/shard_map/ppermute | solution.py:494
  8.4 7.9 %collective-permute-start.4 = (f32[5,32,128]{2,1,0:T(8,128)S(1)}, f32[5,32,128]{2,1,0:T(8,128)S(1)}, u32[]{:S(2)}, u32[]{:S(2)}) collective-permute-start(f32[5,32,128]{2,1,0:T(8,128)S(1)} %get-tuple-element.36.refs_1_.refs_2_), channel_id=1, source_target_pairs={{0,4},{4,0},{8,12},{12,8},{16,20},{20,16},{24,28},{28,24},{1,5},{5... | collective-permute-start | bytes 245768 | tf_op jit(solution)/shard_map/ppermute | solution.py:531
  10.0 7.6 %collective-permute-start.3 = (f32[5,32,128]{2,1,0:T(8,128)S(1)}, f32[5,32,128]{2,1,0:T(8,128)S(1)}, u32[]{:S(2)}, u32[]{:S(2)}) collective-permute-start(f32[5,32,128]{2,1,0:T(8,128)S(1)} %get-tuple-element.36.refs_1_.refs_2_), channel_id=1, source_target_pairs={{0,28},{4,8},{8,4},{12,16},{16,12},{20,24},{24,20},{28,0},{1,29},{... | collective-permute-start | bytes 245768 | tf_op jit(solution)/shard_map/ppermute | solution.py:530
  18.6 5.5 %collective-permute-start.6 = (f32[4,32,128]{2,1,0:T(8,128)S(1)}, f32[4,32,128]{2,1,0:T(8,128)S(1)}, u32[]{:S(2)}, u32[]{:S(2)}) collective-permute-start(f32[4,32,128]{2,1,0:T(8,128)S(1)} %get-tuple-element.44.refs_2_.refs_5_), channel_id=1, source_target_pairs={{0,4},{4,0},{8,12},{12,8},{16,20},{20,16},{24,28},{28,24},{1,5},{5... | collective-permute-start | bytes 196616 | tf_op jit(solution)/shard_map/ppermute | solution.py:531
  18.7 7.3 %collective-permute-start.5 = (f32[4,32,128]{2,1,0:T(8,128)S(1)}, f32[4,32,128]{2,1,0:T(8,128)S(1)}, u32[]{:S(2)}, u32[]{:S(2)}) collective-permute-start(f32[4,32,128]{2,1,0:T(8,128)S(1)} %get-tuple-element.44.refs_2_.refs_5_), channel_id=1, source_target_pairs={{0,28},{4,8},{8,4},{12,16},{16,12},{20,24},{24,20},{28,0},{1,29},{... | collective-permute-start | bytes 196616 | tf_op jit(solution)/shard_map/ppermute | solution.py:530
  21.8 4.2 %collective-permute-start.7 = (f32[14,8,128]{2,1,0:T(8,128)S(1)}, f32[14,8,128]{2,1,0:T(8,128)S(1)}, u32[]{:S(2)}, u32[]{:S(2)}) collective-permute-start(f32[14,8,128]{2,1,0:T(8,128)S(1)} %get-tuple-element.47), channel_id=1, source_target_pairs={{0,2},{1,3},{2,0},{3,1},{4,6},{5,7},{6,4},{7,5},{8,10},{9,11},{10,... | collective-permute-start | bytes 172040 | tf_op jit(solution)/shard_map/ppermute | solution.py:494

commit v8 on v7

--- a/solution.py
+++ b/solution.py
@@ -319,9 +319,11 @@
             remain = jnp.maximum(4.0 - squared * lax.rsqrt(squared) * inverse, 0.0)
             scaled = inverse * remain
             cubed = scaled * scaled * scaled
-            weight = cubed * (remain * (5.0 - remain))
-            weight_ref[plan.code(word)] = jnp.sum(weight.reshape(LANES // 8, 8, LANES), axis=0)
-            slope_ref[stored + start + u] = cubed * (inverse * inverse)
+            if weight_ref is not None:
+                weight = cubed * (remain * (5.0 - remain))
+                weight_ref[plan.code(word)] = jnp.sum(weight.reshape(LANES // 8, 8, LANES), axis=0)
+            if slope_ref is not None:
+                slope_ref[stored + start + u] = cubed * (inverse * inverse)
 
     in_groups(plan, plan_ref, which, groups, work)
 
@@ -340,11 +342,11 @@
     pair_loop(plan, plan_ref, 1, GROUPS, near_ref, far_ref, weight_ref, slope_ref)
 
 
-def second_kernel(plan, plan_ref, own_ref, moving_ref, near_ref, weight_in_ref, slope_in_ref,
-                  density_ref, thermal_ref, weight_ref, slope_ref, far_ref):
+def second_kernel(plan, plan_ref, own_ref, moving_ref, near_ref, weight_in_ref,
+                  density_ref, thermal_ref, weight_ref, far_ref):
     store_far(far_ref, moving_ref, plan.slots)
     store_far_dummy(far_ref, plan.slots)
-    pair_loop(plan, plan_ref, 2, GROUPS, near_ref, far_ref, weight_ref, slope_ref)
+    pair_loop(plan, plan_ref, 2, GROUPS, near_ref, far_ref, weight_ref, None)
     for i in range(plan.slots):
         first = i << plan.entry_bits
         tile = weight_ref[first]
@@ -357,6 +359,12 @@
     thermal_ref[0] = (ADIABATIC - 1.0) * density * own_ref[7] / (safe * safe)
     for f in range(EARLY, 3):
         thermal_ref[1 + f - EARLY] = own_ref[3 + f]
+
+
+def slope_kernel(plan, plan_ref, moving_ref, near_ref, thermal_ref, slope_in_ref, slope_ref, far_ref):
+    store_far(far_ref, moving_ref, plan.slots)
+    store_far_dummy(far_ref, plan.slots)
+    pair_loop(plan, plan_ref, 2, GROUPS, near_ref, far_ref, None, slope_ref)
 
 
 def store_fields(field_ref, moving_ref, thermal_ref, slots):
@@ -554,14 +562,14 @@
         "first",
         {3: 0, 4: 1},
     )
-    density, thermal, weights, slopes = kernel_call(
+    density, thermal, weights = kernel_call(
         lambda *refs: second_kernel(plan, *refs),
-        [("s", lists), ("v", own), ("v", second), ("v", near), ("v", weights), ("v", slopes)],
-        [("v", (slots, lanes), F32), ("v", (4 - EARLY, slots, lanes), F32), weight_out, slope_out],
+        [("s", lists), ("v", own), ("v", second), ("v", near), ("v", weights)],
+        [("v", (slots, lanes), F32), ("v", (4 - EARLY, slots, lanes), F32), weight_out],
         far_table,
         2000,
         "second",
-        {4: 2, 5: 3},
+        {4: 2},
     )
     first_thermal, second_thermal = both_sides(thermal)
     (sums,) = kernel_call(
@@ -573,6 +581,15 @@
         "local_fields",
     )
     bundles = [bundles[0]] + [to_partner(bundles[q], 2 * q) for q in range(1, half)]
+    (slopes,) = kernel_call(
+        lambda *refs: slope_kernel(plan, *refs),
+        [("s", lists), ("v", second), ("v", near), ("a", thermal), ("v", slopes)],
+        [slope_out],
+        far_table,
+        1300,
+        "slopes",
+        {4: 0},
+    )
     (sums,) = kernel_call(
         lambda *refs: first_field_kernel(plan, *refs),
         [("s", lists), ("v", first), ("v", first_thermal), ("v", slopes), ("v", sums)],

time: 27.6 us -> 27.7 us (level)
  starting transfers between devices: 12.6 us -> 13.1 us
  waiting for transfers between devices: 2.53 us -> 2.03 us
    ppermute x2, starting transfers between devices: 1.63 us -> 2.48 us  [both_sides(): first = lax.ppermute(array, 'slab', first_pairs)]
    ppermute x4, waiting for transfers between devices: 2.52 us -> 2.02 us  [to_partner(): lax.ppermute(array, 'tile', [(t, partner_tile(t, step, tiles)) for t in r...]
    ppermute x4, starting transfers between devices: 4.34 us -> 4.03 us  [to_partner(): lax.ppermute(array, 'tile', [(t, partner_tile(t, step, tiles)) for t in r...]
    pallas_call x10 -> x11, Pallas kernels: 11.5 us -> 11.7 us  [kernel_call(): pl.pallas_call(kernel, out_shape=[pltpu.SMEM(shape, dtype) if memory == '...]
  transfers between devices with their start and end apart: 8 -> 8, of which waited for: 2 -> 2; matrix products, arithmetic and copies ran while one was open for 0% -> 0% of each run, Pallas kernels for 29% -> 30%
where the time goes in v8:
time: 27.7 us; the launch traced here: 27.6 us
  starting transfers between devices  13.1 us (47%)
  Pallas kernels  11.7 us (42%)
  waiting for transfers between devices  2.03 us (7%)
  between operations  0.74 us (3%)
    pallas_call x11, Pallas kernels, kernel_call(): pl.pallas_call(kernel, out_shape=[pltpu.SMEM(shape, dtype) if memory == '...  11.7 us
    ppermute x2, starting transfers between devices, both_sides(): second = lax.ppermute(array, 'slab', second_pairs)  6.62 us
    ppermute x4, starting transfers between devices, to_partner(): lax.ppermute(array, 'tile', [(t, partner_tile(t, step, tiles)) for t in r...  4.03 us
    ppermute x2, starting transfers between devices, both_sides(): first = lax.ppermute(array, 'slab', first_pairs)  2.48 us
    ppermute x4, waiting for transfers between devices, to_partner(): lax.ppermute(array, 'tile', [(t, partner_tile(t, step, tiles)) for t in r...  2.02 us
  transfers between devices with their start and end apart: 8, of which 2 were waited for; matrix products, arithmetic and copies ran while one was open for 0% of the time, Pallas kernels for 30%

profile of v8, /device:TPU:0, one launch (start us, length us, event | category | flops | bytes accessed | tf_op | source)
XLA Modules:
  0.0 27.6 jit_solution(1968792149974200503)
XLA Ops:
  0.6 1.2 %pack.1 = (f32[9,8,128]{2,1,0:T(8,128)S(1)}, f32[23,8,128]{2,1,0:T(8,128)S(1)}, f32[9,8,128]{2,1,0:T(8,128)S(1)}, f32[9,8,128]{2,1,0:T(8,128)S(1)}, f32[7,8,128]{2,1,0:T(8,128)S(1)}, /*index=5*/f32[7,8,128]{2,1,0:T(8,128)S(1)}) custom-call(s32[32]{0:T(128)} %refs_0_.1, f32[32,16,128]{2,1,0:T(8,128)} %refs_1_.2), custom_call_target="tpu_custom_call" | custom-call | bytes 4500000 | tf_op jit(solution)/shard_map/pack/pallas_call | solution.py:56
  1.8 0.5 %collective-permute-start = (f32[23,8,128]{2,1,0:T(8,128)S(1)}, f32[23,8,128]{2,1,0:T(8,128)S(1)}, u32[]{:S(2)}, u32[]{:S(2)}) collective-permute-start(f32[23,8,128]{2,1,0:T(8,128)S(1)} %get-tuple-element.27), channel_id=1, source_target_pairs={{0,1},{1,0},{2,3},{3,2},{4,5},{5,4},{6,7},{7,6},{8,9},{9,8},{10,11... | collective-permute-start | bytes 282632 | tf_op jit(solution)/shard_map/ppermute | solution.py:502
  2.3 2.6 %collective-permute-start.1 = (f32[9,8,128]{2,1,0:T(8,128)S(1)}, f32[9,8,128]{2,1,0:T(8,128)S(1)}, u32[]{:S(2)}, u32[]{:S(2)}) collective-permute-start(f32[9,8,128]{2,1,0:T(8,128)S(1)} %get-tuple-element.30), channel_id=1, source_target_pairs={{0,2},{1,3},{2,0},{3,1},{4,6},{5,7},{6,4},{7,5},{8,10},{9,11},{10,... | collective-permute-start | bytes 110600 | tf_op jit(solution)/shard_map/ppermute | solution.py:502
  4.9 0.1 collective-permute-start.2
  5.0 2.2 %plan.1 = (s32[416]{0:T(512)S(4)}, f32[132,8,128]{2,1,0:T(8,128)S(1)}) custom-call(s32[4,32]{1,0:T(4,128)} %bitcast.3, s32[32]{0:T(128)} %refs_1_.3, f32[9,8,128]{2,1,0:T(8,128)S(1)} %get-tuple-element.25.refs_2_.refs_0_), custom_call_target="tpu_custom_call" | custom-call | bytes 6000000 | tf_op jit(solution)/shard_map/plan/pallas_call | solution.py:56
  7.2 0.0 collective-permute-done.1.refs_1_
  7.2 1.1 %collective-permute-done.2.refs_2_ = f32[9,8,128]{2,1,0:T(8,128)S(1)} collective-permute-done((f32[9,8,128]{2,1,0:T(8,128)S(1)}, f32[9,8,128]{2,1,0:T(8,128)S(1)}, u32[]{:S(2)}, u32[]{:S(2)}) %collective-permute-start.2) | collective-permute-done | bytes 36896 | tf_op jit(solution)/shard_map/ppermute | solution.py:502
  8.4 0.0 collective-permute-done.refs_0_
  8.4 1.6 %collective-permute-start.4 = (f32[5,32,128]{2,1,0:T(8,128)S(1)}, f32[5,32,128]{2,1,0:T(8,128)S(1)}, u32[]{:S(2)}, u32[]{:S(2)}) collective-permute-start(f32[5,32,128]{2,1,0:T(8,128)S(1)} %get-tuple-element.35.refs_1_.refs_2_), channel_id=1, source_target_pairs={{0,4},{4,0},{8,12},{12,8},{16,20},{20,16},{24,28},{28,24},{1,5},{5... | collective-permute-start | bytes 245768 | tf_op jit(solution)/shard_map/ppermute | solution.py:539
  10.0 3.6 %collective-permute-start.3 = (f32[5,32,128]{2,1,0:T(8,128)S(1)}, f32[5,32,128]{2,1,0:T(8,128)S(1)}, u32[]{:S(2)}, u32[]{:S(2)}) collective-permute-start(f32[5,32,128]{2,1,0:T(8,128)S(1)} %get-tuple-element.35.refs_1_.refs_2_), channel_id=1, source_target_pairs={{0,28},{4,8},{8,4},{12,16},{16,12},{20,24},{24,20},{28,0},{1,29},{... | collective-permute-start | bytes 245768 | tf_op jit(solution)/shard_map/ppermute | solution.py:538
  13.6 2.3 %local.1 = (f32[2112,128]{1,0:T(8,128)S(1)}, f32[132,8,128]{2,1,0:T(8,128)S(1)}, f32[160,128,128]{2,1,0:T(8,128)S(1)}) custom-call(s32[416]{0:T(512)S(4)} %get-tuple-element.26.refs_5_.refs_0_, f32[5,32,128]{2,1,0:T(8,128)S(1)} %get-tuple-element.35.refs_1_.refs_2_, f32[132,8,128]{2,1,0:T(8,128)S(1)} %get-tuple-element.36.refs_2_), custom_call_target="tpu_custom_call", output_to_operand_aliasing={{1}: (2, {})} | custom-call | bytes 10500000 | tf_op jit(solution)/shard_map/local/pallas_call | solution.py:56
  15.9 0.0 collective-permute-done.4.refs_1_
  15.9 1.2 %first.1 = (f32[132,8,128]{2,1,0:T(8,128)S(1)}, f32[160,128,128]{2,1,0:T(8,128)S(1)}) custom-call(s32[416]{0:T(512)S(4)} %get-tuple-element.26.refs_5_.refs_0_, f32[5,32,128]{2,1,0:T(8,128)S(1)} %collective-permute-done.4.refs_1_, f32[2112,128]{1,0:T(8,128)S(1)} %get-tuple-element.37.refs_2_.refs_3_, ...), custom_call_target="tpu_custom_call", output_to_operand_aliasing={{0}: (3, {}), {1}: (4, {})} | custom-call | bytes 4500000 | tf_op jit(solution)/shard_map/first/pallas_call | solution.py:56
  17.1 0.0 collective-permute-done.3.refs_2_.refs_1_.refs_3_
  17.1 0.9 %second.1 = (f32[32,128]{1,0:T(8,128)S(1)}, f32[4,32,128]{2,1,0:T(8,128)S(1)}, f32[132,8,128]{2,1,0:T(8,128)S(1)}) custom-call(s32[416]{0:T(512)S(4)} %get-tuple-element.26.refs_5_.refs_0_, f32[9,32,128]{2,1,0:T(8,128)S(1)} %get-tuple-element.34.refs_1_, ...), custom_call_target="tpu_custom_call", output_to_operand_aliasing={{2}: (4, {})} | custom-call | bytes 6000000 | tf_op jit(solution)/shard_map/second/pallas_call | solution.py:56
  18.1 0.9 %collective-permute-start.6 = (f32[4,32,128]{2,1,0:T(8,128)S(1)}, f32[4,32,128]{2,1,0:T(8,128)S(1)}, u32[]{:S(2)}, u32[]{:S(2)}) collective-permute-start(f32[4,32,128]{2,1,0:T(8,128)S(1)} %get-tuple-element.42.refs_3_.refs_2_.refs_5_), channel_id=1, source_target_pairs={{0,4},{4,0},{8,12},{12,8},{16,20},{20,16},{24,28},{28,24},{1,5},{5... | collective-permute-start | bytes 196616 | tf_op jit(solution)/shard_map/ppermute | solution.py:539
  19.0 3.0 %collective-permute-start.5 = (f32[4,32,128]{2,1,0:T(8,128)S(1)}, f32[4,32,128]{2,1,0:T(8,128)S(1)}, u32[]{:S(2)}, u32[]{:S(2)}) collective-permute-start(f32[4,32,128]{2,1,0:T(8,128)S(1)} %get-tuple-element.42.refs_3_.refs_2_.refs_5_), channel_id=1, source_target_pairs={{0,28},{4,8},{8,4},{12,16},{16,12},{20,24},{24,20},{28,0},{1,29},{... | collective-permute-start | bytes 196616 | tf_op jit(solution)/shard_map/ppermute | solution.py:538
  22.0 0.9 %collective-permute-start.7 = (f32[14,8,128]{2,1,0:T(8,128)S(1)}, f32[14,8,128]{2,1,0:T(8,128)S(1)}, u32[]{:S(2)}, u32[]{:S(2)}) collective-permute-start(f32[14,8,128]{2,1,0:T(8,128)S(1)} %get-tuple-element.45), channel_id=1, source_target_pairs={{0,2},{1,3},{2,0},{3,1},{4,6},{5,7},{6,4},{7,5},{8,10},{9,11},{10,... | collective-permute-start | bytes 172040 | tf_op jit(solution)/shard_map/ppermute | solution.py:502
  22.9 0.9 %local_fields.1.refs_4_ = f32[132,16,128]{2,1,0:T(8,128)S(1)} custom-call(s32[416]{0:T(512)S(4)} %get-tuple-element.26.refs_5_.refs_0_, f32[5,32,128]{2,1,0:T(8,128)S(1)} %get-tuple-element.35.refs_1_.refs_2_, f32[4,32,128]{2,1,0:T(8,128)S(1)} %get-tuple-element.42.refs_3_.refs_2_.refs_5_, f32[160,128,128]{2,1,0:T(8,128)S(1)} %get-tuple-element.43.refs_4_.refs_3_), custom_call_target="tpu_custom_call" | custom-call | bytes 5100000 | tf_op jit(solution)/shard_map/local_fields/pallas_call | solution.py:56
  23.8 1.0 %slopes.1.refs_3_.refs_7_ = f32[160,128,128]{2,1,0:T(8,128)S(1)} custom-call(s32[416]{0:T(512)S(4)} %get-tuple-element.26.refs_5_.refs_0_, f32[5,32,128]{2,1,0:T(8,128)S(1)} %collective-permute-done.3.refs_2_.refs_1_.refs_3_, f32[2112,128]{1,0:T(8,128)S(1)} %get-tuple-element.37.refs_2_.refs_3_, ...), custom_call_target="tpu_custom_call", output_to_operand_aliasing={{}: (4, {})} | custom-call | bytes 3900000 | tf_op jit(solution)/shard_map/slopes/pallas_call | solution.py:56
  24.8 0.0 collective-permute-done.6.refs_2_
  24.9 0.5 %first_fields.1.refs_8_ = f32[132,16,128]{2,1,0:T(8,128)S(1)} custom-call(s32[416]{0:T(512)S(4)} %get-tuple-element.26.refs_5_.refs_0_, f32[5,32,128]{2,1,0:T(8,128)S(1)} %collective-permute-done.4.refs_1_, f32[4,32,128]{2,1,0:T(8,128)S(1)} %collective-permute-done.6.refs_2_, ...), custom_call_target="tpu_custom_call", output_to_operand_aliasing={{}: (4, {})} | custom-call | bytes 3000000 | tf_op jit(solution)/shard_map/first_fields/pallas_call | solution.py:56
  25.4 0.9 %collective-permute-done.7.refs_10_ = f32[14,8,128]{2,1,0:T(8,128)S(1)} collective-permute-done((f32[14,8,128]{2,1,0:T(8,128)S(1)}, f32[14,8,128]{2,1,0:T(8,128)S(1)}, u32[]{:S(2)}, u32[]{:S(2)}) %collective-permute-start.7) | collective-permute-done | bytes 57376 | tf_op jit(solution)/shard_map/ppermute | solution.py:502
  26.2 0.0 collective-permute-done.5.refs_6_
  26.2 1.4 %final.1 = (f32[512,128]{1,0:T(8,128)}, f32[5,32,128]{2,1,0:T(8,128)}, f32[132,16,128]{2,1,0:T(8,128)S(1)}) custom-call(s32[416]{0:T(512)S(4)} %get-tuple-element.26.refs_5_.refs_0_, f32[9,32,128]{2,1,0:T(8,128)S(1)} %get-tuple-element.34.refs_1_, f32[5,32,128]{2,1,0:T(8,128)S(1)} %get-tuple-element.35.refs_1_.refs_2_, ...), custom_call_target="tpu_custom_call", output_to_operand_aliasing={{2}: (8, {})} | custom-call | bytes 6000000 | tf_op jit(solution)/shard_map/final/pallas_call | solution.py:56
  (2 shorter events, 0.1 us)
Async XLA Ops:
  1.8 6.6 %collective-permute-start = (f32[23,8,128]{2,1,0:T(8,128)S(1)}, f32[23,8,128]{2,1,0:T(8,128)S(1)}, u32[]{:S(2)}, u32[]{:S(2)}) collective-permute-start(f32[23,8,128]{2,1,0:T(8,128)S(1)} %get-tuple-element.27), channel_id=1, source_target_pairs={{0,1},{1,0},{2,3},{3,2},{4,5},{5,4},{6,7},{7,6},{8,9},{9,8},{10,11... | collective-permute-start | bytes 282632 | tf_op jit(solution)/shard_map/ppermute | solution.py:502
  2.3 4.9 %collective-permute-start.1 = (f32[9,8,128]{2,1,0:T(8,128)S(1)}, f32[9,8,128]{2,1,0:T(8,128)S(1)}, u32[]{:S(2)}, u32[]{:S(2)}) collective-permute-start(f32[9,8,128]{2,1,0:T(8,128)S(1)} %get-tuple-element.30), channel_id=1, source_target_pairs={{0,2},{1,3},{2,0},{3,1},{4,6},{5,7},{6,4},{7,5},{8,10},{9,11},{10,... | collective-permute-start | bytes 110600 | tf_op jit(solution)/shard_map/ppermute | solution.py:502
  4.9 3.4 %collective-permute-start.2 = (f32[9,8,128]{2,1,0:T(8,128)S(1)}, f32[9,8,128]{2,1,0:T(8,128)S(1)}, u32[]{:S(2)}, u32[]{:S(2)}) collective-permute-start(f32[9,8,128]{2,1,0:T(8,128)S(1)} %get-tuple-element.31), channel_id=1, source_target_pairs={{0,3},{1,2},{2,1},{3,0},{4,7},{5,6},{6,5},{7,4},{8,11},{9,10},{10,... | collective-permute-start | bytes 110600 | tf_op jit(solution)/shard_map/ppermute | solution.py:502
  8.4 7.5 %collective-permute-start.4 = (f32[5,32,128]{2,1,0:T(8,128)S(1)}, f32[5,32,128]{2,1,0:T(8,128)S(1)}, u32[]{:S(2)}, u32[]{:S(2)}) collective-permute-start(f32[5,32,128]{2,1,0:T(8,128)S(1)} %get-tuple-element.35.refs_1_.refs_2_), channel_id=1, source_target_pairs={{0,4},{4,0},{8,12},{12,8},{16,20},{20,16},{24,28},{28,24},{1,5},{5... | collective-permute-start | bytes 245768 | tf_op jit(solution)/shard_map/ppermute | solution.py:539
  10.0 7.2 %collective-permute-start.3 = (f32[5,32,128]{2,1,0:T(8,128)S(1)}, f32[5,32,128]{2,1,0:T(8,128)S(1)}, u32[]{:S(2)}, u32[]{:S(2)}) collective-permute-start(f32[5,32,128]{2,1,0:T(8,128)S(1)} %get-tuple-element.35.refs_1_.refs_2_), channel_id=1, source_target_pairs={{0,28},{4,8},{8,4},{12,16},{16,12},{20,24},{24,20},{28,0},{1,29},{... | collective-permute-start | bytes 245768 | tf_op jit(solution)/shard_map/ppermute | solution.py:538
  18.1 6.8 %collective-permute-start.6 = (f32[4,32,128]{2,1,0:T(8,128)S(1)}, f32[4,32,128]{2,1,0:T(8,128)S(1)}, u32[]{:S(2)}, u32[]{:S(2)}) collective-permute-start(f32[4,32,128]{2,1,0:T(8,128)S(1)} %get-tuple-element.42.refs_3_.refs_2_.refs_5_), channel_id=1, source_target_pairs={{0,4},{4,0},{8,12},{12,8},{16,20},{20,16},{24,28},{28,24},{1,5},{5... | collective-permute-start | bytes 196616 | tf_op jit(solution)/shard_map/ppermute | solution.py:539
  19.0 7.2 %collective-permute-start.5 = (f32[4,32,128]{2,1,0:T(8,128)S(1)}, f32[4,32,128]{2,1,0:T(8,128)S(1)}, u32[]{:S(2)}, u32[]{:S(2)}) collective-permute-start(f32[4,32,128]{2,1,0:T(8,128)S(1)} %get-tuple-element.42.refs_3_.refs_2_.refs_5_), channel_id=1, source_target_pairs={{0,28},{4,8},{8,4},{12,16},{16,12},{20,24},{24,20},{28,0},{1,29},{... | collective-permute-start | bytes 196616 | tf_op jit(solution)/shard_map/ppermute | solution.py:538
  22.0 4.2 %collective-permute-start.7 = (f32[14,8,128]{2,1,0:T(8,128)S(1)}, f32[14,8,128]{2,1,0:T(8,128)S(1)}, u32[]{:S(2)}, u32[]{:S(2)}) collective-permute-start(f32[14,8,128]{2,1,0:T(8,128)S(1)} %get-tuple-element.45), channel_id=1, source_target_pairs={{0,2},{1,3},{2,0},{3,1},{4,6},{5,7},{6,4},{7,5},{8,10},{9,11},{10,... | collective-permute-start | bytes 172040 | tf_op jit(solution)/shard_map/ppermute | solution.py:502

commit v9 on v8

--- a/solution.py
+++ b/solution.py
@@ -18,6 +18,7 @@
 LANES = 128
 LARGE_GROUPS = (((48, 40), (24, 16)), (16, 8))
 GROUPS = (((24, 16),), (16, 8))
+WEIGHT_GROUPS = (((28, 24), (24, 16)), (16, 8))
 STEP = 8
 EARLY = 0
 CORE = 9
@@ -346,7 +347,7 @@
                   density_ref, thermal_ref, weight_ref, far_ref):
     store_far(far_ref, moving_ref, plan.slots)
     store_far_dummy(far_ref, plan.slots)
-    pair_loop(plan, plan_ref, 2, GROUPS, near_ref, far_ref, weight_ref, None)
+    pair_loop(plan, plan_ref, 2, WEIGHT_GROUPS, near_ref, far_ref, weight_ref, None)
     for i in range(plan.slots):
         first = i << plan.entry_bits
         tile = weight_ref[first]

time: 27.7 us -> 27.7 us (level)
  Pallas kernels: 11.7 us -> 12.1 us
  starting transfers between devices: 13.1 us -> 12.7 us
    ppermute x2, starting transfers between devices: 2.48 us -> 2.06 us  [both_sides(): first = lax.ppermute(array, 'slab', first_pairs)]
    pallas_call x11, Pallas kernels: 11.7 us -> 12.1 us  [kernel_call(): pl.pallas_call(kernel, out_shape=[pltpu.SMEM(shape, dtype) if memory == '...]
  transfers between devices with their start and end apart: 8 -> 8, of which waited for: 2 -> 2; matrix products, arithmetic and copies ran while one was open for 0% -> 0% of each run, Pallas kernels for 30% -> 31%
where the time goes in v9:
time: 27.7 us; the launch traced here: 27.6 us
  starting transfers between devices  12.7 us (46%)
  Pallas kernels  12.1 us (44%)
  waiting for transfers between devices  2.13 us (8%)
  between operations  0.74 us (3%)
    pallas_call x11, Pallas kernels, kernel_call(): pl.pallas_call(kernel, out_shape=[pltpu.SMEM(shape, dtype) if memory == '...  12.1 us
    ppermute x2, starting transfers between devices, both_sides(): second = lax.ppermute(array, 'slab', second_pairs)  6.84 us
    ppermute x4, starting transfers between devices, to_partner(): lax.ppermute(array, 'tile', [(t, partner_tile(t, step, tiles)) for t in r...  3.79 us
    ppermute x4, waiting for transfers between devices, to_partner(): lax.ppermute(array, 'tile', [(t, partner_tile(t, step, tiles)) for t in r...  2.12 us
    ppermute x2, starting transfers between devices, both_sides(): first = lax.ppermute(array, 'slab', first_pairs)  2.06 us
  transfers between devices with their start and end apart: 8, of which 2 were waited for; matrix products, arithmetic and copies ran while one was open for 0% of the time, Pallas kernels for 31%

profile of v9, /device:TPU:0, one launch (start us, length us, event | category | flops | bytes accessed | tf_op | source)
XLA Modules:
  0.0 27.6 jit_solution(7688188104878743683)
XLA Ops:
  0.6 1.2 %pack.1 = (f32[9,8,128]{2,1,0:T(8,128)S(1)}, f32[23,8,128]{2,1,0:T(8,128)S(1)}, f32[9,8,128]{2,1,0:T(8,128)S(1)}, f32[9,8,128]{2,1,0:T(8,128)S(1)}, f32[7,8,128]{2,1,0:T(8,128)S(1)}, /*index=5*/f32[7,8,128]{2,1,0:T(8,128)S(1)}) custom-call(s32[32]{0:T(128)} %refs_0_.1, f32[32,16,128]{2,1,0:T(8,128)} %refs_1_.2), custom_call_target="tpu_custom_call" | custom-call | bytes 4500000 | tf_op jit(solution)/shard_map/pack/pallas_call | solution.py:57
  1.8 0.5 %collective-permute-start = (f32[23,8,128]{2,1,0:T(8,128)S(1)}, f32[23,8,128]{2,1,0:T(8,128)S(1)}, u32[]{:S(2)}, u32[]{:S(2)}) collective-permute-start(f32[23,8,128]{2,1,0:T(8,128)S(1)} %get-tuple-element.27), channel_id=1, source_target_pairs={{0,1},{1,0},{2,3},{3,2},{4,5},{5,4},{6,7},{7,6},{8,9},{9,8},{10,11... | collective-permute-start | bytes 282632 | tf_op jit(solution)/shard_map/ppermute | solution.py:503
  2.3 2.6 %collective-permute-start.1 = (f32[9,8,128]{2,1,0:T(8,128)S(1)}, f32[9,8,128]{2,1,0:T(8,128)S(1)}, u32[]{:S(2)}, u32[]{:S(2)}) collective-permute-start(f32[9,8,128]{2,1,0:T(8,128)S(1)} %get-tuple-element.30), channel_id=1, source_target_pairs={{0,2},{1,3},{2,0},{3,1},{4,6},{5,7},{6,4},{7,5},{8,10},{9,11},{10,... | collective-permute-start | bytes 110600 | tf_op jit(solution)/shard_map/ppermute | solution.py:503
  4.9 0.1 collective-permute-start.2
  5.0 2.2 %plan.1 = (s32[416]{0:T(512)S(4)}, f32[132,8,128]{2,1,0:T(8,128)S(1)}) custom-call(s32[4,32]{1,0:T(4,128)} %bitcast.3, s32[32]{0:T(128)} %refs_1_.3, f32[9,8,128]{2,1,0:T(8,128)S(1)} %get-tuple-element.25.refs_2_.refs_0_), custom_call_target="tpu_custom_call" | custom-call | bytes 6000000 | tf_op jit(solution)/shard_map/plan/pallas_call | solution.py:57
  7.2 0.0 collective-permute-done.1.refs_1_
  7.2 1.1 %collective-permute-done.2.refs_2_ = f32[9,8,128]{2,1,0:T(8,128)S(1)} collective-permute-done((f32[9,8,128]{2,1,0:T(8,128)S(1)}, f32[9,8,128]{2,1,0:T(8,128)S(1)}, u32[]{:S(2)}, u32[]{:S(2)}) %collective-permute-start.2) | collective-permute-done | bytes 36896 | tf_op jit(solution)/shard_map/ppermute | solution.py:503
  8.4 0.0 collective-permute-done.refs_0_
  8.4 1.6 %collective-permute-start.4 = (f32[5,32,128]{2,1,0:T(8,128)S(1)}, f32[5,32,128]{2,1,0:T(8,128)S(1)}, u32[]{:S(2)}, u32[]{:S(2)}) collective-permute-start(f32[5,32,128]{2,1,0:T(8,128)S(1)} %get-tuple-element.35.refs_1_.refs_2_), channel_id=1, source_target_pairs={{0,4},{4,0},{8,12},{12,8},{16,20},{20,16},{24,28},{28,24},{1,5},{5... | collective-permute-start | bytes 245768 | tf_op jit(solution)/shard_map/ppermute | solution.py:540
  10.0 3.6 %collective-permute-start.3 = (f32[5,32,128]{2,1,0:T(8,128)S(1)}, f32[5,32,128]{2,1,0:T(8,128)S(1)}, u32[]{:S(2)}, u32[]{:S(2)}) collective-permute-start(f32[5,32,128]{2,1,0:T(8,128)S(1)} %get-tuple-element.35.refs_1_.refs_2_), channel_id=1, source_target_pairs={{0,28},{4,8},{8,4},{12,16},{16,12},{20,24},{24,20},{28,0},{1,29},{... | collective-permute-start | bytes 245768 | tf_op jit(solution)/shard_map/ppermute | solution.py:539
  13.6 2.8 %local.1 = (f32[2112,128]{1,0:T(8,128)S(1)}, f32[132,8,128]{2,1,0:T(8,128)S(1)}, f32[160,128,128]{2,1,0:T(8,128)S(1)}) custom-call(s32[416]{0:T(512)S(4)} %get-tuple-element.26.refs_5_.refs_0_, f32[5,32,128]{2,1,0:T(8,128)S(1)} %get-tuple-element.35.refs_1_.refs_2_, f32[132,8,128]{2,1,0:T(8,128)S(1)} %get-tuple-element.36.refs_2_), custom_call_target="tpu_custom_call", output_to_operand_aliasing={{1}: (2, {})} | custom-call | bytes 10500000 | tf_op jit(solution)/shard_map/local/pallas_call | solution.py:57
  16.4 0.0 collective-permute-done.4.refs_1_
  16.4 0.9 %first.1 = (f32[132,8,128]{2,1,0:T(8,128)S(1)}, f32[160,128,128]{2,1,0:T(8,128)S(1)}) custom-call(s32[416]{0:T(512)S(4)} %get-tuple-element.26.refs_5_.refs_0_, f32[5,32,128]{2,1,0:T(8,128)S(1)} %collective-permute-done.4.refs_1_, f32[2112,128]{1,0:T(8,128)S(1)} %get-tuple-element.37.refs_2_.refs_3_, ...), custom_call_target="tpu_custom_call", output_to_operand_aliasing={{0}: (3, {}), {1}: (4, {})} | custom-call | bytes 4500000 | tf_op jit(solution)/shard_map/first/pallas_call | solution.py:57
  17.3 0.0 collective-permute-done.3.refs_2_.refs_1_.refs_3_
  17.3 0.9 %second.1 = (f32[32,128]{1,0:T(8,128)S(1)}, f32[4,32,128]{2,1,0:T(8,128)S(1)}, f32[132,8,128]{2,1,0:T(8,128)S(1)}) custom-call(s32[416]{0:T(512)S(4)} %get-tuple-element.26.refs_5_.refs_0_, f32[9,32,128]{2,1,0:T(8,128)S(1)} %get-tuple-element.34.refs_1_, ...), custom_call_target="tpu_custom_call", output_to_operand_aliasing={{2}: (4, {})} | custom-call | bytes 6000000 | tf_op jit(solution)/shard_map/second/pallas_call | solution.py:57
  18.3 0.5 %collective-permute-start.6 = (f32[4,32,128]{2,1,0:T(8,128)S(1)}, f32[4,32,128]{2,1,0:T(8,128)S(1)}, u32[]{:S(2)}, u32[]{:S(2)}) collective-permute-start(f32[4,32,128]{2,1,0:T(8,128)S(1)} %get-tuple-element.42.refs_3_.refs_2_.refs_5_), channel_id=1, source_target_pairs={{0,4},{4,0},{8,12},{12,8},{16,20},{20,16},{24,28},{28,24},{1,5},{5... | collective-permute-start | bytes 196616 | tf_op jit(solution)/shard_map/ppermute | solution.py:540
  18.8 3.3 %collective-permute-start.5 = (f32[4,32,128]{2,1,0:T(8,128)S(1)}, f32[4,32,128]{2,1,0:T(8,128)S(1)}, u32[]{:S(2)}, u32[]{:S(2)}) collective-permute-start(f32[4,32,128]{2,1,0:T(8,128)S(1)} %get-tuple-element.42.refs_3_.refs_2_.refs_5_), channel_id=1, source_target_pairs={{0,28},{4,8},{8,4},{12,16},{16,12},{20,24},{24,20},{28,0},{1,29},{... | collective-permute-start | bytes 196616 | tf_op jit(solution)/shard_map/ppermute | solution.py:539
  22.1 0.6 %collective-permute-start.7 = (f32[14,8,128]{2,1,0:T(8,128)S(1)}, f32[14,8,128]{2,1,0:T(8,128)S(1)}, u32[]{:S(2)}, u32[]{:S(2)}) collective-permute-start(f32[14,8,128]{2,1,0:T(8,128)S(1)} %get-tuple-element.45), channel_id=1, source_target_pairs={{0,2},{1,3},{2,0},{3,1},{4,6},{5,7},{6,4},{7,5},{8,10},{9,11},{10,... | collective-permute-start | bytes 172040 | tf_op jit(solution)/shard_map/ppermute | solution.py:503
  22.7 1.3 %local_fields.1.refs_4_ = f32[132,16,128]{2,1,0:T(8,128)S(1)} custom-call(s32[416]{0:T(512)S(4)} %get-tuple-element.26.refs_5_.refs_0_, f32[5,32,128]{2,1,0:T(8,128)S(1)} %get-tuple-element.35.refs_1_.refs_2_, f32[4,32,128]{2,1,0:T(8,128)S(1)} %get-tuple-element.42.refs_3_.refs_2_.refs_5_, f32[160,128,128]{2,1,0:T(8,128)S(1)} %get-tuple-element.43.refs_4_.refs_3_), custom_call_target="tpu_custom_call" | custom-call | bytes 5100000 | tf_op jit(solution)/shard_map/local_fields/pallas_call | solution.py:57
  24.0 0.8 %slopes.1.refs_3_.refs_7_ = f32[160,128,128]{2,1,0:T(8,128)S(1)} custom-call(s32[416]{0:T(512)S(4)} %get-tuple-element.26.refs_5_.refs_0_, f32[5,32,128]{2,1,0:T(8,128)S(1)} %collective-permute-done.3.refs_2_.refs_1_.refs_3_, f32[2112,128]{1,0:T(8,128)S(1)} %get-tuple-element.37.refs_2_.refs_3_, ...), custom_call_target="tpu_custom_call", output_to_operand_aliasing={{}: (4, {})} | custom-call | bytes 3900000 | tf_op jit(solution)/shard_map/slopes/pallas_call | solution.py:57
  24.8 0.0 collective-permute-done.6.refs_2_
  24.8 0.4 %first_fields.1.refs_8_ = f32[132,16,128]{2,1,0:T(8,128)S(1)} custom-call(s32[416]{0:T(512)S(4)} %get-tuple-element.26.refs_5_.refs_0_, f32[5,32,128]{2,1,0:T(8,128)S(1)} %collective-permute-done.4.refs_1_, f32[4,32,128]{2,1,0:T(8,128)S(1)} %collective-permute-done.6.refs_2_, ...), custom_call_target="tpu_custom_call", output_to_operand_aliasing={{}: (4, {})} | custom-call | bytes 3000000 | tf_op jit(solution)/shard_map/first_fields/pallas_call | solution.py:57
  25.3 1.0 %collective-permute-done.7.refs_10_ = f32[14,8,128]{2,1,0:T(8,128)S(1)} collective-permute-done((f32[14,8,128]{2,1,0:T(8,128)S(1)}, f32[14,8,128]{2,1,0:T(8,128)S(1)}, u32[]{:S(2)}, u32[]{:S(2)}) %collective-permute-start.7) | collective-permute-done | bytes 57376 | tf_op jit(solution)/shard_map/ppermute | solution.py:503
  26.2 0.0 collective-permute-done.5.refs_6_
  26.2 1.4 %final.1 = (f32[512,128]{1,0:T(8,128)}, f32[5,32,128]{2,1,0:T(8,128)}, f32[132,16,128]{2,1,0:T(8,128)S(1)}) custom-call(s32[416]{0:T(512)S(4)} %get-tuple-element.26.refs_5_.refs_0_, f32[9,32,128]{2,1,0:T(8,128)S(1)} %get-tuple-element.34.refs_1_, f32[5,32,128]{2,1,0:T(8,128)S(1)} %get-tuple-element.35.refs_1_.refs_2_, ...), custom_call_target="tpu_custom_call", output_to_operand_aliasing={{2}: (8, {})} | custom-call | bytes 6000000 | tf_op jit(solution)/shard_map/final/pallas_call | solution.py:57
  (2 shorter events, 0.1 us)
Async XLA Ops:
  1.8 6.6 %collective-permute-start = (f32[23,8,128]{2,1,0:T(8,128)S(1)}, f32[23,8,128]{2,1,0:T(8,128)S(1)}, u32[]{:S(2)}, u32[]{:S(2)}) collective-permute-start(f32[23,8,128]{2,1,0:T(8,128)S(1)} %get-tuple-element.27), channel_id=1, source_target_pairs={{0,1},{1,0},{2,3},{3,2},{4,5},{5,4},{6,7},{7,6},{8,9},{9,8},{10,11... | collective-permute-start | bytes 282632 | tf_op jit(solution)/shard_map/ppermute | solution.py:503
  2.3 4.9 %collective-permute-start.1 = (f32[9,8,128]{2,1,0:T(8,128)S(1)}, f32[9,8,128]{2,1,0:T(8,128)S(1)}, u32[]{:S(2)}, u32[]{:S(2)}) collective-permute-start(f32[9,8,128]{2,1,0:T(8,128)S(1)} %get-tuple-element.30), channel_id=1, source_target_pairs={{0,2},{1,3},{2,0},{3,1},{4,6},{5,7},{6,4},{7,5},{8,10},{9,11},{10,... | collective-permute-start | bytes 110600 | tf_op jit(solution)/shard_map/ppermute | solution.py:503
  4.9 3.4 %collective-permute-start.2 = (f32[9,8,128]{2,1,0:T(8,128)S(1)}, f32[9,8,128]{2,1,0:T(8,128)S(1)}, u32[]{:S(2)}, u32[]{:S(2)}) collective-permute-start(f32[9,8,128]{2,1,0:T(8,128)S(1)} %get-tuple-element.31), channel_id=1, source_target_pairs={{0,3},{1,2},{2,1},{3,0},{4,7},{5,6},{6,5},{7,4},{8,11},{9,10},{10,... | collective-permute-start | bytes 110600 | tf_op jit(solution)/shard_map/ppermute | solution.py:503
  8.4 7.9 %collective-permute-start.4 = (f32[5,32,128]{2,1,0:T(8,128)S(1)}, f32[5,32,128]{2,1,0:T(8,128)S(1)}, u32[]{:S(2)}, u32[]{:S(2)}) collective-permute-start(f32[5,32,128]{2,1,0:T(8,128)S(1)} %get-tuple-element.35.refs_1_.refs_2_), channel_id=1, source_target_pairs={{0,4},{4,0},{8,12},{12,8},{16,20},{20,16},{24,28},{28,24},{1,5},{5... | collective-permute-start | bytes 245768 | tf_op jit(solution)/shard_map/ppermute | solution.py:540
  10.0 7.4 %collective-permute-start.3 = (f32[5,32,128]{2,1,0:T(8,128)S(1)}, f32[5,32,128]{2,1,0:T(8,128)S(1)}, u32[]{:S(2)}, u32[]{:S(2)}) collective-permute-start(f32[5,32,128]{2,1,0:T(8,128)S(1)} %get-tuple-element.35.refs_1_.refs_2_), channel_id=1, source_target_pairs={{0,28},{4,8},{8,4},{12,16},{16,12},{20,24},{24,20},{28,0},{1,29},{... | collective-permute-start | bytes 245768 | tf_op jit(solution)/shard_map/ppermute | solution.py:539
  18.3 6.5 %collective-permute-start.6 = (f32[4,32,128]{2,1,0:T(8,128)S(1)}, f32[4,32,128]{2,1,0:T(8,128)S(1)}, u32[]{:S(2)}, u32[]{:S(2)}) collective-permute-start(f32[4,32,128]{2,1,0:T(8,128)S(1)} %get-tuple-element.42.refs_3_.refs_2_.refs_5_), channel_id=1, source_target_pairs={{0,4},{4,0},{8,12},{12,8},{16,20},{20,16},{24,28},{28,24},{1,5},{5... | collective-permute-start | bytes 196616 | tf_op jit(solution)/shard_map/ppermute | solution.py:540
  18.8 7.4 %collective-permute-start.5 = (f32[4,32,128]{2,1,0:T(8,128)S(1)}, f32[4,32,128]{2,1,0:T(8,128)S(1)}, u32[]{:S(2)}, u32[]{:S(2)}) collective-permute-start(f32[4,32,128]{2,1,0:T(8,128)S(1)} %get-tuple-element.42.refs_3_.refs_2_.refs_5_), channel_id=1, source_target_pairs={{0,28},{4,8},{8,4},{12,16},{16,12},{20,24},{24,20},{28,0},{1,29},{... | collective-permute-start | bytes 196616 | tf_op jit(solution)/shard_map/ppermute | solution.py:539
  22.1 4.2 %collective-permute-start.7 = (f32[14,8,128]{2,1,0:T(8,128)S(1)}, f32[14,8,128]{2,1,0:T(8,128)S(1)}, u32[]{:S(2)}, u32[]{:S(2)}) collective-permute-start(f32[14,8,128]{2,1,0:T(8,128)S(1)} %get-tuple-element.45), channel_id=1, source_target_pairs={{0,2},{1,3},{2,0},{3,1},{4,6},{5,7},{6,4},{7,5},{8,10},{9,11},{10,... | collective-permute-start | bytes 172040 | tf_op jit(solution)/shard_map/ppermute | solution.py:503
